TPU v7x, 32 devices: a whole 2x2x4 slice. The times are simulated.
32 devices in a mesh: dp: 16 (over z, y, core), tensor: 2 (over x).
Axes of the slice: x: 2, y: 2, z: 4, core: 2. Of those that a mesh axis runs over, the one named last changes fastest.
Arguments:
- tokens: bfloat16 [2, 16, 128, 2048], P(None, 'dp'), may hold values from -6 to 6
- segment_ids: int32 [2, 16, 128], P(None, 'dp'), may hold values from 0 to 3, never falling along the last dimension, each value on 1 to 64 neighbouring positions
- query_proj: bfloat16 [2048, 2048], P('dp', 'tensor'), may hold values from -0.125 to 0.125
- key_proj: bfloat16 [2048, 2048], P('dp', 'tensor'), may hold values from -0.125 to 0.125
- value_proj: bfloat16 [2048, 2048], P('dp', 'tensor'), may hold values from -0.125 to 0.125
- out_proj: bfloat16 [2048, 2048], P('dp', 'tensor'), may hold values from -0.125 to 0.125
- query_gain: float32 [2048], P('tensor'), may hold values from 0.1 to 1.9
- key_gain: float32 [2048], P('tensor'), may hold values from 0.1 to 1.9
- attn_gain: float32 [2048], replicated, may hold values from 0.1 to 1.9
- gate_proj: bfloat16 [2048, 8192], P('dp', 'tensor'), may hold values from -0.125 to 0.125
- up_proj: bfloat16 [2048, 8192], P('dp', 'tensor'), may hold values from -0.125 to 0.125
- down_proj: bfloat16 [2048, 8192], P('dp', 'tensor'), may hold values from -0.0625 to 0.0625
- mlp_gain: float32 [2048], replicated, may hold values from 0.1 to 1.9
- cotangent: bfloat16 [2, 16, 128, 2048], P(None, 'dp'), may hold values from -6 to 6
Outputs:
- layer_out: bfloat16 [2, 16, 128, 2048], P(None, 'dp')
- tokens_grad: float32 [2, 16, 128, 2048], P(None, 'dp')
- query_proj_grad: float32 [2048, 2048], P('dp', 'tensor')
- key_proj_grad: float32 [2048, 2048], P('dp', 'tensor')
- value_proj_grad: float32 [2048, 2048], P('dp', 'tensor')
- out_proj_grad: float32 [2048, 2048], P('dp', 'tensor')
- query_gain_grad: float32 [2048], P('tensor')
- key_gain_grad: float32 [2048], P('tensor')
- attn_gain_grad: float32 [2048], replicated
- gate_proj_grad: float32 [2048, 8192], P('dp', 'tensor')
- up_proj_grad: float32 [2048, 8192], P('dp', 'tensor')
- down_proj_grad: float32 [2048, 8192], P('dp', 'tensor')
- mlp_gain_grad: float32 [2048], replicated
Inputs may be any that keep to these rules, and one draw needn't show every extreme that they name: `segment_ids`: along each row the segment numbers never fall; each of the 4 segments of a row has 1 to 64 tokens, and one has exactly 64.
All inputs are finite; a program needn't handle non-finite values.
Results may differ from a plain program's by a relative error of at most 0.017.
Values may be sent and summed in bfloat16 or wider, within the bound.
No kernel may reach another device: no remote copies, remote signals or barrier semaphores. Data moves between devices by JAX's collectives and lax.ppermute only.
A program may use at most 768 MiB of HBM per device.

v0:
```python
import math

import jax
import jax.numpy as jnp
from jax import lax
from jax.sharding import PartitionSpec as P

D = 2048
HEAD_DIM = 128


EPSILON = 1e-06
ROPE_BASE = 500000.0


def for_sending(x):
    return jax.tree.map(lambda a: a.astype(jnp.bfloat16) if a.dtype == jnp.float32 else a, x)


def rms_norm(values, weights):
    return values * lax.rsqrt(jnp.mean(values * values, axis=-1, keepdims=True) + EPSILON) * weights


def positions(segment_row):
    places = jnp.arange(segment_row.shape[0], dtype=jnp.int32)
    earlier = (segment_row[None, :] == segment_row[:, None]) & (places[None, :] < places[:, None])
    return jnp.sum(earlier.astype(jnp.int32), axis=1)


def rotary(values, places):
    row_count, row_width = values.shape
    per_head = values.reshape(row_count, row_width // HEAD_DIM, HEAD_DIM)
    halfway = HEAD_DIM // 2
    inverse = jnp.exp(
        jnp.arange(halfway, dtype=jnp.float32) * (-2.0 * math.log(ROPE_BASE) / HEAD_DIM)
    )
    angles = places.astype(jnp.float32)[:, None] * inverse[None, :]
    cosine = jnp.cos(angles)[:, None, :]
    sine_table = jnp.sin(angles)[:, None, :]
    leading = per_head[..., :halfway]
    trailing = per_head[..., halfway:]
    turned = jnp.concatenate(
        [leading * cosine - trailing * sine_table, trailing * cosine + leading * sine_table],
        axis=-1,
    )
    return turned.reshape(row_count, row_width)


def swish_product(gated, lifted):
    return gated / (1.0 + jnp.exp(-gated)) * lifted


def dot_plain(operand, partner):
    return jnp.dot(operand, partner, preferred_element_type=jnp.float32)


def dot_transposed(operand, partner):
    return lax.dot_general(
        operand, partner, (((1,), (1,)), ((), ())), preferred_element_type=jnp.float32
    )


def gather_attention(shards):
    return jax.tree.map(
        lambda part, own: part.astype(own.dtype),
        lax.all_gather(for_sending(shards), "dp", axis=0, tiled=True),
        shards,
    )


def gather_feedforward(shards):
    return jax.tree.map(
        lambda part, own: part.astype(own.dtype),
        lax.all_gather(for_sending(shards), "dp", axis=0, tiled=True),
        shards,
    )


def score_table(query_low, key_low, allowed):
    row_count = query_low.shape[0]
    query_heads = query_low.reshape(row_count, -1, HEAD_DIM)
    key_heads = key_low.reshape(row_count, -1, HEAD_DIM)
    scores = jnp.einsum(
        "qhd,khd->hqk", query_heads, key_heads, preferred_element_type=jnp.float32
    ) * HEAD_DIM ** (-0.5)
    return jnp.where(allowed[None], scores, -1e30)


def attend(query_low, key_low, value_low, allowed):
    row_count = query_low.shape[0]
    scores = score_table(query_low, key_low, allowed)
    row_max = jnp.max(scores, axis=-1, keepdims=True)
    expo = jnp.exp(scores - row_max)
    row_total = jnp.sum(expo, axis=-1, keepdims=True)
    probs_low = (expo / row_total).astype(jnp.bfloat16)
    value_heads = value_low.reshape(row_count, -1, HEAD_DIM)
    mixed = jnp.einsum("hqk,khd->qhd", probs_low, value_heads, preferred_element_type=jnp.float32)
    return (mixed.reshape(row_count, -1).astype(jnp.bfloat16), row_max, row_total)


def attend_back(query_low, key_low, value_low, allowed, row_max, row_total, mixed_grad):
    row_count = query_low.shape[0]
    scores = score_table(query_low, key_low, allowed)
    probs = jnp.exp(scores - row_max) / row_total
    probs_low = probs.astype(jnp.bfloat16)
    query_heads = query_low.reshape(row_count, -1, HEAD_DIM)
    key_heads = key_low.reshape(row_count, -1, HEAD_DIM)
    value_heads = value_low.reshape(row_count, -1, HEAD_DIM)
    grad_heads = mixed_grad.reshape(row_count, -1, HEAD_DIM)
    value_grad = jnp.einsum(
        "hqk,qhd->khd", probs_low, grad_heads, preferred_element_type=jnp.float32
    )
    prob_grad = jnp.einsum(
        "qhd,khd->hqk", grad_heads, value_heads, preferred_element_type=jnp.float32
    )
    score_grad = (
        probs
        * (prob_grad - jnp.sum(probs * prob_grad, axis=-1, keepdims=True))
        * HEAD_DIM ** (-0.5)
    )
    score_low = score_grad.astype(jnp.bfloat16)
    query_grad = jnp.einsum(
        "hqk,khd->qhd", score_low, key_heads, preferred_element_type=jnp.float32
    )
    key_grad = jnp.einsum(
        "hqk,qhd->khd", score_low, query_heads, preferred_element_type=jnp.float32
    )
    return (
        query_grad.reshape(row_count, -1),
        key_grad.reshape(row_count, -1),
        value_grad.reshape(row_count, -1).astype(jnp.bfloat16),
    )


def term_rows(operands, partners):
    pieces = [
        lax.dot_general(
            operand, partner, (((0,), (0,)), ((), ())), preferred_element_type=jnp.float32
        )
        for operand, partner in zip(operands, partners)
    ]
    return jnp.concatenate(pieces, axis=1)


def on_device(
    tokens,
    segment_ids,
    query_proj,
    key_proj,
    value_proj,
    out_proj,
    query_gain,
    key_gain,
    attn_gain,
    gate_proj,
    up_proj,
    down_proj,
    mlp_gain,
    cotangent,
):
    micro_count = tokens.shape[0]
    shard_rows = query_proj.shape[0]
    head_width = query_proj.shape[1]
    hidden_width = gate_proj.shape[1]
    shards = (query_proj, key_proj, value_proj, out_proj, gate_proj, up_proj, down_proj)
    weight_total = jnp.zeros((shard_rows, 4 * head_width + 3 * hidden_width), jnp.float32)
    query_gain_total = jnp.zeros(query_gain.shape, jnp.float32)
    key_gain_total = jnp.zeros(key_gain.shape, jnp.float32)
    attn_gain_total = jnp.zeros(attn_gain.shape, jnp.float32)
    mlp_gain_total = jnp.zeros(mlp_gain.shape, jnp.float32)
    outputs = []
    input_grads = []
    for micro_index in range(micro_count):
        tokens_row = tokens[micro_index, 0]
        segment_row = segment_ids[micro_index, 0]
        cotangent_row = cotangent[micro_index, 0].astype(jnp.float32)
        residual_in = tokens_row.astype(jnp.float32)
        places = positions(segment_row)
        indices = jnp.arange(segment_row.shape[0], dtype=jnp.int32)
        allowed = (segment_row[None, :] == segment_row[:, None]) & (
            indices[None, :] <= indices[:, None]
        )
        query_full, key_full, value_full, out_full = gather_attention(shards[:4])
        queries = dot_plain(tokens_row, query_full)
        keyed = dot_plain(tokens_row, key_full)
        value_low = dot_plain(tokens_row, value_full).astype(jnp.bfloat16)
        query_sq, key_sq = lax.psum(
            (jnp.sum(queries * queries, axis=1), jnp.sum(keyed * keyed, axis=1)), "tensor"
        )
        query_scale = lax.rsqrt(query_sq / D + EPSILON)[:, None]
        key_scale = lax.rsqrt(key_sq / D + EPSILON)[:, None]
        query_normed = queries * query_scale * query_gain
        key_normed = keyed * key_scale * key_gain
        query_turned, query_turn_pull = jax.vjp(
            lambda entries: rotary(entries, places), query_normed
        )
        key_turned, key_turn_pull = jax.vjp(lambda entries: rotary(entries, places), key_normed)
        query_low = query_turned.astype(jnp.bfloat16)
        key_low = key_turned.astype(jnp.bfloat16)
        mixed_low, row_max, row_total = attend(query_low, key_low, value_low, allowed)
        projected = lax.psum(dot_transposed(mixed_low, out_full), "tensor")
        attn_normed, attn_pull = jax.vjp(rms_norm, projected, attn_gain)
        hidden = residual_in + attn_normed
        hidden_low = hidden.astype(jnp.bfloat16)
        gate_full, up_full, down_full = gather_feedforward(shards[4:])
        gated = dot_plain(hidden_low, gate_full)
        lifted = dot_plain(hidden_low, up_full)
        active, swish_pull = jax.vjp(swish_product, gated, lifted)
        active_low = active.astype(jnp.bfloat16)
        reduced = lax.psum(dot_transposed(active_low, down_full), "tensor")
        mlp_normed, mlp_pull = jax.vjp(rms_norm, reduced, mlp_gain)
        outputs.append((hidden + mlp_normed).astype(jnp.bfloat16))
        reduced_grad, mlp_gain_part = mlp_pull(cotangent_row)
        reduced_low = reduced_grad.astype(jnp.bfloat16)
        gate_back, up_back, down_back = gather_feedforward(shards[4:])
        active_grad = dot_plain(reduced_low, down_back)
        gated_grad, lifted_grad = swish_pull(active_grad)
        gated_low = gated_grad.astype(jnp.bfloat16)
        lifted_low = lifted_grad.astype(jnp.bfloat16)
        hidden_part = dot_transposed(gated_low, gate_back) + dot_transposed(lifted_low, up_back)
        hidden_grad = cotangent_row + lax.psum(hidden_part.astype(jnp.bfloat16), "tensor").astype(
            jnp.float32
        )
        projected_grad, attn_gain_part = attn_pull(hidden_grad)
        projected_low = projected_grad.astype(jnp.bfloat16)
        query_back, key_back, value_back, out_back = gather_attention(shards[:4])
        mixed_grad = dot_plain(projected_low, out_back).astype(jnp.bfloat16)
        query_rot_grad, key_rot_grad, value_grad_low = attend_back(
            query_low, key_low, value_low, allowed, row_max, row_total, mixed_grad
        )
        query_normed_grad = query_turn_pull(query_rot_grad)[0]
        key_normed_grad = key_turn_pull(key_rot_grad)[0]
        query_weighted = query_normed_grad * query_gain
        key_weighted = key_normed_grad * key_gain
        query_dot, key_dot = lax.psum(
            (jnp.sum(queries * query_weighted, axis=1), jnp.sum(keyed * key_weighted, axis=1)),
            "tensor",
        )
        query_grad_low = (
            query_scale * query_weighted
            - queries * (query_scale * query_scale * query_scale) * query_dot[:, None] / D
        ).astype(jnp.bfloat16)
        key_grad_low = (
            key_scale * key_weighted
            - keyed * (key_scale * key_scale * key_scale) * key_dot[:, None] / D
        ).astype(jnp.bfloat16)
        query_gain_total = query_gain_total + jnp.sum(
            query_normed_grad * queries * query_scale, axis=0
        )
        key_gain_total = key_gain_total + jnp.sum(key_normed_grad * keyed * key_scale, axis=0)
        attn_gain_total = attn_gain_total + attn_gain_part
        mlp_gain_total = mlp_gain_total + mlp_gain_part
        input_part = (
            dot_transposed(query_grad_low, query_back)
            + dot_transposed(key_grad_low, key_back)
            + dot_transposed(value_grad_low, value_back)
        )
        input_grads.append(
            hidden_grad + lax.psum(input_part.astype(jnp.bfloat16), "tensor").astype(jnp.float32)
        )
        operands = (tokens_row, projected_low, hidden_low, reduced_low)
        partners = (
            jnp.concatenate([query_grad_low, key_grad_low, value_grad_low], axis=1),
            mixed_low,
            jnp.concatenate([gated_low, lifted_low], axis=1),
            active_low,
        )
        weight_total = weight_total + lax.psum_scatter(
            term_rows(operands, partners), "dp", scatter_dimension=0, tiled=True
        )
    query_gain_grad, key_gain_grad, attn_gain_grad, mlp_gain_grad = lax.psum(
        (query_gain_total, key_gain_total, attn_gain_total, mlp_gain_total), "dp"
    )
    bounds = [
        0,
        head_width,
        2 * head_width,
        3 * head_width,
        4 * head_width,
        4 * head_width + hidden_width,
        4 * head_width + 2 * hidden_width,
        4 * head_width + 3 * hidden_width,
    ]
    splits = [weight_total[:, bounds[member] : bounds[member + 1]] for member in range(7)]
    layer_out = jnp.stack(outputs)[:, None]
    tokens_grad = jnp.stack(input_grads)[:, None]
    return (
        layer_out,
        tokens_grad,
        splits[0],
        splits[1],
        splits[2],
        splits[3],
        query_gain_grad,
        key_gain_grad,
        attn_gain_grad,
        splits[4],
        splits[5],
        splits[6],
        mlp_gain_grad,
    )


def solution(mesh):
    in_specs = (
        P(None, "dp", None, None),
        P(None, "dp", None),
        P("dp", "tensor"),
        P("dp", "tensor"),
        P("dp", "tensor"),
        P("dp", "tensor"),
        P("tensor"),
        P("tensor"),
        P(),
        P("dp", "tensor"),
        P("dp", "tensor"),
        P("dp", "tensor"),
        P(),
        P(None, "dp", None, None),
    )
    out_specs = (
        P(None, "dp", None, None),
        P(None, "dp", None, None),
        P("dp", "tensor"),
        P("dp", "tensor"),
        P("dp", "tensor"),
        P("dp", "tensor"),
        P("tensor"),
        P("tensor"),
        P(),
        P("dp", "tensor"),
        P("dp", "tensor"),
        P("dp", "tensor"),
        P(),
    )
    return jax.shard_map(
        on_device, mesh=mesh, in_specs=in_specs, out_specs=out_specs, check_vma=False
    )
```

profile of v0, /device:TPU:24, one launch (start us, length us, event | category | flops | bytes accessed | tf_op | source)
XLA Modules:
  0.0 2426.2 jit_solution(7313031411303650972)
XLA Ops:
  11.6 48.7 %all-gather.12.cloned.1.call-done = bf16[2048,1024]{1,0:T(8,128)(2,1)} async-done(((bf16[128,1024]{1,0:T(8,128)(2,1)}), bf16[2048,1024]{1,0:T(8,128)(2,1)}) %all-gather.12.cloned.1.call-update) | async-done | bytes 4194320 | tf_op jit(solution)/shard_map/all_gather | solution.py:66
  60.3 3.3 multiply_reduce_fusion.14
  64.7 46.8 %all-gather.10.cloned.1.call-done = bf16[2048,1024]{1,0:T(8,128)(2,1)} async-done(((bf16[128,1024]{1,0:T(8,128)(2,1)}), bf16[2048,1024]{1,0:T(8,128)(2,1)}) %all-gather.10.cloned.1.call-update) | async-done | bytes 4194320 | tf_op jit(solution)/shard_map/all_gather | solution.py:66
  111.5 3.1 multiply_reduce_fusion.15
  115.8 4.9 all-reduce.10
  124.7 2.5 fusion.151
  127.2 35.6 %all-gather.8.cloned.1.call-done = bf16[2048,1024]{1,0:T(8,128)(2,1)} async-done(((bf16[128,1024]{1,0:T(8,128)(2,1)}), bf16[2048,1024]{1,0:T(8,128)(2,1)}) %all-gather.8.cloned.1.call-update) | async-done | bytes 4194320 | tf_op jit(solution)/shard_map/all_gather | solution.py:66
  162.8 2.9 fusion.34
  165.7 1.7 convolution_convert_fusion.3
  170.3 3.0 fusion.35
  174.0 39.8 %all-gather.14.cloned.1.call-done = bf16[2048,1024]{1,0:T(8,128)(2,1)} async-done(((bf16[128,1024]{1,0:T(8,128)(2,1)}), bf16[2048,1024]{1,0:T(8,128)(2,1)}) %all-gather.14.cloned.1.call-update) | async-done | bytes 4194320 | tf_op jit(solution)/shard_map/all_gather | solution.py:66
  213.9 4.8 fusion.155
  218.7 2.5 fusion.152
  223.6 60.9 %all-reduce.22.cloned.1.call-done = (f32[128,2048]{1,0:T(8,128)}, f32[128,2048]{1,0:T(8,128)}) async-done(((f32[128,2048]{1,0:T(8,128)}, f32[128,2048]{1,0:T(8,128)}), (f32[128,2048]{1,0:T(8,128)}, f32[128,2048]{1,0:T(8,128)})) %all-reduce.22.cloned.1.call-update) | async-done | bytes 2097168 | tf_op jit(solution)/shard_map/psum | solution.py:201
  287.8 1.9 fusion.62
  289.8 122.0 %all-gather.16.cloned.1.call-done = bf16[2048,4096]{1,0:T(8,128)(2,1)} async-done(((bf16[128,4096]{1,0:T(8,128)(2,1)}), bf16[2048,4096]{1,0:T(8,128)(2,1)}) %all-gather.16.cloned.1.call-update) | async-done | bytes 16777232 | tf_op jit(solution)/shard_map/all_gather | solution.py:74
  411.7 9.6 fusion.153
  421.3 2.1 copy-done
  423.4 3.7 fusion.156
  427.2 112.0 %all-gather.18.cloned.1.call-done = bf16[2048,4096]{1,0:T(8,128)(2,1)} async-done(((bf16[128,4096]{1,0:T(8,128)(2,1)}), bf16[2048,4096]{1,0:T(8,128)(2,1)}) %all-gather.18.cloned.1.call-update) | async-done | bytes 16777232 | tf_op jit(solution)/shard_map/all_gather | solution.py:74
  539.2 10.5 multiply_convert_fusion.2
  549.7 1.9 copy-done.1
  552.2 4.4 multiply_convert_fusion.3
  556.6 110.1 %all-gather.20.cloned.1.call-done = bf16[2048,4096]{1,0:T(8,128)(2,1)} async-done(((bf16[128,4096]{1,0:T(8,128)(2,1)}), bf16[2048,4096]{1,0:T(8,128)(2,1)}) %all-gather.20.cloned.1.call-update) | async-done | bytes 16777232 | tf_op jit(solution)/shard_map/all_gather | solution.py:74
  666.7 12.8 fusion.157
  679.5 12.4 fusion.154
  692.0 63.3 %all-reduce.20.cloned.1.call-done = (f32[128,2048]{1,0:T(8,128)}, f32[128,2048]{1,0:T(8,128)}) async-done(((f32[128,2048]{1,0:T(8,128)}, f32[128,2048]{1,0:T(8,128)}), (f32[128,2048]{1,0:T(8,128)}, f32[128,2048]{1,0:T(8,128)})) %all-reduce.20.cloned.1.call-update) | async-done | bytes 2097168 | tf_op jit(solution)/shard_map/psum | solution.py:210
  755.3 1.5 multiply_reduce_fusion.4
  758.3 2.9 fusion.42
  762.4 14.9 fusion.163
  777.4 7.2 multiply_convert_fusion
  784.6 24.4 %fusion.12 = f32[2048,8192]{1,0:T(8,128)} fusion(bf16[128,2048]{1,0:T(8,128)(2,1)S(1)} %get-tuple-element.96, bf16[128,4096]{1,0:T(8,128)(2,1)S(1)} %get-tuple-element.75, bf16[128,4096]{1,0:T(8,128)(2,1)} %get-tuple-element.76), kind=kOutput, calls=%fused_computation.22 | convolution fusion | flops 4299161600 | bytes 69730304 | tf_op jit(solution)/shard_map/dot_general | solution.py:137
  809.0 10.6 multiply_convert_fusion.1
  821.0 23.7 fusion.8
  844.7 12.7 fusion.160
  857.4 12.8 fusion.158
  870.2 12.4 fusion.4
  882.6 12.6 fusion.5
  895.4 17.3 fusion.165
  912.6 23.0 all-reduce.26.cloned.1.call-done
  935.7 5.2 fusion.64
  946.1 2.6 convolution_bitcast_fusion.5
  948.8 2.4 convolution_bitcast_fusion.3
  951.2 3.0 convolution_convert_fusion.4
  954.4 1.8 convolution_convert_fusion
  957.2 2.2 convolution_bitcast_fusion.4
  959.4 2.9 convolution_bitcast_fusion.2
  962.3 4.6 fusion.164
  966.9 4.7 fusion.162
  974.0 2.6 multiply_add_fusion.7
  979.1 4.9 all-reduce.9
  984.0 2.8 subtract_convert_fusion.2
  986.8 2.1 subtract_convert_fusion.3
  989.0 11.1 convolution_bitcast_fusion.1
  1000.1 24.8 %copy.65 = f32[2048,3072]{1,0:T(8,128)} copy(f32[2048,3072]{0,1:T(8,128)} %convolution_bitcast_fusion.1) | data formatting | bytes 50331648 | tf_op jit(solution)/shard_map/dot_general | solution.py:137
  1024.9 10.2 convolution_bitcast_fusion
  1041.8 2.3 fusion.6
  1044.1 2.3 fusion.7
  1046.5 127.4 %maximum_add_fusion = f32[2048,16384]{1,0:T(8,128)} fusion(f32[2048,4096]{1,0:T(8,128)} %fusion.163, f32[2048,8192]{1,0:T(8,128)} %fusion.8, f32[2048,1024]{1,0:T(8,128)} %fusion.162, f32[2048,3072]{1,0:T(8,128)} %copy.65, f32[2048,4096]{1,0:T(8,128)} %fusion.165, f32[2048,8192]{1,0:T(8,128)} %fusion.12, f32[2048,1024]{1,0:T(8,128)} %fusion.164, ...), kind=kLoop, calls=%fused_computation.4 | loop fusion | flops 234881024 | bytes 402653184 | tf_op jit(solution)/shard_map/add | solution.py:268
  1174.7 51.5 %all-reduce.8 = (f32[1024]{0:T(1024)}, f32[1024]{0:T(1024)}, f32[2048]{0:T(1024)}, f32[2048]{0:T(1024)}) all-reduce(f32[1024]{0:T(1024)S(1)} %add.216, f32[1024]{0:T(1024)S(1)} %add.217, f32[2048]{0:T(1024)S(1)} %add.218, f32[2048]{0:T(1024)S(1)} %add.219), channel_id=1, replica_groups=mesh['dp'=16,'tensor'=2] {'dp'}, use_global_device_ids=true, to_apply=%region_44.45 | all-reduce | flops 6144 | bytes 49152 | tf_op jit(solution)/shard_map/psum | solution.py:271
  1227.3 1.9 add_bitcast_fusion.1
  1230.7 1179.6 %reduce-scatter.2.cloned.1.call-done = f32[128,16384]{1,0:T(8,128)} async-done(((f32[2048,16384]{1,0:T(8,128)}), f32[128,16384]{1,0:T(8,128)}) %reduce-scatter.2.cloned.1.call-update) | async-done | bytes 8388624 | tf_op jit(solution)/shard_map/reduce_scatter | solution.py:268
  2410.4 2.9 fusion.145
  2413.3 5.8 fusion.144
  (347 shorter events, 45.1 us)
Async XLA Ops:
  7.2 56.4 %copy-start.9 = (bf16[2,1,128,2048]{3,2,1,0:T(8,128)(2,1)S(1)}, bf16[2,1,128,2048]{3,2,1,0:T(8,128)(2,1)}, u32[]{:S(2)}) copy-start(bf16[2,1,128,2048]{3,2,1,0:T(8,128)(2,1)} %param.14) | copy-start | bytes 3145732
  7.2 53.1 %all-gather.12.cloned.1.call-start = ((), (), s32[]{:S(2)}) async-start(), calls=%async_computation.3 | async-start | bytes 4456448 | tf_op jit(solution)/shard_map/all_gather | solution.py:66
  7.9 103.6 %all-gather.10.cloned.1.call-start = ((), (), s32[]{:S(2)}) async-start(), calls=%async_computation.2 | async-start | bytes 4456448 | tf_op jit(solution)/shard_map/all_gather | solution.py:66
  8.7 154.1 %all-gather.8.cloned.1.call-start = ((), (), s32[]{:S(2)}) async-start(), calls=%async_computation.1 | async-start | bytes 4456448 | tf_op jit(solution)/shard_map/all_gather | solution.py:66
  9.4 204.5 %all-gather.14.cloned.1.call-start = ((), (), s32[]{:S(2)}) async-start(), calls=%async_computation.4 | async-start | bytes 4456448 | tf_op jit(solution)/shard_map/all_gather | solution.py:66
  10.0 274.5 %all-reduce.22.cloned.1.call-start = ((), (), s32[]{:S(2)}) async-start(), calls=%async_computation.10 | async-start | bytes 4194304 | tf_op jit(solution)/shard_map/psum | solution.py:201
  11.0 154.7 %copy-start.103 = (pred[128,128]{0,1:T(8,128)(4,1)}, pred[128,128]{0,1:T(8,128)(4,1)S(1)}, u32[]{:S(2)}) copy-start(pred[128,128]{0,1:T(8,128)(4,1)S(1)} %get-tuple-element.168) | copy-start | bytes 49156
  11.0 162.4 %copy-start.102 = (pred[128,128]{0,1:T(8,128)(4,1)}, pred[128,128]{0,1:T(8,128)(4,1)S(1)}, u32[]{:S(2)}) copy-start(pred[128,128]{0,1:T(8,128)(4,1)S(1)} %get-tuple-element.167) | copy-start | bytes 49156
  11.5 111.9 %copy-start.66 = (f32[128,64]{1,0:T(8,128)}, f32[128,64]{1,0:T(8,128)S(1)}, u32[]{:S(2)}) copy-start(f32[128,64]{1,0:T(8,128)S(1)} %get-tuple-element.135) | copy-start | bytes 98308
  11.5 111.9 %copy-start.68 = (f32[128,64]{1,0:T(8,128)}, f32[128,64]{1,0:T(8,128)S(1)}, u32[]{:S(2)}) copy-start(f32[128,64]{1,0:T(8,128)S(1)} %get-tuple-element.136) | copy-start | bytes 98308
  11.5 156.4 %copy-start.70 = (f32[128,64]{1,0:T(8,128)}, f32[128,64]{1,0:T(8,128)S(1)}, u32[]{:S(2)}) copy-start(f32[128,64]{1,0:T(8,128)S(1)} %get-tuple-element.149) | copy-start | bytes 98308
  11.6 156.3 %copy-start.72 = (f32[128,64]{1,0:T(8,128)}, f32[128,64]{1,0:T(8,128)S(1)}, u32[]{:S(2)}) copy-start(f32[128,64]{1,0:T(8,128)S(1)} %get-tuple-element.150) | copy-start | bytes 98308
  63.9 58.0 %copy-start.21 = (f32[128,1024]{1,0:T(8,128)}, f32[128,1024]{1,0:T(8,128)S(1)}, u32[]{:S(2)}) copy-start(f32[128,1024]{1,0:T(8,128)S(1)} %get-tuple-element.152) | copy-start | bytes 1572868
  64.7 57.2 %copy-start.23 = (f32[128,1024]{1,0:T(8,128)}, f32[128,1024]{1,0:T(8,128)S(1)}, u32[]{:S(2)}) copy-start(f32[128,1024]{1,0:T(8,128)S(1)} %get-tuple-element.156) | copy-start | bytes 1572868
  64.7 57.2 %copy-start.90 = (f32[1024]{0:T(1024)S(1)}, f32[1024]{0:T(1024)}, u32[]{:S(2)}) copy-start(f32[1024]{0:T(1024)} %param.21) | copy-start | bytes 12292
  124.7 41.0 %copy-start.76 = (bf16[128,8,64]{2,0,1:T(8,128)(2,1)}, bf16[128,8,64]{2,0,1:T(8,128)(2,1)S(1)}, u32[]{:S(2)}) copy-start(bf16[128,8,64]{2,0,1:T(8,128)(2,1)S(1)} %get-tuple-element.78) | copy-start | bytes 393220
  124.7 42.8 %copy-start.74 = (bf16[128,8,64]{2,0,1:T(8,128)(2,1)}, bf16[128,8,64]{2,0,1:T(8,128)(2,1)S(1)}, u32[]{:S(2)}) copy-start(bf16[128,8,64]{2,0,1:T(8,128)(2,1)S(1)} %get-tuple-element.77) | copy-start | bytes 393220
  124.7 41.0 %copy-start.78 = (bf16[128,8,64]{2,0,1:T(8,128)(2,1)S(1)}, bf16[128,8,64]{2,0,1:T(8,128)(2,1)}, u32[]{:S(2)}) copy-start(bf16[128,8,64]{2,0,1:T(8,128)(2,1)} %get-tuple-element.119) | copy-start | bytes 393220
  127.2 40.5 %copy-start.124 = (f32[8,128]{1,0:T(8,128)}, f32[8,128]{1,0:T(8,128)S(1)}, u32[]{:S(2)}) copy-start(f32[8,128]{1,0:T(8,128)S(1)} %get-tuple-element.161) | copy-start | bytes 12292
  167.5 51.2 %copy-start.62 = (bf16[8,128,128]{2,1,0:T(8,128)(2,1)}, bf16[8,128,128]{2,1,0:T(8,128)(2,1)S(1)}, u32[]{:S(2)}) copy-start(bf16[8,128,128]{2,1,0:T(8,128)(2,1)S(1)} %convolution_convert_fusion.3) | copy-start | bytes 786436
  170.3 48.4 %copy-start.126 = (f32[8,128]{1,0:T(8,128)}, f32[8,128]{1,0:T(8,128)S(1)}, u32[]{:S(2)}) copy-start(f32[8,128]{1,0:T(8,128)S(1)} %get-tuple-element.159) | copy-start | bytes 12292
  173.3 45.4 %copy-start.60 = (bf16[16,8,8,128]{3,2,1,0:T(8,128)(2,1)}, bf16[16,8,8,128]{3,2,1,0:T(8,128)(2,1)S(1)}, u32[]{:S(2)}) copy-start(bf16[16,8,8,128]{3,2,1,0:T(8,128)(2,1)S(1)} %fusion.35) | copy-start | bytes 786436
  174.0 47.2 %copy-start.64 = (bf16[8,128,128]{2,1,0:T(8,128)(2,1)}, bf16[8,128,128]{2,1,0:T(8,128)(2,1)S(1)}, u32[]{:S(2)}) copy-start(bf16[8,128,128]{2,1,0:T(8,128)(2,1)S(1)} %convolution_convert_fusion.2) | copy-start | bytes 786436
  221.2 66.6 %copy-start.88 = (f32[2048]{0:T(1024)S(1)}, f32[2048]{0:T(1024)}, u32[]{:S(2)}) copy-start(f32[2048]{0:T(1024)} %param.22) | copy-start | bytes 24580
  221.3 190.5 %all-gather.16.cloned.1.call-start = ((), (), s32[]{:S(2)}) async-start(), calls=%async_computation.5 | async-start | bytes 17825792 | tf_op jit(solution)/shard_map/all_gather | solution.py:74
  221.8 317.4 %all-gather.18.cloned.1.call-start = ((), (), s32[]{:S(2)}) async-start(), calls=%async_computation.6 | async-start | bytes 17825792 | tf_op jit(solution)/shard_map/all_gather | solution.py:74
  222.6 444.1 %all-gather.20.cloned.1.call-start = ((), (), s32[]{:S(2)}) async-start(), calls=%async_computation.7 | async-start | bytes 17825792 | tf_op jit(solution)/shard_map/all_gather | solution.py:74
  223.3 532.0 %all-reduce.20.cloned.1.call-start = ((), (), s32[]{:S(2)}) async-start(), calls=%async_computation.9 | async-start | bytes 4194304 | tf_op jit(solution)/shard_map/psum | solution.py:210
  287.8 133.5 %copy-start.112 = (f32[128]{0:T(128)}, f32[128]{0:T(128)S(1)}, u32[]{:S(2)}) copy-start(f32[128]{0:T(128)S(1)} %fusion.118) | copy-start | bytes 1540
  287.8 133.5 %copy-start.114 = (f32[128]{0:T(128)}, f32[128]{0:T(128)S(1)}, u32[]{:S(2)}) copy-start(f32[128]{0:T(128)S(1)} %fusion.116) | copy-start | bytes 1540
  411.7 11.7 copy-start
  539.2 12.3 copy-start.1
  539.2 13.0 copy-start.49
  552.2 114.5 %copy-start.43 = (bf16[128,4096]{1,0:T(8,128)(2,1)}, bf16[128,4096]{1,0:T(8,128)(2,1)S(1)}, u32[]{:S(2)}) copy-start(bf16[128,4096]{1,0:T(8,128)(2,1)S(1)} %get-tuple-element.163) | copy-start | bytes 3145732
  556.6 122.8 %copy-start.44 = (bf16[128,4096]{1,0:T(8,128)(2,1)}, bf16[128,4096]{1,0:T(8,128)(2,1)S(1)}, u32[]{:S(2)}) copy-start(bf16[128,4096]{1,0:T(8,128)(2,1)S(1)} %get-tuple-element.165) | copy-start | bytes 3145732
  691.9 66.4 %copy-start.11 = (bf16[2,1,128,2048]{3,2,1,0:T(8,128)(2,1)S(1)}, bf16[2,1,128,2048]{3,2,1,0:T(8,128)(2,1)}, u32[]{:S(2)}) copy-start(bf16[2,1,128,2048]{3,2,1,0:T(8,128)(2,1)} %param.27) | copy-start | bytes 3145732
  691.9 66.4 %copy-start.87 = (f32[2048]{0:T(1024)S(1)}, f32[2048]{0:T(1024)}, u32[]{:S(2)}) copy-start(f32[2048]{0:T(1024)} %param.26) | copy-start | bytes 24580
  691.9 243.7 %all-reduce.26.cloned.1.call-start = ((), (), s32[]{:S(2)}) async-start(), calls=%async_computation.12 | async-start | bytes 2097152 | tf_op jit(solution)/shard_map/psum | solution.py:221
  761.2 16.1 slice-start
  762.4 14.9 copy-start.46
  762.4 14.9 slice-start.1
  762.4 14.9 slice-start.2
  762.4 14.9 slice-start.3
  784.6 24.4 %copy-start.47 = (bf16[128,2048]{1,0:T(8,128)(2,1)S(1)}, bf16[128,2048]{1,0:T(8,128)(2,1)}, u32[]{:S(2)}) copy-start(bf16[128,2048]{1,0:T(8,128)(2,1)} %copy-done.46) | copy-start | bytes 1572868
  857.4 12.8 copy-start.41
  895.3 40.4 %copy-start.10 = (bf16[2,1,128,2048]{3,2,1,0:T(8,128)(2,1)S(1)}, bf16[2,1,128,2048]{3,2,1,0:T(8,128)(2,1)}, u32[]{:S(2)}) copy-start(bf16[2,1,128,2048]{3,2,1,0:T(8,128)(2,1)} %param.14) | copy-start | bytes 3145732
  895.3 40.4 %copy-start.13 = (f32[128,2048]{1,0:T(8,128)S(1)}, f32[128,2048]{1,0:T(8,128)}, u32[]{:S(2)}) copy-start(f32[128,2048]{1,0:T(8,128)} %get-tuple-element.60) | copy-start | bytes 3145732
  895.3 40.4 %copy-start.89 = (f32[2048]{0:T(1024)S(1)}, f32[2048]{0:T(1024)}, u32[]{:S(2)}) copy-start(f32[2048]{0:T(1024)} %param.22) | copy-start | bytes 24580
  895.3 40.4 %copy-start.113 = (f32[128]{0:T(128)S(1)}, f32[128]{0:T(128)}, u32[]{:S(2)}) copy-start(f32[128]{0:T(128)} %copy-done.112) | copy-start | bytes 1540
  895.3 40.4 %copy-start.115 = (f32[128]{0:T(128)S(1)}, f32[128]{0:T(128)}, u32[]{:S(2)}) copy-start(f32[128]{0:T(128)} %copy-done.114) | copy-start | bytes 1540
  895.3 332.0 %all-reduce.24.cloned.1.call-start = ((), (), s32[]{:S(2)}) async-start(), calls=%async_computation.11 | async-start | bytes 2097152 | tf_op jit(solution)/shard_map/psum | solution.py:259
  945.9 26.6 %copy-start.54 = (bf16[8,128,128]{2,1,0:T(8,128)(2,1)}, bf16[8,128,128]{2,1,0:T(8,128)(2,1)S(1)}, u32[]{:S(2)}) copy-start(bf16[8,128,128]{2,1,0:T(8,128)(2,1)S(1)} %convolution_convert_fusion.1) | copy-start | bytes 786436
  956.2 15.4 copy-start.56
  977.9 8.9 copy-start.116
  977.9 8.9 copy-start.117
  1000.0 24.8 %copy-start.48 = (bf16[128,1024]{1,0:T(8,128)(2,1)S(1)}, bf16[128,1024]{1,0:T(8,128)(2,1)}, u32[]{:S(2)}) copy-start(bf16[128,1024]{1,0:T(8,128)(2,1)} %get-tuple-element.124) | copy-start | bytes 786436
  1000.1 24.8 %copy-start.53 = (bf16[128,1024]{1,0:T(8,128)(2,1)S(1)}, bf16[128,1024]{1,0:T(8,128)(2,1)}, u32[]{:S(2)}) copy-start(bf16[128,1024]{1,0:T(8,128)(2,1)} %copy.91) | copy-start | bytes 786436
  1024.9 10.2 copy-start.6
  1046.5 1363.9 %reduce-scatter.2.cloned.1.call-start = ((), (), s32[]{:S(2)}) async-start(), calls=%async_computation.8 | async-start | bytes 142606336 | tf_op jit(solution)/shard_map/reduce_scatter | solution.py:268
  1174.0 52.3 %copy-start.50 = (bf16[1,128,2048]{2,1,0:T(8,128)(2,1)S(1)}, bf16[1,128,2048]{2,1,0:T(8,128)(2,1)}, u32[]{:S(2)}) copy-start(bf16[1,128,2048]{2,1,0:T(8,128)(2,1)} %get-tuple-element.85) | copy-start | bytes 1572868
  1174.0 52.2 %copy-start.51 = (bf16[1,128,2048]{2,1,0:T(8,128)(2,1)S(1)}, bf16[1,128,2048]{2,1,0:T(8,128)(2,1)}, u32[]{:S(2)}) copy-start(bf16[1,128,2048]{2,1,0:T(8,128)(2,1)} %get-tuple-element.86) | copy-start | bytes 1572868
  1174.0 53.3 %copy-start.12 = (bf16[2,1,128,2048]{3,2,1,0:T(8,128)(2,1)S(1)}, bf16[2,1,128,2048]{3,2,1,0:T(8,128)(2,1)}, u32[]{:S(2)}) copy-start(bf16[2,1,128,2048]{3,2,1,0:T(8,128)(2,1)} %param.27) | copy-start | bytes 3145732
  1174.0 53.3 %copy-start.29 = (bf16[128,2048]{1,0:T(8,128)(2,1)S(1)}, bf16[128,2048]{1,0:T(8,128)(2,1)}, u32[]{:S(2)}) copy-start(bf16[128,2048]{1,0:T(8,128)(2,1)} %get-tuple-element.64) | copy-start | bytes 1572868
  1174.0 53.3 %copy-start.31 = (bf16[128,2048]{1,0:T(8,128)(2,1)S(1)}, bf16[128,2048]{1,0:T(8,128)(2,1)}, u32[]{:S(2)}) copy-start(bf16[128,2048]{1,0:T(8,128)(2,1)} %get-tuple-element.65) | copy-start | bytes 1572868
  (80 other events, 286.8 us)
Sparse Core Ops, SparseCore 0:
  10.2 50.0 all-gather.11
  62.4 49.0 all-gather.9
  113.7 49.0 all-gather.7
  164.8 49.0 all-gather.13
  221.4 63.0 all-reduce.21
  286.7 124.9 all-gather.15
  414.1 125.0 all-gather.17
  541.6 125.0 all-gather.19
  692.1 63.1 all-reduce.19
  895.4 40.2 all-reduce.25
  1046.6 40.2 all-reduce.23
  1174.2 1236.1 reduce-scatter.1
where the time goes:
time: 2440 us; the launch traced here: 2430 us
  waiting for transfers between devices  1850 us (76%)
  matrix products  289 us (12%)
  other arithmetic  164 us (7%)
  blocking collectives  61.4 us (3%)
  local copies, waits for them, and re-layouts  48.5 us (2%)
    reduce_scatter x1, waiting for transfers between devices, on_device(): lax.psum_scatter(term_rows(operands, partners), 'dp', scatter_dimension=0...  1180 us
    all_gather x3, waiting for transfers between devices, gather_feedforward(): lax.all_gather(for_sending(shards), 'dp', axis=0, tiled=True)  344 us
    all_gather x4, waiting for transfers between devices, gather_attention(): lax.all_gather(for_sending(shards), 'dp', axis=0, tiled=True)  171 us
    add x1, other arithmetic, on_device(): weight_total + lax.psum_scatter(term_rows(operands, partners), 'dp', scat...  127 us
    dot_general x8, matrix products, term_rows(): lax.dot_general(operand, partner, (((0,), (0,)), ((), ())), preferred_ele...  111 us
    dot_general x14, matrix products, dot_transposed(): lax.dot_general(operand, partner, (((1,), (1,)), ((), ())), preferred_ele...  93.7 us
    dot_general x14, matrix products, dot_plain(): return jnp.dot(operand, partner, preferred_element_type=jnp.float32)  63.7 us
    psum x1, waiting for transfers between devices, on_device(): reduced = lax.psum(dot_transposed(active_low, down_full), 'tensor')  63.3 us
  transfers between devices with their start and end apart: 12, of which 11 were waited for; matrix products, arithmetic and copies ran while one was open for 9% of the time, Pallas kernels for 0%

commit v1 on v0

v1 whole, which is shorter than its diff:
```python
import math

import jax
import jax.numpy as jnp
from jax import lax
from jax.sharding import Mesh, PartitionSpec as P

D = 2048
HEAD_DIM = 128
EPSILON = 1e-06
ROPE_BASE = 500000.0
GROUP = 4
CORES = 2
F32 = jnp.float32
BF16 = jnp.bfloat16
TEAM = ("g", "c")


def dot(a, b):
    return jnp.dot(a, b, preferred_element_type=F32)


def dot_nt(a, b):
    return lax.dot_general(a, b, (((1,), (1,)), ((), ())), preferred_element_type=F32)


def dot_tn(a, b):
    return lax.dot_general(a, b, (((0,), (0,)), ((), ())), preferred_element_type=F32)


def swap(value, axis):
    return lax.ppermute(value, axis, [(0, 1), (1, 0)])


def shift(value, by):
    return lax.ppermute(value, "g", [(i, (i + by) % GROUP) for i in range(GROUP)])


def pick(value, index, axis):
    return lax.dynamic_index_in_dim(value, index, axis, keepdims=False)


def put(value, piece, index, axis=0):
    return lax.dynamic_update_index_in_dim(value, piece, index, axis)


def ordered(flag, first, second, axis):
    return jnp.where(
        flag == 0, jnp.stack([first, second], axis), jnp.stack([second, first], axis)
    )


class Place:
    def __init__(self, reps):
        self.reps = reps
        self.g = lax.axis_index("g")
        self.q = lax.axis_index("q")
        self.c = lax.axis_index("c")
        self.x = lax.axis_index("x")

    def to_local(self, value):
        lead = value.shape[:-1]
        value = value.reshape(lead + (GROUP, self.reps, D // (GROUP * self.reps)))
        value = jnp.swapaxes(value, -3, -2)
        if self.reps == 2:
            value = jnp.where(self.q == 0, value, jnp.flip(value, -3))
        return value.reshape(lead + (D,))

    def to_global(self, value):
        lead = value.shape[:-1]
        value = value.reshape(lead + (self.reps, GROUP, D // (GROUP * self.reps)))
        if self.reps == 2:
            value = jnp.where(self.q == 0, value, jnp.flip(value, -3))
        return jnp.swapaxes(value, -3, -2).reshape(lead + (D,))

    def spread(self, shard):
        rows, _, width = shard.shape
        shard = shard.reshape(rows, GROUP, CORES, width)
        mine = pick(shard, self.c, 2)
        got = swap(pick(shard, 1 - self.c, 2), "c")
        both = ordered(self.c, mine, got, 0)
        held = jnp.zeros((GROUP, CORES, rows, width), shard.dtype)
        for by in range(GROUP):
            piece = pick(both, (self.g + by) % GROUP, 2)
            if by:
                piece = shift(piece, by)
            held = put(held, piece, (self.g - by) % GROUP)
        return held.reshape(GROUP * CORES * rows, width)

    def widen(self, held):
        if self.reps != 2:
            tall = lax.all_gather(held, "q", axis=0, tiled=True)
            return tall, swap(tall, "x")
        half = held.shape[0] // 2
        beside = swap(held, "x")
        below = swap(held, "q")
        corner_top = swap(beside[:half], "q")
        corner_low = swap(below[half:], "x")
        return (
            jnp.concatenate([held, below], 0),
            jnp.concatenate([beside, corner_top, corner_low], 0),
        )

    def narrow(self, own, other):
        if self.reps != 2:
            own = own + swap(other, "x")
            return lax.psum_scatter(own, "q", scatter_dimension=0, tiled=True)
        size = own.shape[0] // 2
        half = size // 2
        keep, below = own[:size], own[size:]
        beside, corner = other[:size], other[size:]
        add = lambda a, b: (a.astype(F32) + b.astype(F32)).astype(BF16)
        top = swap(corner[:half], "q")
        low = swap(corner[half:], "x")
        beside = jnp.concatenate([add(beside[:half], top), beside[half:]], 0)
        below = jnp.concatenate([below[:half], add(below[half:], low)], 0)
        from_x = swap(beside, "x")
        from_q = swap(below, "q")
        return (keep.astype(F32) + from_x.astype(F32) + from_q.astype(F32)).astype(BF16)

    def collect(self, held):
        width = held.shape[1]
        held = held.reshape(GROUP, CORES, -1, width)
        slots = jnp.zeros_like(held)
        for by in range(GROUP):
            piece = pick(held, (self.g + by) % GROUP, 0)
            if by:
                piece = shift(piece, by)
            slots = put(slots, piece, (self.g - by) % GROUP)
        mine = pick(slots, self.c, 1)
        got = swap(pick(slots, 1 - self.c, 1), "c")
        both = ordered(self.c, mine, got, 1)
        return both.reshape(GROUP * CORES, -1, width)

    def team_sum(self, value):
        value = value + swap(value, "c")
        for step in (1, 2):
            value = value + lax.ppermute(value, "g", [(i, i ^ step) for i in range(GROUP)])
        return value

    def total(self, value):
        value = self.team_sum(value)
        value = value + swap(value, "x")
        return value + swap(value, "q") if self.reps == 2 else lax.psum(value, "q")


def rope_tables(segments):
    places = jnp.arange(segments.shape[1], dtype=jnp.int32)
    same = segments[:, :, None] == segments[:, None, :]
    earlier = same & (places[None, None, :] < places[None, :, None])
    allowed = same & (places[None, None, :] <= places[None, :, None])
    spot = jnp.sum(earlier.astype(jnp.int32), axis=2).astype(F32)
    halfway = HEAD_DIM // 2
    inverse = jnp.exp(jnp.arange(halfway, dtype=F32) * (-2.0 * math.log(ROPE_BASE) / HEAD_DIM))
    angles = spot[:, :, None] * inverse
    return allowed, jnp.cos(angles), jnp.sin(angles)


def turn(values, cosine, sine):
    halfway = HEAD_DIM // 2
    a, b = values[..., :halfway], values[..., halfway:]
    cosine, sine = cosine[:, :, None], sine[:, :, None]
    return jnp.concatenate([a * cosine - b * sine, b * cosine + a * sine], -1)


def norm_scale(values):
    return lax.rsqrt(jnp.mean(values * values, axis=-1, keepdims=True) + EPSILON)


def norm_back(values, scale, gain, grad):
    weighted = grad * gain
    inner = jnp.sum(values * weighted, axis=-1, keepdims=True) / D
    return (
        scale * weighted - values * (scale * scale * scale) * inner,
        jnp.sum(grad * values * scale, axis=0),
    )


def on_device(
    reps,
    tokens,
    segment_ids,
    query_proj,
    key_proj,
    value_proj,
    out_proj,
    query_gain,
    key_gain,
    attn_gain,
    gate_proj,
    up_proj,
    down_proj,
    mlp_gain,
    cotangent,
):
    place = Place(reps)
    slots = GROUP * CORES
    shard_rows = query_proj.shape[0]
    length = tokens.shape[2]
    slot = place.g * CORES + place.c

    own_row = place.to_local(pick(tokens, place.x, 0)[0])
    own_cotangent = place.to_local(pick(cotangent, place.x, 0)[0]).astype(F32)
    attn_gain = place.to_local(attn_gain)
    mlp_gain = place.to_local(mlp_gain)

    by_slot = lambda w: w.reshape(shard_rows, slots, -1)
    attn_shard = jnp.concatenate(
        [by_slot(w) for w in (query_proj, key_proj, value_proj, out_proj)], axis=2
    )
    attn_held = place.spread(attn_shard)
    all_rows = lax.all_gather(own_row, TEAM, axis=0, tiled=True)

    segments = pick(segment_ids, place.x, 0)
    segments = ordered(place.c, segments, swap(segments, "c"), 0)[:, 0]
    gathered = jnp.zeros((GROUP,) + segments.shape, segments.dtype)
    for by in range(GROUP):
        piece = shift(segments, by) if by else segments
        gathered = put(gathered, piece, (place.g - by) % GROUP)
    segments = gathered.reshape(slots, length)
    allowed, cosine, sine = rope_tables(segments)

    gains = jnp.stack([pick(w.reshape(slots, HEAD_DIM), slot, 0) for w in (query_gain, key_gain)])
    gains = jnp.stack([gains, swap(gains, "x")], 1)

    attn_own, attn_other = place.widen(attn_held)
    gate_full = jnp.concatenate(place.widen(place.spread(by_slot(gate_proj))), 1)
    up_full = jnp.concatenate(place.widen(place.spread(by_slot(up_proj))), 1)
    down_full = jnp.concatenate(place.widen(place.spread(by_slot(down_proj))), 1)

    cut = 3 * HEAD_DIM
    qkv_full = jnp.concatenate([attn_own[:, :cut], attn_other[:, :cut]], 1)
    out_full = jnp.concatenate([attn_own[:, cut:], attn_other[:, cut:]], 1)

    qkv = dot(all_rows, qkv_full).reshape(slots, length, 2, 3, HEAD_DIM)
    queries, keyed, value_low = qkv[:, :, :, 0], qkv[:, :, :, 1], qkv[:, :, :, 2].astype(BF16)
    squares = jnp.stack(
        [jnp.sum(queries * queries, axis=(2, 3)), jnp.sum(keyed * keyed, axis=(2, 3))]
    )
    scales = lax.rsqrt(place.team_sum(squares) / D + EPSILON)[:, :, :, None, None]
    query_low = turn(queries * scales[0] * gains[0], cosine, sine).astype(BF16)
    key_low = turn(keyed * scales[1] * gains[1], cosine, sine).astype(BF16)

    def einsum(spec, a, b):
        return jnp.einsum(spec, a, b, preferred_element_type=F32)

    root = HEAD_DIM ** (-0.5)
    scores = einsum("bqhd,bkhd->bhqk", query_low, key_low) * root
    scores = jnp.where(allowed[:, None], scores, -1e30)
    expo = jnp.exp(scores - jnp.max(scores, axis=-1, keepdims=True))
    probs = expo / jnp.sum(expo, axis=-1, keepdims=True)
    probs_low = probs.astype(BF16)
    mixed = einsum("bhqk,bkhd->bqhd", probs_low, value_low).astype(BF16)
    mixed = mixed.reshape(slots * length, 2 * HEAD_DIM)

    def team_scatter(value):
        return lax.psum_scatter(
            value.astype(BF16), TEAM, scatter_dimension=0, tiled=True
        ).astype(F32)

    def team_gather(value):
        return lax.all_gather(value, TEAM, axis=0, tiled=True)

    projected = team_scatter(dot_nt(mixed, out_full))
    projected_scale = norm_scale(projected)
    hidden = own_row.astype(F32) + projected * projected_scale * attn_gain
    hidden_all = team_gather(hidden.astype(BF16))
    lifted = dot(hidden_all, up_full)
    gated = dot(hidden_all, gate_full)
    active = (gated / (1.0 + jnp.exp(-gated)) * lifted).astype(BF16)
    reduced = team_scatter(dot_nt(active, down_full))
    reduced_scale = norm_scale(reduced)

    reduced_grad, mlp_gain_grad = norm_back(reduced, reduced_scale, mlp_gain, own_cotangent)
    reduced_all = team_gather(reduced_grad.astype(BF16))
    own_out = place.to_global((hidden + reduced * reduced_scale * mlp_gain).astype(BF16))
    layer_out = ordered(place.x, own_out, swap(own_out, "x"), 0)[:, None]

    active_grad = dot(reduced_all, down_full)
    gate_sigmoid = 1.0 / (1.0 + jnp.exp(-gated))
    gated_grad = (active_grad * lifted * gate_sigmoid * (1.0 + gated * (1.0 - gate_sigmoid))).astype(
        BF16
    )
    lifted_grad = (active_grad * gated * gate_sigmoid).astype(BF16)
    hidden_grad = own_cotangent + team_scatter(
        dot_nt(gated_grad, gate_full) + dot_nt(lifted_grad, up_full)
    )
    projected_grad, attn_gain_grad = norm_back(projected, projected_scale, attn_gain, hidden_grad)
    projected_all = team_gather(projected_grad.astype(BF16))

    def send_grad(grad):
        width = grad.shape[1] // 2
        low = grad.astype(BF16)
        return place.collect(place.narrow(low[:, :width], low[:, width:]))

    down_grad = send_grad(dot_tn(reduced_all, active))
    gate_grad = send_grad(dot_tn(hidden_all, gated_grad))
    up_grad = send_grad(dot_tn(hidden_all, lifted_grad))

    mixed_grad = dot(projected_all, out_full).astype(BF16)
    mixed_grad = mixed_grad.reshape(slots, length, 2, HEAD_DIM)
    value_grad = einsum("bhqk,bqhd->bkhd", probs_low, mixed_grad)
    prob_grad = einsum("bqhd,bkhd->bhqk", mixed_grad, value_low)
    score_grad = (
        probs * (prob_grad - jnp.sum(probs * prob_grad, axis=-1, keepdims=True)) * root
    ).astype(BF16)
    query_normed_grad = turn(einsum("bhqk,bkhd->bqhd", score_grad, key_low), cosine, -sine)
    key_normed_grad = turn(einsum("bhqk,bqhd->bkhd", score_grad, query_low), cosine, -sine)
    query_weighted = query_normed_grad * gains[0]
    key_weighted = key_normed_grad * gains[1]
    inner = jnp.stack(
        [jnp.sum(queries * query_weighted, axis=(2, 3)), jnp.sum(keyed * key_weighted, axis=(2, 3))]
    )
    inner = place.team_sum(inner)[:, :, :, None, None] / D
    query_grad = scales[0] * query_weighted - queries * scales[0] ** 3 * inner[0]
    key_grad = scales[1] * key_weighted - keyed * scales[1] ** 3 * inner[1]
    qkv_grad = jnp.stack([query_grad, key_grad, value_grad], 3).astype(BF16)
    qkv_grad = qkv_grad.reshape(slots * length, 6 * HEAD_DIM)

    input_grad = hidden_grad + team_scatter(dot_nt(qkv_grad, qkv_full))
    own_grad = place.to_global(input_grad.astype(BF16))
    tokens_grad = ordered(place.x, own_grad, swap(own_grad, "x"), 0)[:, None].astype(F32)

    qkv_weight_grad = dot_tn(all_rows, qkv_grad).astype(BF16)
    out_weight_grad = dot_tn(projected_all, mixed).astype(BF16)
    attn_grad = place.collect(
        place.narrow(
            jnp.concatenate([qkv_weight_grad[:, :cut], out_weight_grad[:, :HEAD_DIM]], 1),
            jnp.concatenate([qkv_weight_grad[:, cut:], out_weight_grad[:, HEAD_DIM:]], 1),
        )
    )

    head_gain_grads = jnp.stack(
        [
            jnp.sum(query_normed_grad * queries * scales[0], axis=(0, 1)),
            jnp.sum(key_normed_grad * keyed * scales[1], axis=(0, 1)),
        ]
    )
    spots = jnp.zeros((2, 2, slots, HEAD_DIM), F32)
    for head in range(2):
        spots = lax.dynamic_update_slice(
            spots,
            head_gain_grads[:, head][:, None, None],
            (0, place.x if head == 0 else 1 - place.x, slot, 0),
        )
    summed = place.total(
        jnp.concatenate(
            [
                spots.reshape(2, D),
                place.to_global(attn_gain_grad)[None],
                place.to_global(mlp_gain_grad)[None],
            ]
        )
    )
    half_of = lambda v: pick(v.reshape(2, -1), place.x, 0)

    def unslot(grad):
        return jnp.swapaxes(grad, 0, 1).reshape(shard_rows, -1).astype(F32)

    return (
        layer_out,
        tokens_grad,
        *[unslot(attn_grad[:, :, i * HEAD_DIM : (i + 1) * HEAD_DIM]) for i in range(4)],
        half_of(summed[0]),
        half_of(summed[1]),
        summed[2],
        unslot(gate_grad),
        unslot(up_grad),
        unslot(down_grad),
        summed[3],
    )


def solution(mesh):
    reps = mesh.shape["dp"] // (GROUP * CORES)
    folded = Mesh(
        mesh.devices.reshape(GROUP, reps, CORES, mesh.shape["tensor"]), ("g", "q", "c", "x")
    )
    dp = ("g", "q", "c")
    row = P(None, dp, None, None)
    weight = P(dp, "x")
    gain = P("x")
    in_specs = (row, P(None, dp, None)) + (weight,) * 4 + (gain, gain, P()) + (weight,) * 3
    in_specs += (P(), row)
    out_specs = (row, row) + (weight,) * 4 + (gain, gain, P()) + (weight,) * 3 + (P(),)

    def body(*args):
        return on_device(reps, *args)

    return jax.shard_map(
        body, mesh=folded, in_specs=in_specs, out_specs=out_specs, check_vma=False
    )
```

time: 2440 us -> 965 us (0.40)
  waiting for transfers between devices: 1850 us -> 461 us
  matrix products: 289 us -> 154 us
  starting transfers between devices: 0.68 us -> 126 us
  other arithmetic: 164 us -> 74 us
  local copies, waits for them, and re-layouts: 48.5 us -> 127 us
  blocking collectives: 61.4 us -> 0 us
    reduce_scatter x1 -> x4, waiting for transfers between devices: 1180 us -> 138 us  [team_scatter(): lax.psum_scatter(value.astype(BF16), TEAM, scatter_dimension=0, tiled=True)]
    all_gather x7 -> x4, waiting for transfers between devices: 515 us -> 46 us  [the longest x3 46 us: team_gather(): return lax.all_gather(value, TEAM, axis=0, tiled=True)]
    ppermute x0 -> x82, waiting for transfers between devices: none -> 278 us  [the longest x49 169 us: swap(): return lax.ppermute(value, axis, [(0, 1), (1, 0)])]
    psum x4 -> x0, waiting for transfers between devices: 147 us -> none  [the longest x1 63.3 us: on_device(): reduced = lax.psum(dot_transposed(active_low, down_full), 'tensor')]
    dot_general x46 -> x20, matrix products: 285 us -> 151 us  [the longest x5 64.8 us: dot_nt(): lax.dot_general(a, b, (((1,), (1,)), ((), ())), preferred_element_type=F32)]
    add x5 -> x9, other arithmetic: 127 us -> 0.09 us  [the longest x3 0.04 us: team_sum(): value = value + swap(value, 'c')]
    ppermute x0 -> x82, starting transfers between devices: none -> 114 us  [the longest x27 53.3 us: shift(): lax.ppermute(value, 'g', [(i, (i + by) % GROUP) for i in range(GROUP)])]
    psum x3 -> x0, blocking collectives: 61.4 us -> none  [the longest x1 51.5 us: on_device(): lax.psum((query_gain_total, key_gain_total, attn_gain_total, mlp_gain_tot...]
  transfers between devices with their start and end apart: 12 -> 90, of which waited for: 11 -> 35; matrix products, arithmetic and copies ran while one was open for 9% -> 25% of each run, Pallas kernels for 0% -> 0%
where the time goes in v1:
time: 965 us; the launch traced here: 959 us
  waiting for transfers between devices  461 us (48%)
  matrix products  154 us (16%)
  local copies, waits for them, and re-layouts  127 us (13%)
  starting transfers between devices  126 us (13%)
  other arithmetic  74 us (8%)
  between operations  16.4 us (2%)
    ppermute x49, waiting for transfers between devices, swap(): return lax.ppermute(value, axis, [(0, 1), (1, 0)])  169 us
    reduce_scatter x4, waiting for transfers between devices, team_scatter(): lax.psum_scatter(value.astype(BF16), TEAM, scatter_dimension=0, tiled=True)  138 us
    ppermute x27, waiting for transfers between devices, shift(): lax.ppermute(value, 'g', [(i, (i + by) % GROUP) for i in range(GROUP)])  100 us
    dot_general x5, matrix products, dot_nt(): lax.dot_general(a, b, (((1,), (1,)), ((), ())), preferred_element_type=F32)  64.8 us
    ppermute x27, starting transfers between devices, shift(): lax.ppermute(value, 'g', [(i, (i + by) % GROUP) for i in range(GROUP)])  53.3 us
    dot_general x5, matrix products, dot(): return jnp.dot(a, b, preferred_element_type=F32)  51.5 us
    ppermute x49, starting transfers between devices, swap(): return lax.ppermute(value, axis, [(0, 1), (1, 0)])  46.5 us
    all_gather x3, waiting for transfers between devices, team_gather(): return lax.all_gather(value, TEAM, axis=0, tiled=True)  46 us
  transfers between devices with their start and end apart: 90, of which 35 were waited for; matrix products, arithmetic and copies ran while one was open for 25% of the time, Pallas kernels for 0%

profile of v1, /device:TPU:24, one launch (start us, length us, event | category | flops | bytes accessed | tf_op | source)
XLA Modules:
  0.0 959.2 jit_solution(18380242357748167907)
XLA Ops:
  17.8 10.9 %collective-permute-done.1 = bf16[2,128,512]{2,1,0:T(8,128)(2,1)S(1)} collective-permute-done((bf16[2,128,512]{2,1,0:T(8,128)(2,1)S(1)}, bf16[2,128,512]{2,1,0:T(8,128)(2,1)S(1)}, u32[]{:S(2)}, u32[]{:S(2)}) %collective-permute-start.1) | collective-permute-done | bytes 262176 | tf_op jit(solution)/shard_map/ppermute | solution.py:36
  28.8 35.8 %collective-permute-done.2 = bf16[2,128,512]{2,1,0:T(8,128)(2,1)S(1)} collective-permute-done((bf16[2,128,512]{2,1,0:T(8,128)(2,1)S(1)}, bf16[2,128,512]{2,1,0:T(8,128)(2,1)S(1)}, u32[]{:S(2)}, u32[]{:S(2)}) %collective-permute-start.2) | collective-permute-done | bytes 262176 | tf_op jit(solution)/shard_map/ppermute | solution.py:36
  71.4 15.4 %collective-permute-done.5 = bf16[1024,512]{1,0:T(8,128)(2,1)S(1)} collective-permute-done((bf16[1024,512]{1,0:T(8,128)(2,1)S(1)}, bf16[1024,512]{1,0:T(8,128)(2,1)S(1)}, u32[]{:S(2)}, u32[]{:S(2)}) %collective-permute-start.5) | collective-permute-done | bytes 1048608 | tf_op jit(solution)/shard_map/ppermute | solution.py:32
  92.6 3.7 collective-permute-done.6
  101.0 6.2 fusion.4
  113.9 3.0 collective-permute-start.13
  116.8 2.9 fusion.79
  119.8 6.2 collective-permute-start.14
  133.1 3.5 fusion.114
  139.3 3.4 convolution_convert_fusion
  143.5 46.3 %reduce-scatter.5.cloned.1.call-done = bf16[128,2048]{1,0:T(8,128)(2,1)} async-done(((bf16[1024,2048]{1,0:T(8,128)(2,1)}), bf16[128,2048]{1,0:T(8,128)(2,1)}) %reduce-scatter.5.cloned.1.call-update) | async-done | bytes 524304 | tf_op jit(solution)/shard_map/reduce_scatter | solution.py:257
  193.2 11.9 %reduce-scatter.7.cloned.1.call-start = ((), (), s32[]{:S(2)}) async-start(), calls=%async_computation.7 | async-start | bytes 4718592 | tf_op jit(solution)/shard_map/reduce_scatter | solution.py:257
  225.8 3.3 collective-permute-start.17
  231.6 3.2 collective-permute-start.25
  237.9 5.1 collective-permute-done.17
  245.0 14.9 %collective-permute-done.18 = bf16[2,128,512]{2,1,0:T(8,128)(2,1)S(1)} collective-permute-done((bf16[2,128,512]{2,1,0:T(8,128)(2,1)S(1)}, bf16[2,128,512]{2,1,0:T(8,128)(2,1)S(1)}, u32[]{:S(2)}, u32[]{:S(2)}) %collective-permute-start.18) | collective-permute-done | bytes 262176 | tf_op jit(solution)/shard_map/ppermute | solution.py:36
  260.0 13.1 %collective-permute-start.34 = (bf16[2,128,512]{2,1,0:T(8,128)(2,1)S(1)}, bf16[2,128,512]{2,1,0:T(8,128)(2,1)S(1)}, u32[]{:S(2)}, u32[]{:S(2)}) collective-permute-start(bf16[2,128,512]{2,1,0:T(8,128)(2,1)S(1)} %get-tuple-element.104), channel_id=1, source_target_pairs={{0,16},{8,24},{16,0},{24,8},{1,17},{9,25},{17,1},{25,9},{2,18},{10... | collective-permute-start | bytes 786440 | tf_op jit(solution)/shard_map/ppermute | solution.py:36
  273.1 4.2 collective-permute-start.35
  277.3 16.3 %collective-permute-done.26 = bf16[2,128,512]{2,1,0:T(8,128)(2,1)S(1)} collective-permute-done((bf16[2,128,512]{2,1,0:T(8,128)(2,1)S(1)}, bf16[2,128,512]{2,1,0:T(8,128)(2,1)S(1)}, u32[]{:S(2)}, u32[]{:S(2)}) %collective-permute-start.26) | collective-permute-done | bytes 262176 | tf_op jit(solution)/shard_map/ppermute | solution.py:36
  297.4 7.4 collective-permute-done.34
  307.9 11.6 %collective-permute-done.21 = bf16[1024,512]{1,0:T(8,128)(2,1)S(1)} collective-permute-done((bf16[1024,512]{1,0:T(8,128)(2,1)S(1)}, bf16[1024,512]{1,0:T(8,128)(2,1)S(1)}, u32[]{:S(2)}, u32[]{:S(2)}) %collective-permute-start.21) | collective-permute-done | bytes 1048608 | tf_op jit(solution)/shard_map/ppermute | solution.py:32
  322.8 19.3 %collective-permute-done.29 = bf16[1024,512]{1,0:T(8,128)(2,1)S(1)} collective-permute-done((bf16[1024,512]{1,0:T(8,128)(2,1)S(1)}, bf16[1024,512]{1,0:T(8,128)(2,1)S(1)}, u32[]{:S(2)}, u32[]{:S(2)}) %collective-permute-start.29) | collective-permute-done | bytes 1048608 | tf_op jit(solution)/shard_map/ppermute | solution.py:32
  346.0 18.5 %collective-permute-done.37 = bf16[1024,512]{1,0:T(8,128)(2,1)S(1)} collective-permute-done((bf16[1024,512]{1,0:T(8,128)(2,1)S(1)}, bf16[1024,512]{1,0:T(8,128)(2,1)S(1)}, u32[]{:S(2)}, u32[]{:S(2)}) %collective-permute-start.37) | collective-permute-done | bytes 1048608 | tf_op jit(solution)/shard_map/ppermute | solution.py:32
  369.3 8.2 collective-permute-done.22
  378.3 9.9 %fusion.104 = f32[1024,1024]{1,0:T(8,128)S(1)} fusion(bf16[1024,2048]{1,0:T(8,128)(2,1)} %all-gather.7.cloned.1.call-done, bf16[512,512]{1,0:T(8,128)(2,1)} %collective-permute-done.23, bf16[512,512]{1,0:T(8,128)(2,1)} %copy-done.82, bf16[1024,512]{1,0:T(8,128)(2,1)} %copy-done.49, bf16[1024,512]{1,0:T(8,128)(2,1)} %copy-done.51, ...), kind=kOutput, calls=%fused_computation.347 | convolution fusion | flops 4315938816 | bytes 12582912 | tf_op jit(solution)/shard_map/dot_general | solution.py:20
  388.8 17.1 %multiply_convert_fusion.2 = (bf16[1024,1024]{1,0:T(8,128)(2,1)S(1)}, f32[1024,1024]{1,0:T(8,128)}) fusion(f32[1024,1024]{1,0:T(8,128)S(1)} %fusion.104, bf16[1024,2048]{1,0:T(8,128)(2,1)S(1)} %copy-done.78, bf16[512,512]{1,0:T(8,128)(2,1)} %collective-permute-done.31, bf16[512,512]{1,0:T(8,128)(2,1)} %collective-permute-done.30, ...), kind=kOutput, calls=%fused_computation.8 | convolution fusion | flops 4321181696 | bytes 18874368 | tf_op jit(solution)/shard_map/dot_general | solution.py:20
  407.2 16.8 %convolution_convert_fusion.5 = bf16[1024,2048]{1,0:T(8,128)(2,1)} fusion(bf16[1024,1024]{1,0:T(8,128)(2,1)S(1)} %get-tuple-element.150, bf16[512,512]{1,0:T(8,128)(2,1)} %collective-permute-done.39, bf16[512,512]{1,0:T(8,128)(2,1)} %collective-permute-done.38, bf16[1024,512]{1,0:T(8,128)(2,1)S(1)} %copy-done.60, bf16[1024,512]{1,0:T(8,128)(2,1)S(1)} %copy-done.62, ...), kind=kOutput, calls=%fused_computation.16 | convolution fusion | flops 4318035968 | bytes 10485760 | tf_op jit(solution)/shard_map/dot_general | solution.py:24
  428.9 42.9 %reduce-scatter.7.cloned.1.call-done = bf16[128,2048]{1,0:T(8,128)(2,1)} async-done(((bf16[1024,2048]{1,0:T(8,128)(2,1)}), bf16[128,2048]{1,0:T(8,128)(2,1)}) %reduce-scatter.7.cloned.1.call-update) | async-done | bytes 524304 | tf_op jit(solution)/shard_map/reduce_scatter | solution.py:257
  476.7 45.9 %all-gather.9.cloned.1.call-done = bf16[1024,2048]{1,0:T(8,128)(2,1)} async-done(((bf16[128,2048]{1,0:T(8,128)(2,1)}), bf16[1024,2048]{1,0:T(8,128)(2,1)}) %all-gather.9.cloned.1.call-update) | async-done | bytes 4194320 | tf_op jit(solution)/shard_map/all_gather | solution.py:262
  522.7 13.9 %multiply_convert_fusion.1 = (bf16[1024,1024]{1,0:T(8,128)(2,1)}, bf16[1024,1024]{1,0:T(8,128)(2,1)}) fusion(f32[1024,1024]{1,0:T(8,128)} %copy-done.88, f32[1024,1024]{1,0:T(8,128)} %get-tuple-element.151, bf16[1024,2048]{1,0:T(8,128)(2,1)} %all-gather.9.cloned.1.call-done, bf16[512,512]{1,0:T(8,128)(2,1)} %collective-permute-done.39, ...), kind=kOutput, calls=%fused_computation.7 | convolution fusion | flops 4329570304 | bytes 20971520 | tf_op jit(solution)/shard_map/dot_general | solution.py:20
  536.6 16.7 %fusion.102 = f32[1024,2048]{1,0:T(8,128)S(1)} fusion(bf16[1024,1024]{1,0:T(8,128)(2,1)} %get-tuple-element.37, bf16[512,512]{1,0:T(8,128)(2,1)} %collective-permute-done.31, bf16[512,512]{1,0:T(8,128)(2,1)} %collective-permute-done.30, bf16[1024,512]{1,0:T(8,128)(2,1)S(1)} %copy-done.55, bf16[1024,512]{1,0:T(8,128)(2,1)S(1)} %copy-done.58, ...), kind=kOutput, calls=%fused_computation.345 | convolution fusion | flops 4315938816 | bytes 14680064 | tf_op jit(solution)/shard_map/dot_general | solution.py:24
  553.4 20.1 %add_convert_fusion = bf16[1024,2048]{1,0:T(8,128)(2,1)} fusion(f32[1024,2048]{1,0:T(8,128)S(1)} %fusion.102, bf16[1024,1024]{1,0:T(8,128)(2,1)} %get-tuple-element.36, bf16[512,512]{1,0:T(8,128)(2,1)} %collective-permute-done.23, bf16[512,512]{1,0:T(8,128)(2,1)S(1)} %copy-done.83, bf16[1024,512]{1,0:T(8,128)(2,1)S(1)} %copy-done.50, ...), kind=kOutput, calls=%fused_computation.2 | convolution fusion | flops 4320133120 | bytes 18874368 | tf_op jit(solution)/shard_map/dot_general | solution.py:24
  573.7 48.4 %reduce-scatter.9.cloned.1.call-done = bf16[128,2048]{1,0:T(8,128)(2,1)} async-done(((bf16[1024,2048]{1,0:T(8,128)(2,1)}), bf16[128,2048]{1,0:T(8,128)(2,1)}) %reduce-scatter.9.cloned.1.call-update) | async-done | bytes 524304 | tf_op jit(solution)/shard_map/reduce_scatter | solution.py:257
  623.5 2.7 fusion.24
  626.3 7.6 convolution_convert_fusion.3
  637.7 5.1 convolution_convert_fusion.2
  646.5 4.9 convolution_convert_fusion.4
  655.3 4.9 collective-permute-done.74
  664.7 6.7 collective-permute-done.58
  675.9 18.6 %collective-permute-done.67 = bf16[1024,512]{1,0:T(8,128)(2,1)S(1)} collective-permute-done((bf16[1024,512]{1,0:T(8,128)(2,1)S(1)}, bf16[1024,512]{1,0:T(8,128)(2,1)S(1)}, u32[]{:S(2)}, u32[]{:S(2)}) %collective-permute-start.67) | collective-permute-done | bytes 1048608 | tf_op jit(solution)/shard_map/ppermute | solution.py:32
  703.0 14.1 %collective-permute-done.75 = bf16[1024,512]{1,0:T(8,128)(2,1)} collective-permute-done((bf16[1024,512]{1,0:T(8,128)(2,1)}, bf16[1024,512]{1,0:T(8,128)(2,1)}, u32[]{:S(2)}, u32[]{:S(2)}) %collective-permute-start.75) | collective-permute-done | bytes 1048608 | tf_op jit(solution)/shard_map/ppermute | solution.py:32
  717.4 2.9 collective-permute-start.72
  724.7 14.3 %collective-permute-done.59 = bf16[1024,512]{1,0:T(8,128)(2,1)} collective-permute-done((bf16[1024,512]{1,0:T(8,128)(2,1)}, bf16[1024,512]{1,0:T(8,128)(2,1)}, u32[]{:S(2)}, u32[]{:S(2)}) %collective-permute-start.59) | collective-permute-done | bytes 1048608 | tf_op jit(solution)/shard_map/ppermute | solution.py:32
  747.0 4.4 convolution_convert_fusion.10
  756.4 3.2 convolution_bitcast_fusion
  759.6 4.3 convolution_bitcast_fusion.1
  769.5 3.3 collective-permute-start.62
  774.6 4.7 collective-permute-done.42
  781.1 2.8 collective-permute-done.43
  788.6 7.9 convolution_convert_fusion.1
  807.1 4.0 convolution_convert_fusion.6
  817.7 10.7 %collective-permute-done.45 = bf16[512,512]{0,1:T(8,128)(2,1)} collective-permute-done((bf16[512,512]{0,1:T(8,128)(2,1)}, bf16[512,512]{0,1:T(8,128)(2,1)}, u32[]{:S(2)}, u32[]{:S(2)}) %collective-permute-start.45) | collective-permute-done | bytes 524320 | tf_op jit(solution)/shard_map/ppermute | solution.py:32
  839.4 2.9 maximum_select_fusion.9
  845.8 10.3 %collective-permute-done.46 = bf16[1024,512]{0,1:T(8,128)(2,1)} collective-permute-done((bf16[1024,512]{0,1:T(8,128)(2,1)}, bf16[1024,512]{0,1:T(8,128)(2,1)}, u32[]{:S(2)}, u32[]{:S(2)}) %collective-permute-start.46) | collective-permute-done | bytes 1048608 | tf_op jit(solution)/shard_map/ppermute | solution.py:32
  856.0 3.5 collective-permute-done.48
  859.5 3.2 add_convert_fusion.4
  866.8 2.8 collective-permute-start.49
  871.8 2.7 maximum_select_fusion.8
  886.8 9.8 %collective-permute-done.50 = bf16[2,128,512]{2,1,0:T(8,128)(2,1)} collective-permute-done((bf16[2,128,512]{2,1,0:T(8,128)(2,1)}, bf16[2,128,512]{2,1,0:T(8,128)(2,1)}, u32[]{:S(2)}, u32[]{:S(2)}) %collective-permute-start.50) | collective-permute-done | bytes 262176 | tf_op jit(solution)/shard_map/ppermute | solution.py:36
  905.9 3.0 copy.270
  910.8 3.0 copy.269
  928.7 2.9 copy.268
  942.5 2.8 fusion.46
  945.3 4.5 collective-permute-done.40
  (583 shorter events, 258.3 us)
Async XLA Ops:
  7.2 93.8 %all-gather.5.cloned.1.call-start = ((), (), s32[]{:S(2)}) async-start(), calls=%async_computation.4 | async-start | bytes 4718592 | tf_op jit(solution)/shard_map/all_gather | solution.py:212
  10.5 179.3 %reduce-scatter.5.cloned.1.call-start = ((), (), s32[]{:S(2)}) async-start(), calls=%async_computation.5 | async-start | bytes 4718592 | tf_op jit(solution)/shard_map/reduce_scatter | solution.py:257
  13.2 55.7 %collective-permute-start.15 = (f32[2,128]{1,0:T(2,128)S(1)}, f32[2,128]{1,0:T(2,128)S(1)}, u32[]{:S(2)}, u32[]{:S(2)}) collective-permute-start(f32[2,128]{1,0:T(2,128)S(1)} %pad_maximum_fusion.35), channel_id=1, source_target_pairs={{0,1},{1,0},{2,3},{3,2},{4,5},{5,4},{6,7},{7,6},{8,9},{9,8},{10,11... | collective-permute-start | bytes 3080 | tf_op jit(solution)/shard_map/ppermute | solution.py:32
  15.5 50.8 %collective-permute-start.8 = (s32[1,128]{1,0:T(1,128)S(1)}, s32[1,128]{1,0:T(1,128)S(1)}, u32[]{:S(2)}, u32[]{:S(2)}) collective-permute-start(s32[1,128]{1,0:T(1,128)S(1)} %fusion.135), channel_id=1, source_target_pairs={{0,2},{2,0},{1,3},{3,1},{4,6},{6,4},{5,7},{7,5},{8,10},{10,8},{9,1... | collective-permute-start | bytes 1544 | tf_op jit(solution)/shard_map/ppermute | solution.py:32
  15.6 49.0 %collective-permute-start.2 = (bf16[2,128,512]{2,1,0:T(8,128)(2,1)S(1)}, bf16[2,128,512]{2,1,0:T(8,128)(2,1)S(1)}, u32[]{:S(2)}, u32[]{:S(2)}) collective-permute-start(bf16[2,128,512]{2,1,0:T(8,128)(2,1)S(1)} %get-tuple-element.121), channel_id=1, source_target_pairs={{0,16},{8,24},{16,0},{24,8},{1,17},{9,25},{17,1},{25,9},{2,18},{10... | collective-permute-start | bytes 786440 | tf_op jit(solution)/shard_map/ppermute | solution.py:36
  17.3 47.4 %collective-permute-start.3 = (bf16[2,128,512]{2,1,0:T(8,128)(2,1)S(1)}, bf16[2,128,512]{2,1,0:T(8,128)(2,1)S(1)}, u32[]{:S(2)}, u32[]{:S(2)}) collective-permute-start(bf16[2,128,512]{2,1,0:T(8,128)(2,1)S(1)} %get-tuple-element.120), channel_id=1, source_target_pairs={{0,24},{8,0},{16,8},{24,16},{1,25},{9,1},{17,9},{25,17},{2,26},{10... | collective-permute-start | bytes 786440 | tf_op jit(solution)/shard_map/ppermute | solution.py:36
  64.7 22.0 %collective-permute-start.5 = (bf16[1024,512]{1,0:T(8,128)(2,1)S(1)}, bf16[1024,512]{1,0:T(8,128)(2,1)S(1)}, u32[]{:S(2)}, u32[]{:S(2)}) collective-permute-start(bf16[1024,512]{1,0:T(8,128)(2,1)S(1)} %bitcast.365), channel_id=1, source_target_pairs={{0,1},{1,0},{2,3},{3,2},{4,5},{5,4},{6,7},{7,6},{8,9},{9,8},{10,11... | collective-permute-start | bytes 3145736 | tf_op jit(solution)/shard_map/ppermute | solution.py:32
  64.8 24.2 %collective-permute-start.4 = (bf16[1024,512]{1,0:T(8,128)(2,1)S(1)}, bf16[1024,512]{1,0:T(8,128)(2,1)S(1)}, u32[]{:S(2)}, u32[]{:S(2)}) collective-permute-start(bf16[1024,512]{1,0:T(8,128)(2,1)S(1)} %bitcast.366), channel_id=1, source_target_pairs={{0,4},{4,0},{1,5},{5,1},{2,6},{6,2},{3,7},{7,3},{8,12},{12,8},{9,1... | collective-permute-start | bytes 3145736 | tf_op jit(solution)/shard_map/ppermute | solution.py:32
  68.9 20.1 %collective-permute-start.11 = (s32[2,128]{1,0:T(2,128)S(1)}, s32[2,128]{1,0:T(2,128)S(1)}, u32[]{:S(2)}, u32[]{:S(2)}) collective-permute-start(s32[2,128]{1,0:T(2,128)S(1)} %add_select_fusion.1), channel_id=1, source_target_pairs={{0,24},{8,0},{16,8},{24,16},{1,25},{9,1},{17,9},{25,17},{2,26},{10... | collective-permute-start | bytes 3080 | tf_op jit(solution)/shard_map/ppermute | solution.py:36
  142.7 235.6 %all-gather.7.cloned.1.call-start = ((), (), s32[]{:S(2)}) async-start(), calls=%async_computation.6 | async-start | bytes 4718592 | tf_op jit(solution)/shard_map/all_gather | solution.py:262
  193.2 278.6 %reduce-scatter.7.cloned.1.call-start = ((), (), s32[]{:S(2)}) async-start(), calls=%async_computation.7 | async-start | bytes 4718592 | tf_op jit(solution)/shard_map/reduce_scatter | solution.py:257
  229.0 30.9 %collective-permute-start.18 = (bf16[2,128,512]{2,1,0:T(8,128)(2,1)S(1)}, bf16[2,128,512]{2,1,0:T(8,128)(2,1)S(1)}, u32[]{:S(2)}, u32[]{:S(2)}) collective-permute-start(bf16[2,128,512]{2,1,0:T(8,128)(2,1)S(1)} %get-tuple-element.109), channel_id=1, source_target_pairs={{0,16},{8,24},{16,0},{24,8},{1,17},{9,25},{17,1},{25,9},{2,18},{10... | collective-permute-start | bytes 786440 | tf_op jit(solution)/shard_map/ppermute | solution.py:36
  229.0 30.9 %collective-permute-start.19 = (bf16[2,128,512]{2,1,0:T(8,128)(2,1)S(1)}, bf16[2,128,512]{2,1,0:T(8,128)(2,1)S(1)}, u32[]{:S(2)}, u32[]{:S(2)}) collective-permute-start(bf16[2,128,512]{2,1,0:T(8,128)(2,1)S(1)} %get-tuple-element.108), channel_id=1, source_target_pairs={{0,24},{8,0},{16,8},{24,16},{1,25},{9,1},{17,9},{25,17},{2,26},{10... | collective-permute-start | bytes 786440 | tf_op jit(solution)/shard_map/ppermute | solution.py:36
  231.6 41.5 %collective-permute-start.25 = (bf16[2,128,512]{2,1,0:T(8,128)(2,1)S(1)}, bf16[2,128,512]{2,1,0:T(8,128)(2,1)S(1)}, u32[]{:S(2)}, u32[]{:S(2)}) collective-permute-start(bf16[2,128,512]{2,1,0:T(8,128)(2,1)S(1)} %get-tuple-element.115), channel_id=1, source_target_pairs={{0,8},{8,16},{16,24},{24,0},{1,9},{9,17},{17,25},{25,1},{2,10},{10... | collective-permute-start | bytes 786440 | tf_op jit(solution)/shard_map/ppermute | solution.py:36
  235.1 58.5 %collective-permute-start.26 = (bf16[2,128,512]{2,1,0:T(8,128)(2,1)S(1)}, bf16[2,128,512]{2,1,0:T(8,128)(2,1)S(1)}, u32[]{:S(2)}, u32[]{:S(2)}) collective-permute-start(bf16[2,128,512]{2,1,0:T(8,128)(2,1)S(1)} %get-tuple-element.114), channel_id=1, source_target_pairs={{0,16},{8,24},{16,0},{24,8},{1,17},{9,25},{17,1},{25,9},{2,18},{10... | collective-permute-start | bytes 786440 | tf_op jit(solution)/shard_map/ppermute | solution.py:36
  243.0 52.1 %collective-permute-start.27 = (bf16[2,128,512]{2,1,0:T(8,128)(2,1)S(1)}, bf16[2,128,512]{2,1,0:T(8,128)(2,1)S(1)}, u32[]{:S(2)}, u32[]{:S(2)}) collective-permute-start(bf16[2,128,512]{2,1,0:T(8,128)(2,1)S(1)} %get-tuple-element.113), channel_id=1, source_target_pairs={{0,24},{8,0},{16,8},{24,16},{1,25},{9,1},{17,9},{25,17},{2,26},{10... | collective-permute-start | bytes 786440 | tf_op jit(solution)/shard_map/ppermute | solution.py:36
  259.9 36.8 %collective-permute-start.33 = (bf16[2,128,512]{2,1,0:T(8,128)(2,1)S(1)}, bf16[2,128,512]{2,1,0:T(8,128)(2,1)S(1)}, u32[]{:S(2)}, u32[]{:S(2)}) collective-permute-start(bf16[2,128,512]{2,1,0:T(8,128)(2,1)S(1)} %get-tuple-element.105), channel_id=1, source_target_pairs={{0,8},{8,16},{16,24},{24,0},{1,9},{9,17},{17,25},{25,1},{2,10},{10... | collective-permute-start | bytes 786440 | tf_op jit(solution)/shard_map/ppermute | solution.py:36
  260.0 44.8 %collective-permute-start.34 = (bf16[2,128,512]{2,1,0:T(8,128)(2,1)S(1)}, bf16[2,128,512]{2,1,0:T(8,128)(2,1)S(1)}, u32[]{:S(2)}, u32[]{:S(2)}) collective-permute-start(bf16[2,128,512]{2,1,0:T(8,128)(2,1)S(1)} %get-tuple-element.104), channel_id=1, source_target_pairs={{0,16},{8,24},{16,0},{24,8},{1,17},{9,25},{17,1},{25,9},{2,18},{10... | collective-permute-start | bytes 786440 | tf_op jit(solution)/shard_map/ppermute | solution.py:36
  273.1 33.2 %collective-permute-start.35 = (bf16[2,128,512]{2,1,0:T(8,128)(2,1)S(1)}, bf16[2,128,512]{2,1,0:T(8,128)(2,1)S(1)}, u32[]{:S(2)}, u32[]{:S(2)}) collective-permute-start(bf16[2,128,512]{2,1,0:T(8,128)(2,1)S(1)} %get-tuple-element.103), channel_id=1, source_target_pairs={{0,24},{8,0},{16,8},{24,16},{1,25},{9,1},{17,9},{25,17},{2,26},{10... | collective-permute-start | bytes 786440 | tf_op jit(solution)/shard_map/ppermute | solution.py:36
  293.6 26.0 %collective-permute-start.21 = (bf16[1024,512]{1,0:T(8,128)(2,1)S(1)}, bf16[1024,512]{1,0:T(8,128)(2,1)S(1)}, u32[]{:S(2)}, u32[]{:S(2)}) collective-permute-start(bf16[1024,512]{1,0:T(8,128)(2,1)S(1)} %bitcast.398), channel_id=1, source_target_pairs={{0,1},{1,0},{2,3},{3,2},{4,5},{5,4},{6,7},{7,6},{8,9},{9,8},{10,11... | collective-permute-start | bytes 3145736 | tf_op jit(solution)/shard_map/ppermute | solution.py:32
  295.1 26.1 %collective-permute-start.20 = (bf16[1024,512]{1,0:T(8,128)(2,1)S(1)}, bf16[1024,512]{1,0:T(8,128)(2,1)S(1)}, u32[]{:S(2)}, u32[]{:S(2)}) collective-permute-start(bf16[1024,512]{1,0:T(8,128)(2,1)S(1)} %bitcast.399), channel_id=1, source_target_pairs={{0,4},{4,0},{1,5},{5,1},{2,6},{6,2},{3,7},{7,3},{8,12},{12,8},{9,1... | collective-permute-start | bytes 3145736 | tf_op jit(solution)/shard_map/ppermute | solution.py:32
  296.7 45.3 %collective-permute-start.29 = (bf16[1024,512]{1,0:T(8,128)(2,1)S(1)}, bf16[1024,512]{1,0:T(8,128)(2,1)S(1)}, u32[]{:S(2)}, u32[]{:S(2)}) collective-permute-start(bf16[1024,512]{1,0:T(8,128)(2,1)S(1)} %bitcast.402), channel_id=1, source_target_pairs={{0,1},{1,0},{2,3},{3,2},{4,5},{5,4},{6,7},{7,6},{8,9},{9,8},{10,11... | collective-permute-start | bytes 3145736 | tf_op jit(solution)/shard_map/ppermute | solution.py:32
  304.8 38.9 %collective-permute-start.28 = (bf16[1024,512]{1,0:T(8,128)(2,1)S(1)}, bf16[1024,512]{1,0:T(8,128)(2,1)S(1)}, u32[]{:S(2)}, u32[]{:S(2)}) collective-permute-start(bf16[1024,512]{1,0:T(8,128)(2,1)S(1)} %bitcast.403), channel_id=1, source_target_pairs={{0,4},{4,0},{1,5},{5,1},{2,6},{6,2},{3,7},{7,3},{8,12},{12,8},{9,1... | collective-permute-start | bytes 3145736 | tf_op jit(solution)/shard_map/ppermute | solution.py:32
  306.4 58.1 %collective-permute-start.37 = (bf16[1024,512]{1,0:T(8,128)(2,1)S(1)}, bf16[1024,512]{1,0:T(8,128)(2,1)S(1)}, u32[]{:S(2)}, u32[]{:S(2)}) collective-permute-start(bf16[1024,512]{1,0:T(8,128)(2,1)S(1)} %bitcast.406), channel_id=1, source_target_pairs={{0,1},{1,0},{2,3},{3,2},{4,5},{5,4},{6,7},{7,6},{8,9},{9,8},{10,11... | collective-permute-start | bytes 3145736 | tf_op jit(solution)/shard_map/ppermute | solution.py:32
  319.6 47.3 %collective-permute-start.36 = (bf16[1024,512]{1,0:T(8,128)(2,1)S(1)}, bf16[1024,512]{1,0:T(8,128)(2,1)S(1)}, u32[]{:S(2)}, u32[]{:S(2)}) collective-permute-start(bf16[1024,512]{1,0:T(8,128)(2,1)S(1)} %bitcast.407), channel_id=1, source_target_pairs={{0,4},{4,0},{1,5},{5,1},{2,6},{6,2},{3,7},{7,3},{8,12},{12,8},{9,1... | collective-permute-start | bytes 3145736 | tf_op jit(solution)/shard_map/ppermute | solution.py:32
  321.3 56.2 %collective-permute-start.22 = (bf16[512,512]{1,0:T(8,128)(2,1)S(1)}, bf16[512,512]{1,0:T(8,128)(2,1)S(1)}, u32[]{:S(2)}, u32[]{:S(2)}) collective-permute-start(bf16[512,512]{1,0:T(8,128)(2,1)S(1)} %slice.368), channel_id=1, source_target_pairs={{0,4},{4,0},{1,5},{5,1},{2,6},{6,2},{3,7},{7,3},{8,12},{12,8},{9,1... | collective-permute-start | bytes 1572872 | tf_op jit(solution)/shard_map/ppermute | solution.py:32
  342.1 36.2 %collective-permute-start.23 = (bf16[512,512]{1,0:T(8,128)(2,1)S(1)}, bf16[512,512]{1,0:T(8,128)(2,1)}, u32[]{:S(2)}, u32[]{:S(2)}) collective-permute-start(bf16[512,512]{1,0:T(8,128)(2,1)S(1)} %slice.369), channel_id=1, source_target_pairs={{0,1},{1,0},{2,3},{3,2},{4,5},{5,4},{6,7},{7,6},{8,9},{9,8},{10,11... | collective-permute-start | bytes 1572872 | tf_op jit(solution)/shard_map/ppermute | solution.py:32
  343.7 45.0 %collective-permute-start.30 = (bf16[512,512]{1,0:T(8,128)(2,1)S(1)}, bf16[512,512]{1,0:T(8,128)(2,1)}, u32[]{:S(2)}, u32[]{:S(2)}) collective-permute-start(bf16[512,512]{1,0:T(8,128)(2,1)S(1)} %slice.370), channel_id=1, source_target_pairs={{0,4},{4,0},{1,5},{5,1},{2,6},{6,2},{3,7},{7,3},{8,12},{12,8},{9,1... | collective-permute-start | bytes 1572872 | tf_op jit(solution)/shard_map/ppermute | solution.py:32
  364.5 24.3 %collective-permute-start.31 = (bf16[512,512]{1,0:T(8,128)(2,1)}, bf16[512,512]{1,0:T(8,128)(2,1)}, u32[]{:S(2)}, u32[]{:S(2)}) collective-permute-start(bf16[512,512]{1,0:T(8,128)(2,1)} %slice.371), channel_id=1, source_target_pairs={{0,1},{1,0},{2,3},{3,2},{4,5},{5,4},{6,7},{7,6},{8,9},{9,8},{10,11... | collective-permute-start | bytes 1572872 | tf_op jit(solution)/shard_map/ppermute | solution.py:32
  366.9 39.0 %collective-permute-start.38 = (bf16[512,512]{1,0:T(8,128)(2,1)}, bf16[512,512]{1,0:T(8,128)(2,1)}, u32[]{:S(2)}, u32[]{:S(2)}) collective-permute-start(bf16[512,512]{1,0:T(8,128)(2,1)} %slice.372), channel_id=1, source_target_pairs={{0,4},{4,0},{1,5},{5,1},{2,6},{6,2},{3,7},{7,3},{8,12},{12,8},{9,1... | collective-permute-start | bytes 1572872 | tf_op jit(solution)/shard_map/ppermute | solution.py:32
  377.5 28.5 %collective-permute-start.39 = (bf16[512,512]{1,0:T(8,128)(2,1)}, bf16[512,512]{1,0:T(8,128)(2,1)}, u32[]{:S(2)}, u32[]{:S(2)}) collective-permute-start(bf16[512,512]{1,0:T(8,128)(2,1)} %slice.373), channel_id=1, source_target_pairs={{0,1},{1,0},{2,3},{3,2},{4,5},{5,4},{6,7},{7,6},{8,9},{9,8},{10,11... | collective-permute-start | bytes 1572872 | tf_op jit(solution)/shard_map/ppermute | solution.py:32
  424.0 98.6 %all-gather.9.cloned.1.call-start = ((), (), s32[]{:S(2)}) async-start(), calls=%async_computation.8 | async-start | bytes 4718592 | tf_op jit(solution)/shard_map/all_gather | solution.py:262
  476.7 145.4 %reduce-scatter.9.cloned.1.call-start = ((), (), s32[]{:S(2)}) async-start(), calls=%async_computation.9 | async-start | bytes 4718592 | tf_op jit(solution)/shard_map/reduce_scatter | solution.py:257
  573.5 173.5 %all-gather.11.cloned.1.call-start = ((), (), s32[]{:S(2)}) async-start(), calls=%async_computation.10 | async-start | bytes 4718592 | tf_op jit(solution)/shard_map/all_gather | solution.py:262
  626.2 294.7 %reduce-scatter.11.cloned.1.call-start = ((), (), s32[]{:S(2)}) async-start(), calls=%async_computation.11 | async-start | bytes 4718592 | tf_op jit(solution)/shard_map/reduce_scatter | solution.py:257
  634.1 18.6 %collective-permute-start.66 = (bf16[512,512]{1,0:T(8,128)(2,1)S(1)}, bf16[512,512]{1,0:T(8,128)(2,1)S(1)}, u32[]{:S(2)}, u32[]{:S(2)}) collective-permute-start(bf16[512,512]{1,0:T(8,128)(2,1)S(1)} %get-tuple-element.46), channel_id=1, source_target_pairs={{0,4},{4,0},{1,5},{5,1},{2,6},{6,2},{3,7},{7,3},{8,12},{12,8},{9,1... | collective-permute-start | bytes 1572872 | tf_op jit(solution)/shard_map/ppermute | solution.py:32
  634.9 19.2 %collective-permute-start.68 = (bf16[512,512]{1,0:T(8,128)(2,1)S(1)}, bf16[512,512]{1,0:T(8,128)(2,1)S(1)}, u32[]{:S(2)}, u32[]{:S(2)}) collective-permute-start(bf16[512,512]{1,0:T(8,128)(2,1)S(1)} %get-tuple-element.47), channel_id=1, source_target_pairs={{0,1},{1,0},{2,3},{3,2},{4,5},{5,4},{6,7},{7,6},{8,9},{9,8},{10,11... | collective-permute-start | bytes 1572872 | tf_op jit(solution)/shard_map/ppermute | solution.py:32
  643.0 17.2 %collective-permute-start.74 = (bf16[512,512]{1,0:T(8,128)(2,1)S(1)}, bf16[512,512]{1,0:T(8,128)(2,1)S(1)}, u32[]{:S(2)}, u32[]{:S(2)}) collective-permute-start(bf16[512,512]{1,0:T(8,128)(2,1)S(1)} %get-tuple-element.40), channel_id=1, source_target_pairs={{0,4},{4,0},{1,5},{5,1},{2,6},{6,2},{3,7},{7,3},{8,12},{12,8},{9,1... | collective-permute-start | bytes 1572872 | tf_op jit(solution)/shard_map/ppermute | solution.py:32
  651.6 19.9 %collective-permute-start.58 = (bf16[512,512]{1,0:T(8,128)(2,1)S(1)}, bf16[512,512]{1,0:T(8,128)(2,1)S(1)}, u32[]{:S(2)}, u32[]{:S(2)}) collective-permute-start(bf16[512,512]{1,0:T(8,128)(2,1)S(1)} %get-tuple-element.52), channel_id=1, source_target_pairs={{0,4},{4,0},{1,5},{5,1},{2,6},{6,2},{3,7},{7,3},{8,12},{12,8},{9,1... | collective-permute-start | bytes 1572872 | tf_op jit(solution)/shard_map/ppermute | solution.py:32
  652.7 19.4 %collective-permute-start.60 = (bf16[512,512]{1,0:T(8,128)(2,1)S(1)}, bf16[512,512]{1,0:T(8,128)(2,1)S(1)}, u32[]{:S(2)}, u32[]{:S(2)}) collective-permute-start(bf16[512,512]{1,0:T(8,128)(2,1)S(1)} %get-tuple-element.53), channel_id=1, source_target_pairs={{0,1},{1,0},{2,3},{3,2},{4,5},{5,4},{6,7},{7,6},{8,9},{9,8},{10,11... | collective-permute-start | bytes 1572872 | tf_op jit(solution)/shard_map/ppermute | solution.py:32
  654.5 40.1 %collective-permute-start.67 = (bf16[1024,512]{1,0:T(8,128)(2,1)S(1)}, bf16[1024,512]{1,0:T(8,128)(2,1)S(1)}, u32[]{:S(2)}, u32[]{:S(2)}) collective-permute-start(bf16[1024,512]{1,0:T(8,128)(2,1)S(1)} %pad_maximum_fusion.14), channel_id=1, source_target_pairs={{0,1},{1,0},{2,3},{3,2},{4,5},{5,4},{6,7},{7,6},{8,9},{9,8},{10,11... | collective-permute-start | bytes 3145736 | tf_op jit(solution)/shard_map/ppermute | solution.py:32
  660.2 36.8 %collective-permute-start.69 = (bf16[1024,512]{1,0:T(8,128)(2,1)S(1)}, bf16[1024,512]{1,0:T(8,128)(2,1)}, u32[]{:S(2)}, u32[]{:S(2)}) collective-permute-start(bf16[1024,512]{1,0:T(8,128)(2,1)S(1)} %pad_maximum_fusion.15), channel_id=1, source_target_pairs={{0,4},{4,0},{1,5},{5,1},{2,6},{6,2},{3,7},{7,3},{8,12},{12,8},{9,1... | collective-permute-start | bytes 3145736 | tf_op jit(solution)/shard_map/ppermute | solution.py:32
  662.2 54.9 %collective-permute-start.75 = (bf16[1024,512]{1,0:T(8,128)(2,1)}, bf16[1024,512]{1,0:T(8,128)(2,1)}, u32[]{:S(2)}, u32[]{:S(2)}) collective-permute-start(bf16[1024,512]{1,0:T(8,128)(2,1)} %pad_maximum_fusion.16), channel_id=1, source_target_pairs={{0,1},{1,0},{2,3},{3,2},{4,5},{5,4},{6,7},{7,6},{8,9},{9,8},{10,11... | collective-permute-start | bytes 3145736 | tf_op jit(solution)/shard_map/ppermute | solution.py:32
  671.4 45.9 %collective-permute-start.77 = (bf16[1024,512]{1,0:T(8,128)(2,1)}, bf16[1024,512]{1,0:T(8,128)(2,1)}, u32[]{:S(2)}, u32[]{:S(2)}) collective-permute-start(bf16[1024,512]{1,0:T(8,128)(2,1)} %pad_maximum_fusion.17), channel_id=1, source_target_pairs={{0,4},{4,0},{1,5},{5,1},{2,6},{6,2},{3,7},{7,3},{8,12},{12,8},{9,1... | collective-permute-start | bytes 3145736 | tf_op jit(solution)/shard_map/ppermute | solution.py:32
  673.5 65.5 %collective-permute-start.59 = (bf16[1024,512]{1,0:T(8,128)(2,1)}, bf16[1024,512]{1,0:T(8,128)(2,1)}, u32[]{:S(2)}, u32[]{:S(2)}) collective-permute-start(bf16[1024,512]{1,0:T(8,128)(2,1)} %pad_maximum_fusion.12), channel_id=1, source_target_pairs={{0,1},{1,0},{2,3},{3,2},{4,5},{5,4},{6,7},{7,6},{8,9},{9,8},{10,11... | collective-permute-start | bytes 3145736 | tf_op jit(solution)/shard_map/ppermute | solution.py:32
  695.5 44.4 %collective-permute-start.61 = (bf16[1024,512]{1,0:T(8,128)(2,1)}, bf16[1024,512]{1,0:T(8,128)(2,1)}, u32[]{:S(2)}, u32[]{:S(2)}) collective-permute-start(bf16[1024,512]{1,0:T(8,128)(2,1)} %pad_maximum_fusion.13), channel_id=1, source_target_pairs={{0,4},{4,0},{1,5},{5,1},{2,6},{6,2},{3,7},{7,3},{8,12},{12,8},{9,1... | collective-permute-start | bytes 3145736 | tf_op jit(solution)/shard_map/ppermute | solution.py:32
  701.2 44.5 %collective-permute-start.70 = (bf16[2,128,512]{2,1,0:T(8,128)(2,1)S(1)}, bf16[2,128,512]{2,1,0:T(8,128)(2,1)S(1)}, u32[]{:S(2)}, u32[]{:S(2)}) collective-permute-start(bf16[2,128,512]{2,1,0:T(8,128)(2,1)S(1)} %get-tuple-element.81), channel_id=1, source_target_pairs={{0,8},{8,16},{16,24},{24,0},{1,9},{9,17},{17,25},{25,1},{2,10},{10... | collective-permute-start | bytes 786440 | tf_op jit(solution)/shard_map/ppermute | solution.py:36
  717.1 50.7 %collective-permute-start.71 = (bf16[2,128,512]{2,1,0:T(8,128)(2,1)}, bf16[2,128,512]{2,1,0:T(8,128)(2,1)}, u32[]{:S(2)}, u32[]{:S(2)}) collective-permute-start(bf16[2,128,512]{2,1,0:T(8,128)(2,1)} %get-tuple-element.80), channel_id=1, source_target_pairs={{0,16},{8,24},{16,0},{24,8},{1,17},{9,25},{17,1},{25,9},{2,18},{10... | collective-permute-start | bytes 786440 | tf_op jit(solution)/shard_map/ppermute | solution.py:36
  717.4 82.2 %collective-permute-start.72 = (bf16[2,128,512]{2,1,0:T(8,128)(2,1)S(1)}, bf16[2,128,512]{2,1,0:T(8,128)(2,1)}, u32[]{:S(2)}, u32[]{:S(2)}) collective-permute-start(bf16[2,128,512]{2,1,0:T(8,128)(2,1)S(1)} %get-tuple-element.79), channel_id=1, source_target_pairs={{0,24},{8,0},{16,8},{24,16},{1,25},{9,1},{17,9},{25,17},{2,26},{10... | collective-permute-start | bytes 786440 | tf_op jit(solution)/shard_map/ppermute | solution.py:36
  739.0 33.9 %collective-permute-start.78 = (bf16[2,128,512]{2,1,0:T(8,128)(2,1)}, bf16[2,128,512]{2,1,0:T(8,128)(2,1)}, u32[]{:S(2)}, u32[]{:S(2)}) collective-permute-start(bf16[2,128,512]{2,1,0:T(8,128)(2,1)} %get-tuple-element.75), channel_id=1, source_target_pairs={{0,8},{8,16},{16,24},{24,0},{1,9},{9,17},{17,25},{25,1},{2,10},{10... | collective-permute-start | bytes 786440 | tf_op jit(solution)/shard_map/ppermute | solution.py:36
  739.9 56.6 %collective-permute-start.79 = (bf16[2,128,512]{2,1,0:T(8,128)(2,1)}, bf16[2,128,512]{2,1,0:T(8,128)(2,1)}, u32[]{:S(2)}, u32[]{:S(2)}) collective-permute-start(bf16[2,128,512]{2,1,0:T(8,128)(2,1)} %get-tuple-element.74), channel_id=1, source_target_pairs={{0,16},{8,24},{16,0},{24,8},{1,17},{9,25},{17,1},{25,9},{2,18},{10... | collective-permute-start | bytes 786440 | tf_op jit(solution)/shard_map/ppermute | solution.py:36
  745.8 53.8 %collective-permute-start.80 = (bf16[2,128,512]{2,1,0:T(8,128)(2,1)}, bf16[2,128,512]{2,1,0:T(8,128)(2,1)}, u32[]{:S(2)}, u32[]{:S(2)}) collective-permute-start(bf16[2,128,512]{2,1,0:T(8,128)(2,1)} %get-tuple-element.73), channel_id=1, source_target_pairs={{0,24},{8,0},{16,8},{24,16},{1,25},{9,1},{17,9},{25,17},{2,26},{10... | collective-permute-start | bytes 786440 | tf_op jit(solution)/shard_map/ppermute | solution.py:36
  769.5 34.2 %collective-permute-start.62 = (bf16[2,128,512]{2,1,0:T(8,128)(2,1)S(1)}, bf16[2,128,512]{2,1,0:T(8,128)(2,1)S(1)}, u32[]{:S(2)}, u32[]{:S(2)}) collective-permute-start(bf16[2,128,512]{2,1,0:T(8,128)(2,1)S(1)} %copy-done.48), channel_id=1, source_target_pairs={{0,8},{8,16},{16,24},{24,0},{1,9},{9,17},{17,25},{25,1},{2,10},{10... | collective-permute-start | bytes 786440 | tf_op jit(solution)/shard_map/ppermute | solution.py:36
  783.8 31.1 %collective-permute-start.63 = (bf16[2,128,512]{2,1,0:T(8,128)(2,1)}, bf16[2,128,512]{2,1,0:T(8,128)(2,1)}, u32[]{:S(2)}, u32[]{:S(2)}) collective-permute-start(bf16[2,128,512]{2,1,0:T(8,128)(2,1)} %get-tuple-element.86), channel_id=1, source_target_pairs={{0,16},{8,24},{16,0},{24,8},{1,17},{9,25},{17,1},{25,9},{2,18},{10... | collective-permute-start | bytes 786440 | tf_op jit(solution)/shard_map/ppermute | solution.py:36
  796.5 101.8 %collective-permute-start.64 = (bf16[2,128,512]{2,1,0:T(8,128)(2,1)}, bf16[2,128,512]{2,1,0:T(8,128)(2,1)}, u32[]{:S(2)}, u32[]{:S(2)}) collective-permute-start(bf16[2,128,512]{2,1,0:T(8,128)(2,1)} %get-tuple-element.85), channel_id=1, source_target_pairs={{0,24},{8,0},{16,8},{24,16},{1,25},{9,1},{17,9},{25,17},{2,26},{10... | collective-permute-start | bytes 786440 | tf_op jit(solution)/shard_map/ppermute | solution.py:36
  803.7 34.5 %collective-permute-start.81 = (bf16[4,128,512]{2,1,0:T(8,128)(2,1)}, bf16[4,128,512]{2,1,0:T(8,128)(2,1)}, u32[]{:S(2)}, u32[]{:S(2)}) collective-permute-start(bf16[4,128,512]{2,1,0:T(8,128)(2,1)} %get-tuple-element.72), channel_id=1, source_target_pairs={{0,2},{2,0},{1,3},{3,1},{4,6},{6,4},{5,7},{7,5},{8,10},{10,8},{9,1... | collective-permute-start | bytes 1572872 | tf_op jit(solution)/shard_map/ppermute | solution.py:32
  830.9 25.1 %collective-permute-start.46 = (bf16[1024,512]{0,1:T(8,128)(2,1)}, bf16[1024,512]{0,1:T(8,128)(2,1)}, u32[]{:S(2)}, u32[]{:S(2)}) collective-permute-start(bf16[1024,512]{0,1:T(8,128)(2,1)} %pad_maximum_fusion.10), channel_id=1, source_target_pairs={{0,1},{1,0},{2,3},{3,2},{4,5},{5,4},{6,7},{7,6},{8,9},{9,8},{10,11... | collective-permute-start | bytes 3145736 | tf_op jit(solution)/shard_map/ppermute | solution.py:32
  834.7 24.8 %collective-permute-start.48 = (bf16[1024,512]{0,1:T(8,128)(2,1)}, bf16[1024,512]{0,1:T(8,128)(2,1)}, u32[]{:S(2)}, u32[]{:S(2)}) collective-permute-start(bf16[1024,512]{0,1:T(8,128)(2,1)} %pad_maximum_fusion.11), channel_id=1, source_target_pairs={{0,4},{4,0},{1,5},{5,1},{2,6},{6,2},{3,7},{7,3},{8,12},{12,8},{9,1... | collective-permute-start | bytes 3145736 | tf_op jit(solution)/shard_map/ppermute | solution.py:32
  837.7 34.1 %collective-permute-start.73 = (bf16[4,128,512]{2,1,0:T(8,128)(2,1)}, bf16[4,128,512]{2,1,0:T(8,128)(2,1)}, u32[]{:S(2)}, u32[]{:S(2)}) collective-permute-start(bf16[4,128,512]{2,1,0:T(8,128)(2,1)} %get-tuple-element.78), channel_id=1, source_target_pairs={{0,2},{2,0},{1,3},{3,1},{4,6},{6,4},{5,7},{7,5},{8,10},{10,8},{9,1... | collective-permute-start | bytes 1572872 | tf_op jit(solution)/shard_map/ppermute | solution.py:32
  843.5 27.6 %collective-permute-start.55 = (f32[4,2048]{1,0:T(4,128)S(1)}, f32[4,2048]{1,0:T(4,128)S(1)}, u32[]{:S(2)}, u32[]{:S(2)}) collective-permute-start(f32[4,2048]{1,0:T(4,128)S(1)} %add.450), channel_id=1, source_target_pairs={{0,16},{8,24},{16,0},{24,8},{1,17},{9,25},{17,1},{25,9},{2,18},{10... | collective-permute-start | bytes 98312 | tf_op jit(solution)/shard_map/ppermute | solution.py:138
  866.8 18.3 %collective-permute-start.49 = (bf16[2,128,512]{2,1,0:T(8,128)(2,1)}, bf16[2,128,512]{2,1,0:T(8,128)(2,1)}, u32[]{:S(2)}, u32[]{:S(2)}) collective-permute-start(bf16[2,128,512]{2,1,0:T(8,128)(2,1)} %bitcast.102), channel_id=1, source_target_pairs={{0,8},{8,16},{16,24},{24,0},{1,9},{9,17},{17,25},{25,1},{2,10},{10... | collective-permute-start | bytes 786440 | tf_op jit(solution)/shard_map/ppermute | solution.py:36
  875.2 39.4 %collective-permute-start.57 = (f32[4,2048]{1,0:T(4,128)S(1)}, f32[4,2048]{1,0:T(4,128)S(1)}, u32[]{:S(2)}, u32[]{:S(2)}) collective-permute-start(f32[4,2048]{1,0:T(4,128)S(1)} %add.452), channel_id=1, source_target_pairs={{0,4},{4,0},{1,5},{5,1},{2,6},{6,2},{3,7},{7,3},{8,12},{12,8},{9,1... | collective-permute-start | bytes 98312 | tf_op jit(solution)/shard_map/ppermute | solution.py:32
  880.5 17.8 %collective-permute-start.51 = (bf16[2,128,512]{2,1,0:T(8,128)(2,1)}, bf16[2,128,512]{2,1,0:T(8,128)(2,1)S(1)}, u32[]{:S(2)}, u32[]{:S(2)}) collective-permute-start(bf16[2,128,512]{2,1,0:T(8,128)(2,1)} %bitcast.416), channel_id=1, source_target_pairs={{0,24},{8,0},{16,8},{24,16},{1,25},{9,1},{17,9},{25,17},{2,26},{10... | collective-permute-start | bytes 786440 | tf_op jit(solution)/shard_map/ppermute | solution.py:36
  924.5 18.1 %collective-permute-start.44 = (bf16[128,2048]{1,0:T(8,128)(2,1)}, bf16[128,2048]{1,0:T(8,128)(2,1)}, u32[]{:S(2)}, u32[]{:S(2)}) collective-permute-start(bf16[128,2048]{1,0:T(8,128)(2,1)} %copy.237), channel_id=1, source_target_pairs={{0,1},{1,0},{2,3},{3,2},{4,5},{5,4},{6,7},{7,6},{8,9},{9,8},{10,11... | collective-permute-start | bytes 1572872 | tf_op jit(solution)/shard_map/ppermute | solution.py:32
  (118 other events, 1549.3 us)
Sparse Core Ops, SparseCore 0:
  10.6 65.2 all-gather.4
  142.8 46.9 reduce-scatter.4
  193.3 49.9 all-gather.6
  424.2 47.5 reduce-scatter.6
  476.8 45.8 all-gather.8
  573.6 48.4 reduce-scatter.8
  626.4 45.6 all-gather.10
  796.6 49.6 reduce-scatter.10

commit v2 on v1

v2 whole, which is shorter than its diff:
```python
import math

import jax
import jax.numpy as jnp
from jax import lax
from jax.experimental import pallas as pl
from jax.experimental.pallas import tpu as pltpu
from jax.sharding import Mesh, PartitionSpec as P

D = 2048
HEAD_DIM = 128
EPSILON = 1e-06
ROPE_BASE = 500000.0
GROUP = 4
CORES = 2
F32 = jnp.float32
BF16 = jnp.bfloat16
TEAM = ("g", "c")


def dot(a, b):
    return jnp.dot(a, b, preferred_element_type=F32)


def dot_nt(a, b):
    return lax.dot_general(a, b, (((1,), (1,)), ((), ())), preferred_element_type=F32)


def dot_tn(a, b):
    return lax.dot_general(a, b, (((0,), (0,)), ((), ())), preferred_element_type=F32)


def swap(value, axis):
    return lax.ppermute(value, axis, [(0, 1), (1, 0)])


def shift(value, by):
    return lax.ppermute(value, "g", [(i, (i + by) % GROUP) for i in range(GROUP)])


def pick(value, index, axis):
    return lax.dynamic_index_in_dim(value, index, axis, keepdims=False)


def put(value, piece, index, axis=0):
    return lax.dynamic_update_index_in_dim(value, piece, index, axis)


def ordered(flag, first, second, axis):
    return jnp.where(
        flag == 0, jnp.stack([first, second], axis), jnp.stack([second, first], axis)
    )


def add(*values):
    return sum(v.astype(F32) for v in values).astype(BF16)


class Order:
    def __init__(self):
        self.token = jnp.zeros((), F32)

    def __call__(self, *values):
        *values, self.token = lax.optimization_barrier((*values, self.token))
        return values[0] if len(values) == 1 else values


def assemble(pieces, moves, shapes):
    def kernel(*refs):
        sources, (*targets, sems) = refs[: len(pieces)], refs[len(pieces) :]
        copies = []
        for number, (source, columns, target, row, column) in enumerate(moves):
            rows, width = pieces[source].shape[0], columns[1] - columns[0]
            copies.append(
                pltpu.make_async_copy(
                    sources[source].at[:, pl.ds(columns[0], width)],
                    targets[target].at[pl.ds(row, rows), pl.ds(column, width)],
                    sems.at[number],
                )
            )
        for copy in copies:
            copy.start()
        for copy in copies:
            copy.wait()

    out = pl.pallas_call(
        kernel,
        out_shape=[jax.ShapeDtypeStruct(shape, pieces[0].dtype) for shape in shapes],
        in_specs=[pl.BlockSpec(memory_space=pl.ANY)] * len(pieces),
        out_specs=[pl.BlockSpec(memory_space=pltpu.VMEM)] * len(shapes),
        scratch_shapes=[pltpu.SemaphoreType.DMA((len(moves),))],
        compiler_params=pltpu.CompilerParams(vmem_limit_bytes=24 << 20),
        cost_estimate=pl.CostEstimate(
            flops=0,
            bytes_accessed=sum(4 * math.prod(shape) for shape in shapes),
            transcendentals=0,
        ),
    )(*pieces)
    return out


def reorder(values, flag, orders):
    size = values.shape[1] // len(orders[0])

    def kernel(flag_ref, source, target):
        for number, order in enumerate(orders):

            @pl.when(flag_ref[0] == number)
            def _():
                for to, block in enumerate(order):
                    target[:, to * size : (to + 1) * size] = source[
                        :, block * size : (block + 1) * size
                    ]

    return pl.pallas_call(
        kernel,
        out_shape=jax.ShapeDtypeStruct(values.shape, values.dtype),
        in_specs=[
            pl.BlockSpec(memory_space=pltpu.SMEM),
            pl.BlockSpec(memory_space=pltpu.VMEM),
        ],
        out_specs=pl.BlockSpec(memory_space=pltpu.VMEM),
        cost_estimate=pl.CostEstimate(
            flops=0, bytes_accessed=4 * values.size, transcendentals=0
        ),
    )(jnp.reshape(flag, (1,)).astype(jnp.int32), values)


def vmem_call(kernel, shapes, scalars, arrays):
    flags = jnp.stack([jnp.asarray(v, jnp.int32) for v in scalars])
    spec = pl.BlockSpec(memory_space=pltpu.VMEM)
    return pl.pallas_call(
        kernel,
        out_shape=shapes,
        in_specs=[pl.BlockSpec(memory_space=pltpu.SMEM)] + [spec] * len(arrays),
        out_specs=[spec] * len(shapes),
        compiler_params=pltpu.CompilerParams(vmem_limit_bytes=VMEM_LIMIT),
        cost_estimate=pl.CostEstimate(flops=0, bytes_accessed=LOCAL_BYTES, transcendentals=0),
    )(flags, *arrays)


def pack(shards, g):
    rows, width = shards[0].shape[0], shards[0].shape[1] // (GROUP * CORES)
    count = len(shards)

    def kernel(flags, *refs):
        sources, targets = refs[:count], refs[count:]
        for by in range(GROUP):
            to = lax.rem(flags[0] + by, GROUP)
            for core in range(CORES):
                start = pl.multiple_of((to * CORES + core) * width, width)
                for number in range(count):
                    at = (core * count + number) * width
                    targets[by][:, at : at + width] = sources[number][:, pl.ds(start, width)]

    shape = jax.ShapeDtypeStruct((rows, CORES * count * width), shards[0].dtype)
    return vmem_call(kernel, [shape] * GROUP, [g], shards)


def sort(pieces, g, c):
    rows, half = pieces[0].shape[0], pieces[0].shape[1] // CORES

    def kernel(flags, *refs):
        sources, targets = refs[:GROUP], refs[GROUP:]
        for by in range(GROUP):
            row = pl.multiple_of(lax.rem(flags[0] + GROUP - by, GROUP) * rows, rows)
            for number in range(CORES):
                core = flags[1] if number == 0 else 1 - flags[1]
                targets[number][pl.ds(row, rows), :] = sources[by][
                    :, pl.ds(pl.multiple_of(core * half, half), half)
                ]

    shape = jax.ShapeDtypeStruct((GROUP * rows, half), pieces[0].dtype)
    return vmem_call(kernel, [shape] * CORES, [g, c], pieces)


def unpack(pieces, g, count):
    rows, width = pieces[0].shape[0], pieces[0].shape[1] // (CORES * count)

    def kernel(flags, *refs):
        sources, targets = refs[:GROUP], refs[GROUP:]
        for by in range(GROUP):
            source = lax.rem(flags[0] + GROUP - by, GROUP)
            for core in range(CORES):
                start = pl.multiple_of((source * CORES + core) * width, width)
                for number in range(count):
                    at = (core * count + number) * width
                    targets[number][:, pl.ds(start, width)] = sources[by][
                        :, at : at + width
                    ].astype(F32)

    shape = jax.ShapeDtypeStruct((rows, GROUP * CORES * width), F32)
    return vmem_call(kernel, [shape] * count, [g], pieces)


def by_core(mine, got, c):
    rows = mine.shape[0]

    def kernel(flags, first, second, target):
        target[pl.ds(pl.multiple_of(flags[0] * rows, rows), rows), :] = first[...]
        target[pl.ds(pl.multiple_of((1 - flags[0]) * rows, rows), rows), :] = second[...]

    [out] = vmem_call(
        kernel,
        [jax.ShapeDtypeStruct((CORES * rows, mine.shape[1]), mine.dtype)],
        [c],
        [mine, got],
    )
    return out


def deal(mine, got, g, c):
    rows, width = mine.shape[0] // GROUP, mine.shape[1]

    def kernel(flags, first, second, *targets):
        for by in range(GROUP):
            row = pl.multiple_of(lax.rem(flags[0] + by, GROUP) * rows, rows)
            for number, source in enumerate((first, second)):
                core = flags[1] if number == 0 else 1 - flags[1]
                at = pl.ds(pl.multiple_of(core * width, width), width)
                targets[by][:, at] = source[pl.ds(row, rows), :]

    shape = jax.ShapeDtypeStruct((rows, CORES * width), mine.dtype)
    return vmem_call(kernel, [shape] * GROUP, [g, c], [mine, got])


def weight_grads(factors, reps, cuts):
    step = 256
    count = factors[0][0].shape[0]
    total = sum(cuts)
    starts = [sum(cuts[:number]) for number in range(len(cuts))]

    def products(lefts, rights, own, other):
        for left, right, start, width in zip(lefts, rights, starts, cuts):
            product = mm(left[...], right[...], TN).astype(BF16)
            own[:, start : start + width] = product[:, :width]
            other[:, start : start + width] = product[:, width:]

    lefts = [left for left, _ in factors]
    rights = [right for _, right in factors]
    size = len(factors)
    whole = [pl.BlockSpec(v.shape, lambda i: (0, 0)) for v in rights]
    params = {
        "compiler_params": pltpu.CompilerParams(vmem_limit_bytes=VMEM_LIMIT),
        "cost_estimate": pl.CostEstimate(flops=0, bytes_accessed=LOCAL_BYTES, transcendentals=0),
    }
    if reps != 2:

        def kernel(*refs):
            products(refs[:size], refs[size : 2 * size], *refs[2 * size :])

        out = pl.BlockSpec((step, total), lambda i: (i, 0))
        return pl.pallas_call(
            kernel,
            grid=(D // step,),
            in_specs=[pl.BlockSpec((count, step), lambda i: (0, i))] * size + whole,
            out_specs=[out, out],
            out_shape=[jax.ShapeDtypeStruct((D, total), BF16)] * 2,
            **params,
        )(*lefts, *rights)

    steps = D // 2 // step
    half = steps // 2

    def kernel(*refs):
        upper, lower, right = refs[:size], refs[size : 2 * size], refs[2 * size : 3 * size]
        to_q, to_x, beside_top, below_low, keep = refs[3 * size :]

        @pl.when(pl.program_id(0) < half)
        def _():
            products(upper, right, keep, beside_top)
            products(lower, right, to_q.at[1], to_q.at[0])

        @pl.when(pl.program_id(0) >= half)
        def _():
            products(upper, right, keep, to_x.at[1])
            products(lower, right, below_low, to_x.at[0])

    first = lambda i: jnp.minimum(i, half - 1)
    last = lambda i: jnp.maximum(i - half, 0)
    rows = D // 4
    return pl.pallas_call(
        kernel,
        grid=(steps,),
        in_specs=[pl.BlockSpec((count, step), lambda i: (0, i))] * size
        + [pl.BlockSpec((count, step), lambda i: (0, i + steps))] * size
        + whole,
        out_specs=[
            pl.BlockSpec((2, step, total), lambda i: (0, first(i), 0)),
            pl.BlockSpec((2, step, total), lambda i: (0, last(i), 0)),
            pl.BlockSpec((step, total), lambda i: (first(i), 0)),
            pl.BlockSpec((step, total), lambda i: (last(i), 0)),
            pl.BlockSpec((step, total), lambda i: (i, 0)),
        ],
        out_shape=[
            jax.ShapeDtypeStruct(shape, BF16)
            for shape in (
                (2, rows, total), (2, rows, total), (rows, total), (rows, total), (2 * rows, total)
            )
        ],
        **params,
    )(*lefts, *lefts, *rights)


NN, NT, TN = ((1,), (0,)), ((1,), (1,)), ((0,), (0,))
VMEM_LIMIT = 60 << 20
LOCAL_BYTES = 200 << 20
HEADS_HERE = 2
ROOT = HEAD_DIM ** (-0.5)


def mm(a, b, dims=NN):
    return lax.dot_general(a, b, (dims, ((), ())), preferred_element_type=F32)


def eye(size):
    return lax.broadcasted_iota(jnp.int32, (size, size), 0) == lax.broadcasted_iota(
        jnp.int32, (size, size), 1
    )


def to_column(row):
    return jnp.sum(jnp.where(eye(row.shape[1]), row, 0.0), axis=1, keepdims=True)


def to_row(column):
    return jnp.sum(jnp.where(eye(column.shape[0]), column, 0.0), axis=0, keepdims=True)


def head(values, kind, number):
    start = (number * 3 + kind) * HEAD_DIM
    return values[:, start : start + HEAD_DIM]


def pair(values, number):
    return values[:, number * HEAD_DIM : (number + 1) * HEAD_DIM]


def rotated(values, cosine, sine):
    return values * cosine + pltpu.roll(values, HEAD_DIM // 2, 1) * sine


def allowed_keys(segment_row):
    size = segment_row.shape[1]
    same = to_column(segment_row) == segment_row
    later = lax.broadcasted_iota(jnp.int32, (size, size), 1) > lax.broadcasted_iota(
        jnp.int32, (size, size), 0
    )
    return jnp.logical_and(same, jnp.logical_not(later))


def softmax_of(query, key, allowed):
    scores = jnp.where(allowed, mm(query, key, NT) * ROOT, -1e30)
    expo = jnp.exp(scores - jnp.max(scores, axis=1, keepdims=True))
    return expo / jnp.sum(expo, axis=1, keepdims=True)


def scale_of(squares, kind):
    return to_column(lax.rsqrt(squares[kind : kind + 1] / D + EPSILON))


def row_call(kernel, rows, ins, outs):
    def spec(shape, block):
        if block == "whole":
            return pl.BlockSpec(shape, lambda i: (0,) * len(shape))
        return pl.BlockSpec((block,) + shape[1:], lambda i: (i,) + (0,) * (len(shape) - 1))

    return pl.pallas_call(
        kernel,
        grid=(rows,),
        in_specs=[spec(v.shape, block) for v, block in ins],
        out_specs=[spec(shape, block) for shape, _, block in outs],
        out_shape=[jax.ShapeDtypeStruct(shape, dtype) for shape, dtype, _ in outs],
        compiler_params=pltpu.CompilerParams(vmem_limit_bytes=VMEM_LIMIT),
        cost_estimate=pl.CostEstimate(flops=0, bytes_accessed=0, transcendentals=0),
    )(*[v for v, _ in ins])


def project_kernel(tokens, weights, out, squares):
    product = mm(tokens[...], weights[...])
    out[...] = product
    for kind in range(2):
        total = 0.0
        for number in range(HEADS_HERE):
            part = head(product, kind, number)
            total = total + jnp.sum(part * part, axis=1, keepdims=True)
        squares[0, kind : kind + 1] = to_row(total)


def attend_kernel(
    qkv, squares, gains, cosine, sine, segments, weights, query_out, key_out, value_out, mixed, out
):
    allowed = allowed_keys(segments[0])
    scales = [scale_of(squares[0], kind) for kind in range(2)]
    for number in range(HEADS_HERE):
        low = [
            rotated(
                head(qkv, kind, number) * scales[kind] * gains[kind, number : number + 1],
                cosine[...],
                sine[...],
            ).astype(BF16)
            for kind in range(2)
        ]
        value = head(qkv, 2, number).astype(BF16)
        probs = softmax_of(*low, allowed).astype(BF16)
        where = slice(number * HEAD_DIM, (number + 1) * HEAD_DIM)
        query_out[:, where] = low[0]
        key_out[:, where] = low[1]
        value_out[:, where] = value
        mixed[:, where] = mm(probs, value).astype(BF16)
    out[...] = mm(mixed[...], weights[...], NT).astype(BF16)


def attend_back_kernel(
    grads, weights, queries, keys, values, qkv, squares, gains, cosine, sine, segments,
    weighted, value_grad, inner, gain_grad,
):
    @pl.when(pl.program_id(0) == 0)
    def _():
        gain_grad[...] = jnp.zeros_like(gain_grad)

    allowed = allowed_keys(segments[0])
    scales = [scale_of(squares[0], kind) for kind in range(2)]
    mixed_grads = mm(grads[...], weights[...]).astype(BF16)
    sums = [0.0, 0.0]
    for number in range(HEADS_HERE):
        query, key, value = pair(queries, number), pair(keys, number), pair(values, number)
        mixed_grad = pair(mixed_grads, number)
        probs = softmax_of(query, key, allowed)
        where = slice(number * HEAD_DIM, (number + 1) * HEAD_DIM)
        value_grad[:, where] = mm(probs.astype(BF16), mixed_grad, TN).astype(BF16)
        prob_grad = mm(mixed_grad, value, NT)
        score_grad = probs * (prob_grad - jnp.sum(probs * prob_grad, axis=1, keepdims=True))
        score_low = (score_grad * ROOT).astype(BF16)
        turned = (mm(score_low, key), mm(score_low, query, TN))
        for kind in range(2):
            normed = rotated(turned[kind], cosine[...], -sine[...])
            part = head(qkv, kind, number)
            gain_grad[kind, number : number + 1] += jnp.sum(
                normed * part * scales[kind], axis=0, keepdims=True
            )
            normed = normed * gains[kind, number : number + 1]
            sums[kind] = sums[kind] + jnp.sum(part * normed, axis=1, keepdims=True)
            start = (kind * HEADS_HERE + number) * HEAD_DIM
            weighted[:, start : start + HEAD_DIM] = normed
    for kind in range(2):
        inner[0, kind : kind + 1] = to_row(sums[kind])


def input_grad_kernel(weighted, qkv, squares, inner, value_grad, weights, qkv_grad, out):
    for kind in range(2):
        scale = scale_of(squares[0], kind)
        shift_by = scale * scale * scale * (to_column(inner[0][kind : kind + 1]) / D)
        for number in range(HEADS_HERE):
            start = (kind * HEADS_HERE + number) * HEAD_DIM
            part = weighted[:, start : start + HEAD_DIM]
            start = (number * 3 + kind) * HEAD_DIM
            qkv_grad[:, start : start + HEAD_DIM] = (
                scale * part - head(qkv, kind, number) * shift_by
            ).astype(BF16)
    for number in range(HEADS_HERE):
        start = (number * 3 + 2) * HEAD_DIM
        qkv_grad[:, start : start + HEAD_DIM] = pair(value_grad, number)
    out[...] = mm(qkv_grad[...], weights[...], NT).astype(BF16)


class Place:
    def __init__(self, reps):
        self.reps = reps
        self.g = lax.axis_index("g")
        self.q = lax.axis_index("q")
        self.c = lax.axis_index("c")
        self.x = lax.axis_index("x")

    def orders(self):
        return [
            [
                (g * self.reps + (q ^ flip)) * CORES + c
                for q in range(self.reps)
                for c in range(CORES)
                for g in range(GROUP)
            ]
            for flip in ((0, 1) if self.reps == 2 else (0,))
        ]

    def shuffle(self, value, orders):
        if self.reps == 2:
            return reorder(value, self.q, orders)
        rows, size = value.shape[0], D // len(orders[0])
        blocks = value.reshape(rows, -1, size)
        return jnp.stack([blocks[:, i] for i in orders[0]], 1).reshape(rows, D)

    def to_local(self, value):
        return self.shuffle(value, self.orders())

    def to_global(self, value):
        return self.shuffle(
            value, [[order.index(i) for i in range(len(order))] for order in self.orders()]
        )

    def send(self, pieces):
        return [pieces[0]] + [shift(pieces[by], by) for by in range(1, GROUP)]

    def spread(self, shards):
        return self.send(pack(shards, self.g))

    def settle(self, pieces):
        mine, other = sort(pieces, self.g, self.c)
        return [mine, swap(other, "c")]

    def settled(self, halves):
        return by_core(*halves, self.c)

    def widen(self, held):
        if self.reps != 2:
            return [lax.all_gather(held, "q", axis=0, tiled=True)]
        return [held, swap(held, "q"), swap(held, "x")]

    def widened(self, blocks):
        if self.reps != 2:
            return [*blocks, swap(blocks[0], "x")]
        half = blocks[0].shape[0] // 2
        return [*blocks, swap(blocks[2][:half], "q"), swap(blocks[1][half:], "x")]

    def join(self, blocks, cuts):
        rows = blocks[0].shape[0]
        spots = [(0, 0), (0, 1)]
        if self.reps == 2:
            spots = [(0, 0), (rows, 0), (0, 1), (rows, 1), (rows + rows // 2, 1)]
        moves, shapes = [], [(D, 2 * (stop - start)) for start, stop in cuts]
        for number, (start, stop) in enumerate(cuts):
            for at, (row, side) in enumerate(spots):
                moves.append((at, (start, stop), number, row, side * (stop - start)))
        return assemble(blocks, moves, shapes)

    def narrow(self, parts):
        if self.reps != 2:
            return [swap(parts[1], "x")]
        return [swap(parts[0], "q"), swap(parts[1], "x")]

    def narrow_next(self, parts, came):
        if self.reps != 2:
            total = add(parts[0], came[0])
            return [lax.psum_scatter(total, "q", scatter_dimension=0, tiled=True)]
        _, _, beside_top, below_low, _ = parts
        return [swap(add(beside_top, came[0][0]), "x"), swap(add(below_low, came[1][0]), "q")]

    def narrowed(self, parts, came, more):
        if self.reps != 2:
            return jnp.split(more[0], 2)
        half = parts[4].shape[0] // 2
        return (
            add(parts[4][:half], more[0], came[0][1]),
            add(parts[4][half:], came[1][1], more[1]),
        )

    def unsettle(self, halves):
        top, low = halves
        mine, other = jnp.where(self.c == 0, top, low), jnp.where(self.c == 0, low, top)
        return [mine, swap(other, "c")]

    def collect(self, halves):
        return self.send(deal(*halves, self.g, self.c))


def rope_tables(segments):
    places = jnp.arange(segments.shape[1], dtype=jnp.int32)
    same = segments[:, :, None] == segments[:, None, :]
    earlier = same & (places[None, None, :] < places[None, :, None])
    spot = jnp.sum(earlier.astype(jnp.int32), axis=2).astype(F32)
    halfway = HEAD_DIM // 2
    inverse = jnp.exp(jnp.arange(halfway, dtype=F32) * (-2.0 * math.log(ROPE_BASE) / HEAD_DIM))
    angles = spot.reshape(-1, 1) * inverse
    cosine, sine = jnp.cos(angles), jnp.sin(angles)
    return jnp.concatenate([cosine, cosine], 1), jnp.concatenate([-sine, sine], 1)


def norm_scale(values):
    return lax.rsqrt(jnp.mean(values * values, axis=-1, keepdims=True) + EPSILON)


def norm_back(values, scale, gain, grad):
    weighted = grad * gain
    inner = jnp.sum(values * weighted, axis=-1, keepdims=True) / D
    return (
        scale * weighted - values * (scale * scale * scale) * inner,
        jnp.sum(grad * values * scale, axis=0),
    )


def on_device(
    reps,
    tokens,
    segment_ids,
    query_proj,
    key_proj,
    value_proj,
    out_proj,
    query_gain,
    key_gain,
    attn_gain,
    gate_proj,
    up_proj,
    down_proj,
    mlp_gain,
    cotangent,
):
    place = Place(reps)
    slots = GROUP * CORES
    shard_rows = query_proj.shape[0]
    length = tokens.shape[2]
    slot = place.g * CORES + place.c

    step = Order()
    count = slots * length
    cut = 3 * HEAD_DIM

    def team_scatter(value):
        return lax.psum_scatter(value, TEAM, scatter_dimension=0, tiled=True)

    def team_gather(value):
        return lax.all_gather(value, TEAM, axis=0, tiled=True)

    def team_sum(value):
        value = value + step(swap(value, "c"))
        for by in (1, 2):
            value = value + step(
                lax.ppermute(value, "g", [(i, i ^ by) for i in range(GROUP)])
            )
        return value

    attn = place.spread([query_proj, key_proj, value_proj, out_proj])
    own_row = place.to_local(pick(tokens, place.x, 0)[0])
    segments = pick(segment_ids, place.x, 0)
    segments = ordered(place.c, segments, swap(segments, "c"), 0)[:, 0]
    gate = pack([gate_proj, up_proj], place.g)
    feed = pack([down_proj], place.g)
    attn, own_row, segments, gate, feed = step(attn, own_row, segments, gate, feed)
    all_rows = team_gather(own_row)
    segments = [segments] + [shift(segments, by) for by in range(1, GROUP)]
    attn = step(place.settle(attn))
    attn = place.widen(place.settled(attn))
    gains = jnp.stack([pick(w.reshape(slots, HEAD_DIM), slot, 0) for w in (query_gain, key_gain)])
    gains = jnp.stack([gains, swap(gains, "x")], 1)
    gathered = jnp.zeros((GROUP,) + segments[0].shape, segments[0].dtype)
    for by, piece in enumerate(segments):
        gathered = put(gathered, piece, (place.g - by) % GROUP)
    segments = gathered.reshape(slots, length)
    cosine, sine = rope_tables(segments)
    segments = segments.astype(F32)[:, None]
    attn, gains, segments, gate = step(attn, gains, segments, gate)
    gate = place.send(gate)
    attn = step(place.widened(attn))
    qkv_full, out_full = step(place.join(attn, [(0, cut), (cut, 4 * HEAD_DIM)]))
    all_rows, cosine, sine = step(all_rows, cosine, sine)

    qkv, squares = step(
        *row_call(
            project_kernel,
            slots,
            [(all_rows, length), (qkv_full, "whole")],
            [((count, 6 * HEAD_DIM), F32, length), ((slots, 2, length), F32, 1)],
        )
    )
    gate = step(place.settle(step(gate)))
    gate = place.widen(place.settled(gate))
    squares = team_sum(squares)
    squares, feed = step(squares, feed)
    feed = place.send(feed)
    low = ((count, 2 * HEAD_DIM), BF16, length)
    query_low, key_low, value_low, mixed, attn_part = step(
        *row_call(
            attend_kernel,
            slots,
            [
                (qkv, length),
                (squares, 1),
                (gains, "whole"),
                (cosine, length),
                (sine, length),
                (segments, 1),
                (out_full, "whole"),
            ],
            [low, low, low, low, ((count, D), BF16, length)],
        )
    )
    attn_part, gate, feed = step(attn_part, gate, feed)
    projected = team_scatter(attn_part)
    gate = place.widened(gate)
    feed = place.settle(feed)
    feed = place.widen(place.settled(step(feed)))
    gate = step(gate)
    width = gate_proj.shape[1] // slots
    projected = step(projected)
    projected = projected.astype(F32)
    attn_gain, mlp_gain = place.to_local(jnp.stack([attn_gain, mlp_gain]))
    projected_scale = norm_scale(projected)
    hidden = own_row.astype(F32) + projected * projected_scale * attn_gain
    hidden_low, hidden = step(hidden.astype(BF16), hidden)
    hidden_all = team_gather(hidden_low)
    gate_full, up_full = step(place.join(gate, [(0, width), (width, 2 * width)]))
    feed = place.widened(step(feed))
    [down_full] = place.join(step(feed), [(0, width)])
    own_cotangent = place.to_local(pick(cotangent, place.x, 0)[0]).astype(F32)
    hidden_all, gate_full, up_full, down_full, own_cotangent = step(
        hidden_all, gate_full, up_full, down_full, own_cotangent
    )

    lifted = dot(hidden_all, up_full)
    gated = dot(hidden_all, gate_full)
    active = (gated / (1.0 + jnp.exp(-gated)) * lifted).astype(BF16)
    reduced = team_scatter(step(dot_nt(active, down_full).astype(BF16)))
    reduced = step(reduced).astype(F32)
    reduced_scale = norm_scale(reduced)
    reduced_grad, mlp_gain_grad = norm_back(reduced, reduced_scale, mlp_gain, own_cotangent)
    reduced_all = team_gather(step(reduced_grad.astype(BF16)))
    own_out = place.to_global((hidden + reduced * reduced_scale * mlp_gain).astype(BF16))
    layer_out = ordered(place.x, own_out, swap(own_out, "x"), 0)[:, None]
    reduced_all, mlp_gain_grad, layer_out = step(reduced_all, mlp_gain_grad, layer_out)

    active_grad = dot(reduced_all, down_full)
    gate_sigmoid = 1.0 / (1.0 + jnp.exp(-gated))
    gated_grad = (
        active_grad * lifted * gate_sigmoid * (1.0 + gated * (1.0 - gate_sigmoid))
    ).astype(BF16)
    lifted_grad = (active_grad * gated * gate_sigmoid).astype(BF16)
    hidden_part = dot_nt(gated_grad, gate_full) + dot_nt(lifted_grad, up_full)
    hidden_part, gated_grad, lifted_grad = step(hidden_part.astype(BF16), gated_grad, lifted_grad)
    hidden_part = team_scatter(hidden_part)
    down = step(weight_grads([(reduced_all, active)], reps, [width]))
    down_came = place.narrow(down)
    feed = step(
        weight_grads([(hidden_all, gated_grad), (hidden_all, lifted_grad)], reps, [width, width])
    )
    down_came = step(down_came)
    down_more = place.narrow_next(down, down_came)
    hidden_grad = own_cotangent + step(hidden_part).astype(F32)
    projected_grad, attn_gain_grad = norm_back(projected, projected_scale, attn_gain, hidden_grad)
    projected_low, hidden_grad, attn_gain_grad = step(
        projected_grad.astype(BF16), hidden_grad, attn_gain_grad
    )
    projected_all = team_gather(projected_low)
    down_more, feed = step(down_more, feed)
    feed_came = place.narrow(feed)
    down = step(place.unsettle(place.narrowed(down, down_came, down_more)))
    norm_gain_grads = place.to_global(jnp.stack([attn_gain_grad, mlp_gain_grad]))
    down = deal(*down, place.g, place.c)
    norm_gain_grads, down = step(norm_gain_grads, down)

    projected_all, down = step(projected_all, down)
    down = place.send(down)
    weighted, value_grad, inner, head_gain_grads = step(
        *row_call(
            attend_back_kernel,
            slots,
            [
                (projected_all, length),
                (out_full, "whole"),
                (query_low, length),
                (key_low, length),
                (value_low, length),
                (qkv, length),
                (squares, 1),
                (gains, "whole"),
                (cosine, length),
                (sine, length),
                (segments, 1),
            ],
            [
                ((count, 4 * HEAD_DIM), F32, length),
                low,
                ((slots, 2, length), F32, 1),
                (gains.shape, F32, "whole"),
            ],
        )
    )
    spots = jnp.zeros((2, 2, slots, HEAD_DIM), F32)
    for number in range(2):
        spots = lax.dynamic_update_slice(
            spots,
            head_gain_grads[:, number][:, None, None],
            (0, place.x if number == 0 else 1 - place.x, slot, 0),
        )
    message = jnp.concatenate([v.reshape(-1, HEAD_DIM) for v in (inner, spots, norm_gain_grads)])
    message, feed_came = step(message, feed_came)
    feed_more = place.narrow_next(feed, feed_came)
    down = step(down)
    message = team_sum(message)
    inner, gain_grads = message[: 2 * slots].reshape(inner.shape), message[2 * slots :]
    qkv_grad, input_part = step(
        *row_call(
            input_grad_kernel,
            slots,
            [
                (weighted, length),
                (qkv, length),
                (squares, 1),
                (inner, 1),
                (value_grad, length),
                (qkv_full, "whole"),
            ],
            [((count, 6 * HEAD_DIM), BF16, length), ((count, D), BF16, length)],
        )
    )
    input_part = team_scatter(input_part)
    feed = place.unsettle(place.narrowed(feed, feed_came, step(feed_more)))
    feed = place.collect(step(feed))
    attn = step(
        weight_grads([(all_rows, qkv_grad), (projected_all, mixed)], reps, [cut, HEAD_DIM])
    )
    attn_came = place.narrow(attn)
    [down_grad] = step(unpack(down, place.g, 1))
    attn_came = step(attn_came)
    attn_more = place.narrow_next(attn, attn_came)
    gain_x = swap(gain_grads, "x")
    feed = step(feed)
    attn_more = step(attn_more)
    attn = place.unsettle(place.narrowed(attn, attn_came, attn_more))
    attn, gain_x = step(attn, gain_x)
    attn = place.collect(attn)
    gain_grads = gain_grads + gain_x
    gain_q = swap(gain_grads, "q") if reps == 2 else lax.psum(gain_grads, "q") - gain_grads
    gate_grad, up_grad = step(unpack(feed, place.g, 2))
    input_part, gain_q = step(input_part, gain_q)
    own_grad = place.to_global((hidden_grad + input_part.astype(F32)).astype(BF16))
    own_grad_x = swap(own_grad, "x")
    summed = (gain_grads + gain_q).reshape(4, D)
    attn_grads = unpack(step(attn), place.g, 4)
    tokens_grad = ordered(place.x, own_grad, step(own_grad_x), 0)[:, None].astype(F32)
    summed = summed + step.token
    half_of = lambda v: pick(v.reshape(2, -1), place.x, 0)
    return (
        layer_out,
        tokens_grad,
        *attn_grads,
        half_of(summed[0]),
        half_of(summed[1]),
        summed[2],
        gate_grad,
        up_grad,
        down_grad,
        summed[3],
    )


def solution(mesh):
    reps = mesh.shape["dp"] // (GROUP * CORES)
    folded = Mesh(
        mesh.devices.reshape(GROUP, reps, CORES, mesh.shape["tensor"]), ("g", "q", "c", "x")
    )
    dp = ("g", "q", "c")
    row = P(None, dp, None, None)
    weight = P(dp, "x")
    gain = P("x")
    in_specs = (row, P(None, dp, None)) + (weight,) * 4 + (gain, gain, P()) + (weight,) * 3
    in_specs += (P(), row)
    out_specs = (row, row) + (weight,) * 4 + (gain, gain, P()) + (weight,) * 3 + (P(),)

    def body(*args):
        return on_device(reps, *args)

    return jax.shard_map(
        body, mesh=folded, in_specs=in_specs, out_specs=out_specs, check_vma=False
    )
```

time: 965 us -> 759 us (0.79)
  Pallas kernels: 0 us -> 142 us
  matrix products: 154 us -> 42.6 us
  local copies, waits for them, and re-layouts: 127 us -> 33.6 us
  starting transfers between devices: 126 us -> 61 us
  waiting for transfers between devices: 461 us -> 407 us
  other arithmetic: 74 us -> 47 us
    pallas_call x0 -> x31, Pallas kernels: none -> 142 us  [the longest x4 53.4 us: row_call(): pl.pallas_call(kernel, grid=(rows,), in_specs=[spec(v.shape, block) for v...]
    reduce_scatter x4, waiting for transfers between devices: 138 us -> 78.1 us  [team_scatter(): return lax.psum_scatter(value, TEAM, scatter_dimension=0, tiled=True)]
    dot_general x5 -> x3, matrix products: 64.8 us -> 16.9 us  [dot_nt(): lax.dot_general(a, b, (((1,), (1,)), ((), ())), preferred_element_type=F32)]
    dot_general x10 -> x0, matrix products: 34.7 us -> none  [the longest x5 22.8 us: dot_tn(): lax.dot_general(a, b, (((0,), (0,)), ((), ())), preferred_element_type=F32)]
    ppermute x27 -> x21, starting transfers between devices: 53.3 us -> 23.8 us  [shift(): lax.ppermute(value, 'g', [(i, (i + by) % GROUP) for i in range(GROUP)])]
    dynamic_slice x26 -> x3, local copies, waits for them, and re-layouts: 31.1 us -> 1.99 us  [pick(): return lax.dynamic_index_in_dim(value, index, axis, keepdims=False)]
    dot_general x5 -> x3, matrix products: 51.5 us -> 25.7 us  [dot(): return jnp.dot(a, b, preferred_element_type=F32)]
    unnamed x209 -> x124, local copies, waits for them, and re-layouts: 37.3 us -> 19 us
  transfers between devices with their start and end apart: 90 -> 71, of which waited for: 35 -> 44; matrix products, arithmetic and copies ran while one was open for 25% -> 6% of each run, Pallas kernels for 0% -> 16%
where the time goes in v2:
time: 759 us; the launch traced here: 748 us
  waiting for transfers between devices  407 us (54%)
  Pallas kernels  142 us (19%)
  starting transfers between devices  61 us (8%)
  other arithmetic  47 us (6%)
  matrix products  42.6 us (6%)
  local copies, waits for them, and re-layouts  33.6 us (4%)
  between operations  15.1 us (2%)
    ppermute x38, waiting for transfers between devices, swap(): return lax.ppermute(value, axis, [(0, 1), (1, 0)])  153 us
    ppermute x21, waiting for transfers between devices, shift(): lax.ppermute(value, 'g', [(i, (i + by) % GROUP) for i in range(GROUP)])  117 us
    reduce_scatter x4, waiting for transfers between devices, team_scatter(): return lax.psum_scatter(value, TEAM, scatter_dimension=0, tiled=True)  78.1 us
    pallas_call x4, Pallas kernels, row_call(): pl.pallas_call(kernel, grid=(rows,), in_specs=[spec(v.shape, block) for v...  53.4 us
    all_gather x4, waiting for transfers between devices, team_gather(): return lax.all_gather(value, TEAM, axis=0, tiled=True)  44.8 us
    pallas_call x15, Pallas kernels, vmem_call(): pl.pallas_call(kernel, out_shape=shapes, in_specs=[pl.BlockSpec(memory_sp...  39.5 us
    ppermute x38, starting transfers between devices, swap(): return lax.ppermute(value, axis, [(0, 1), (1, 0)])  33.6 us
    pallas_call x3, Pallas kernels, weight_grads(): pl.pallas_call(kernel, grid=(steps,), in_specs=[pl.BlockSpec((count, step...  33.1 us
  transfers between devices with their start and end apart: 71, of which 44 were waited for; matrix products, arithmetic and copies ran while one was open for 6% of the time, Pallas kernels for 16%

profile of v2, /device:TPU:24, one launch (start us, length us, event | category | flops | bytes accessed | tf_op | source)
XLA Modules:
  0.0 748.5 jit_solution(13595439118016867501)
XLA Ops:
  8.0 2.4 shard_map.237
  17.9 3.0 shard_map.239
  20.9 15.2 %collective-permute-done.1.refs_2_ = bf16[128,1024]{1,0:T(8,128)(2,1)S(1)} collective-permute-done((bf16[128,1024]{1,0:T(8,128)(2,1)}, bf16[128,1024]{1,0:T(8,128)(2,1)S(1)}, u32[]{:S(2)}, u32[]{:S(2)}) %collective-permute-start.1) | collective-permute-done | bytes 262176 | tf_op jit(solution)/shard_map/ppermute | solution.py:38
  55.6 15.1 %collective-permute-done.8.refs_1_ = bf16[1024,512]{1,0:T(8,128)(2,1)S(1)} collective-permute-done((bf16[1024,512]{1,0:T(8,128)(2,1)}, bf16[1024,512]{1,0:T(8,128)(2,1)S(1)}, u32[]{:S(2)}, u32[]{:S(2)}) %collective-permute-start.8) | collective-permute-done | bytes 1048608 | tf_op jit(solution)/shard_map/ppermute | solution.py:34
  80.4 4.7 collective-permute-done.11.refs_3_
  88.8 9.6 %shard_map.244 = (f32[1024,768]{1,0:T(8,128)}, f32[8,2,128]{2,1,0:T(2,128)}) custom-call(bf16[1024,2048]{1,0:T(8,128)(2,1)} %all-gather.5.cloned.1.call-done.tokens.refs_0_.refs_2_, bf16[2048,768]{1,0:T(8,128)(2,1)} %copy-done.2), custom_call_target="tpu_custom_call" | custom-call | tf_op jit(solution)/shard_map/pallas_call | solution.py:368
  98.4 27.2 %collective-permute-done.15.refs_2_ = bf16[128,2048]{1,0:T(8,128)(2,1)S(1)} collective-permute-done((bf16[128,2048]{1,0:T(8,128)(2,1)}, bf16[128,2048]{1,0:T(8,128)(2,1)S(1)}, u32[]{:S(2)}, u32[]{:S(2)}) %collective-permute-start.15) | collective-permute-done | bytes 524320 | tf_op jit(solution)/shard_map/ppermute | solution.py:38
  127.1 3.0 shard_map.245
  130.1 2.9 collective-permute-done.17.second
  134.0 3.0 shard_map.247.refs_0_
  141.1 3.6 collective-permute-done.18
  145.8 3.5 collective-permute-done.19
  152.9 13.8 %shard_map.246 = (bf16[1024,256]{1,0:T(8,128)(2,1)}, bf16[1024,256]{1,0:T(8,128)(2,1)}, bf16[1024,256]{1,0:T(8,128)(2,1)}, bf16[1024,256]{1,0:T(8,128)(2,1)}, bf16[1024,2048]{1,0:T(8,128)(2,1)}) custom-call(f32[1024,768]{1,0:T(8,128)} %get-tuple-element.362.qkv, f32[8,2,128]{2,1,0:T(2,128)} %add.204.squares, f32[2,2,128]{2,1,0:T(2,128)} %pad_maximum_fusion.5.gains, ...), custom_call_target="tpu_custom_call" | custom-call | tf_op jit(solution)/shard_map/pallas_call | solution.py:368
  166.8 6.4 collective-permute-done.23.refs_2_
  173.2 11.7 %collective-permute-done.20.refs_1_ = bf16[1024,1024]{1,0:T(8,128)(2,1)S(1)} collective-permute-done((bf16[1024,1024]{1,0:T(8,128)(2,1)}, bf16[1024,1024]{1,0:T(8,128)(2,1)S(1)}, u32[]{:S(2)}, u32[]{:S(2)}) %collective-permute-start.20) | collective-permute-done | bytes 2097184 | tf_op jit(solution)/shard_map/ppermute | solution.py:34
  198.7 14.4 %collective-permute-done.25.refs_3_ = bf16[512,1024]{1,0:T(8,128)(2,1)S(1)} collective-permute-done((bf16[512,1024]{1,0:T(8,128)(2,1)}, bf16[512,1024]{1,0:T(8,128)(2,1)S(1)}, u32[]{:S(2)}, u32[]{:S(2)}) %collective-permute-start.25) | collective-permute-done | bytes 1048608 | tf_op jit(solution)/shard_map/ppermute | solution.py:34
  213.1 3.6 collective-permute-done.26.refs_4_
  216.7 17.1 %reduce-scatter.5.cloned.1.call-done = bf16[128,2048]{1,0:T(8,128)(2,1)} async-done(((bf16[1024,2048]{1,0:T(8,128)(2,1)}), bf16[128,2048]{1,0:T(8,128)(2,1)}) %reduce-scatter.5.cloned.1.call-update) | async-done | bytes 524304 | tf_op jit(solution)/shard_map/reduce_scatter | solution.py:619
  235.0 2.6 fusion.38
  243.7 2.4 shard_map.250
  250.2 14.8 %collective-permute-done.28.refs_1_ = bf16[1024,512]{1,0:T(8,128)(2,1)S(1)} collective-permute-done((bf16[1024,512]{1,0:T(8,128)(2,1)}, bf16[1024,512]{1,0:T(8,128)(2,1)S(1)}, u32[]{:S(2)}, u32[]{:S(2)}) %collective-permute-start.28) | collective-permute-done | bytes 1048608 | tf_op jit(solution)/shard_map/ppermute | solution.py:34
  275.2 5.7 collective-permute-done.30.refs_3_
  285.9 7.6 %fusion.41 = f32[1024,1024]{1,0:T(8,128)S(1)} fusion(bf16[1024,2048]{1,0:T(8,128)(2,1)} %all-gather.7.cloned.1.call-done.refs_0_.refs_1_.refs_2_.refs_3_, bf16[2048,1024]{1,0:T(8,128)(2,1)} %copy-done.18), kind=kOutput, calls=%fused_computation.116 | convolution fusion | flops 4294967296 | bytes 12582912 | tf_op jit(solution)/shard_map/dot_general | solution.py:22
  293.6 6.5 multiply_convert_fusion.2
  301.4 6.2 convolution_convert_fusion
  307.7 48.3 %reduce-scatter.7.cloned.1.call-done = bf16[128,2048]{1,0:T(8,128)(2,1)} async-done(((bf16[1024,2048]{1,0:T(8,128)(2,1)}), bf16[128,2048]{1,0:T(8,128)(2,1)}) %reduce-scatter.7.cloned.1.call-update) | async-done | bytes 524304 | tf_op jit(solution)/shard_map/reduce_scatter | solution.py:619
  358.6 2.4 fusion.24
  361.1 2.4 shard_map.254
  364.2 13.2 %collective-permute-done.32 = bf16[128,2048]{1,0:T(8,128)(2,1)S(1)} collective-permute-done((bf16[128,2048]{1,0:T(8,128)(2,1)}, bf16[128,2048]{1,0:T(8,128)(2,1)S(1)}, u32[]{:S(2)}, u32[]{:S(2)}) %collective-permute-start.32) | collective-permute-done | bytes 524320 | tf_op jit(solution)/shard_map/ppermute | solution.py:34
  377.4 2.4 maximum_select_fusion
  379.8 27.2 %all-gather.9.cloned.1.call-done.refs_0_.refs_1_ = bf16[1024,2048]{1,0:T(8,128)(2,1)} async-done(((bf16[128,2048]{1,0:T(8,128)(2,1)}), bf16[1024,2048]{1,0:T(8,128)(2,1)}) %all-gather.9.cloned.1.call-update) | async-done | bytes 4194320 | tf_op jit(solution)/shard_map/all_gather | solution.py:622
  407.0 11.5 %multiply_convert_fusion = (bf16[1024,1024]{1,0:T(8,128)(2,1)S(1)}, bf16[1024,1024]{1,0:T(8,128)(2,1)S(1)}) fusion(f32[1024,1024]{1,0:T(8,128)} %copy-done.61, f32[1024,1024]{1,0:T(8,128)} %get-tuple-element.652, bf16[1024,2048]{1,0:T(8,128)(2,1)} %all-gather.9.cloned.1.call-done.refs_0_.refs_1_, bf16[2048,1024]{1,0:T(8,128)(2,1)} %copy-done.6), kind=kOutput, calls=%fused_computation.1 | convolution fusion | flops 4308598784 | bytes 20971520 | tf_op jit(solution)/shard_map/dot_general | solution.py:22
  418.6 4.6 fusion.42
  423.2 6.2 add_convert_fusion
  429.6 8.8 %shard_map.255 = (bf16[2,512,512]{2,1,0:T(8,128)(2,1)}, bf16[2,512,512]{2,1,0:T(8,128)(2,1)}, bf16[512,512]{1,0:T(8,128)(2,1)}, bf16[512,512]{1,0:T(8,128)(2,1)}, bf16[1024,512]{1,0:T(8,128)(2,1)}) custom-call(bf16[1024,2048]{1,0:T(8,128)(2,1)} %all-gather.9.cloned.1.call-done.refs_0_.refs_1_, ...), custom_call_target="tpu_custom_call" | custom-call | bytes 209715200 | tf_op jit(solution)/shard_map/pallas_call | solution.py:282
  441.4 14.7 %shard_map.256 = (bf16[2,512,1024]{2,1,0:T(8,128)(2,1)}, bf16[2,512,1024]{2,1,0:T(8,128)(2,1)}, bf16[512,1024]{1,0:T(8,128)(2,1)}, bf16[512,1024]{1,0:T(8,128)(2,1)}, bf16[1024,1024]{1,0:T(8,128)(2,1)}) custom-call(bf16[1024,2048]{1,0:T(8,128)(2,1)} %all-gather.7.cloned.1.call-done.refs_0_.refs_1_.refs_2_.refs_3_, ...), custom_call_target="tpu_custom_call" | custom-call | bytes 209715200 | tf_op jit(solution)/shard_map/pallas_call | solution.py:282
  456.1 7.9 %collective-permute-done.33 = bf16[2,512,512]{2,1,0:T(8,128)(2,1)} collective-permute-done((bf16[2,512,512]{2,1,0:T(8,128)(2,1)}, bf16[2,512,512]{2,1,0:T(8,128)(2,1)}, u32[]{:S(2)}, u32[]{:S(2)}) %collective-permute-start.33) | collective-permute-done | bytes 1048608 | tf_op jit(solution)/shard_map/ppermute | solution.py:34
  465.2 12.7 %reduce-scatter.9.cloned.1.call-done = bf16[128,2048]{1,0:T(8,128)(2,1)} async-done(((bf16[1024,2048]{1,0:T(8,128)(2,1)}), bf16[128,2048]{1,0:T(8,128)(2,1)}) %reduce-scatter.9.cloned.1.call-update) | async-done | bytes 524304 | tf_op jit(solution)/shard_map/reduce_scatter | solution.py:619
  485.5 10.2 %collective-permute-done.36 = bf16[512,512]{1,0:T(8,128)(2,1)S(1)} collective-permute-done((bf16[512,512]{1,0:T(8,128)(2,1)S(1)}, bf16[512,512]{1,0:T(8,128)(2,1)S(1)}, u32[]{:S(2)}, u32[]{:S(2)}) %collective-permute-start.36) | collective-permute-done | bytes 524320 | tf_op jit(solution)/shard_map/ppermute | solution.py:34
  495.7 2.5 collective-permute-done.35
  500.2 2.8 broadcast_select_fusion.4
  508.8 17.6 %all-gather.11.cloned.1.call-done.grads.refs_1_.refs_3_ = bf16[1024,2048]{1,0:T(8,128)(2,1)} async-done(((bf16[128,2048]{1,0:T(8,128)(2,1)}), bf16[1024,2048]{1,0:T(8,128)(2,1)}) %all-gather.11.cloned.1.call-update) | async-done | bytes 4194320 | tf_op jit(solution)/shard_map/all_gather | solution.py:622
  526.4 16.9 %shard_map.259 = (f32[1024,512]{1,0:T(8,128)}, bf16[1024,256]{1,0:T(8,128)(2,1)}, f32[8,2,128]{2,1,0:T(2,128)}, f32[2,2,128]{2,1,0:T(2,128)}) custom-call(bf16[1024,2048]{1,0:T(8,128)(2,1)} %all-gather.11.cloned.1.call-done.grads.refs_1_.refs_3_, bf16[2048,256]{1,0:T(8,128)(2,1)} %copy-done.8, bf16[1024,256]{1,0:T(8,128)(2,1)} %get-tuple-element.514.queries, ...), custom_call_target="tpu_custom_call" | custom-call | tf_op jit(solution)/shard_map/pallas_call | solution.py:368
  543.3 2.7 collective-permute-start.41
  548.6 4.3 collective-permute-done.41.refs_1_
  552.8 16.7 %collective-permute-done.42.refs_2_ = bf16[128,1024]{1,0:T(8,128)(2,1)S(1)} collective-permute-done((bf16[128,1024]{1,0:T(8,128)(2,1)S(1)}, bf16[128,1024]{1,0:T(8,128)(2,1)S(1)}, u32[]{:S(2)}, u32[]{:S(2)}) %collective-permute-start.42) | collective-permute-done | bytes 262176 | tf_op jit(solution)/shard_map/ppermute | solution.py:38
  569.7 3.9 collective-permute-done.44
  575.6 2.9 collective-permute-done.45
  579.1 13.2 %shard_map.260 = (bf16[1024,768]{1,0:T(8,128)(2,1)}, bf16[1024,2048]{1,0:T(8,128)(2,1)}) custom-call(f32[1024,512]{1,0:T(8,128)} %get-tuple-element.522.weighted, f32[1024,768]{1,0:T(8,128)} %get-tuple-element.362.qkv, f32[8,2,128]{2,1,0:T(2,128)} %add.204.squares, f32[8,2,128]{2,1,0:T(2,128)} %bitcast.138, bf16[1024,256]{1,0:T(8,128)(2,1)} %get-tuple-element.541.value_grad, ...), custom_call_target="tpu_custom_call" | custom-call | tf_op jit(solution)/shard_map/pallas_call | solution.py:368
  600.0 17.7 %collective-permute-done.47 = bf16[512,1024]{1,0:T(8,128)(2,1)S(1)} collective-permute-done((bf16[512,1024]{1,0:T(8,128)(2,1)S(1)}, bf16[512,1024]{1,0:T(8,128)(2,1)S(1)}, u32[]{:S(2)}, u32[]{:S(2)}) %collective-permute-start.47) | collective-permute-done | bytes 1048608 | tf_op jit(solution)/shard_map/ppermute | solution.py:34
  617.7 2.9 collective-permute-done.46
  620.6 4.1 broadcast_select_fusion
  624.6 9.6 %shard_map.261 = (bf16[2,512,512]{2,1,0:T(8,128)(2,1)}, bf16[2,512,512]{2,1,0:T(8,128)(2,1)}, bf16[512,512]{1,0:T(8,128)(2,1)}, bf16[512,512]{1,0:T(8,128)(2,1)}, bf16[1024,512]{1,0:T(8,128)(2,1)}) custom-call(bf16[1024,2048]{1,0:T(8,128)(2,1)} %all-gather.5.cloned.1.call-done.tokens.refs_0_.refs_2_, ...), custom_call_target="tpu_custom_call" | custom-call | bytes 209715200 | tf_op jit(solution)/shard_map/pallas_call | solution.py:282
  637.2 2.6 shard_map.262
  639.9 3.1 shard_map.263
  646.8 14.2 %collective-permute-done.49 = bf16[2,512,512]{2,1,0:T(8,128)(2,1)S(1)} collective-permute-done((bf16[2,512,512]{2,1,0:T(8,128)(2,1)}, bf16[2,512,512]{2,1,0:T(8,128)(2,1)S(1)}, u32[]{:S(2)}, u32[]{:S(2)}) %collective-permute-start.49) | collective-permute-done | bytes 1048608 | tf_op jit(solution)/shard_map/ppermute | solution.py:34
  666.9 23.9 %collective-permute-done.54.refs_2_ = bf16[128,2048]{1,0:T(8,128)(2,1)} collective-permute-done((bf16[128,2048]{1,0:T(8,128)(2,1)}, bf16[128,2048]{1,0:T(8,128)(2,1)}, u32[]{:S(2)}, u32[]{:S(2)}) %collective-permute-start.54) | collective-permute-done | bytes 524320 | tf_op jit(solution)/shard_map/ppermute | solution.py:38
  693.6 3.4 collective-permute-done.57
  698.6 3.8 shard_map.264
  709.2 2.5 collective-permute-start.61
  713.7 3.4 collective-permute-done.60.refs_1_
  717.1 16.9 %collective-permute-done.61.refs_2_ = bf16[128,1024]{1,0:T(8,128)(2,1)S(1)} collective-permute-done((bf16[128,1024]{1,0:T(8,128)(2,1)}, bf16[128,1024]{1,0:T(8,128)(2,1)S(1)}, u32[]{:S(2)}, u32[]{:S(2)}) %collective-permute-start.61) | collective-permute-done | bytes 262176 | tf_op jit(solution)/shard_map/ppermute | solution.py:38
  734.8 2.6 shard_map.267
  738.7 2.7 fusion.25
  (323 shorter events, 158.0 us)
Async XLA Ops:
  7.2 81.6 %all-gather.5.cloned.1.call-start = ((), (), s32[]{:S(2)}) async-start(), calls=%async_computation.4 | async-start | bytes 4718592 | tf_op jit(solution)/shard_map/all_gather | solution.py:622
  8.0 12.9 %collective-permute-start.3 = (s32[1,128]{1,0:T(1,128)S(1)}, s32[1,128]{1,0:T(1,128)S(1)}, u32[]{:S(2)}, u32[]{:S(2)}) collective-permute-start(s32[1,128]{1,0:T(1,128)S(1)} %fusion.37), channel_id=1, source_target_pairs={{0,2},{2,0},{1,3},{3,1},{4,6},{6,4},{5,7},{7,5},{8,10},{10,8},{9,1... | collective-permute-start | bytes 1544 | tf_op jit(solution)/shard_map/ppermute | solution.py:34
  10.4 10.5 %collective-permute-start = (bf16[128,1024]{1,0:T(8,128)(2,1)}, bf16[128,1024]{1,0:T(8,128)(2,1)S(1)}, u32[]{:S(2)}, u32[]{:S(2)}) collective-permute-start(bf16[128,1024]{1,0:T(8,128)(2,1)} %get-tuple-element.317), channel_id=1, source_target_pairs={{0,8},{8,16},{16,24},{24,0},{1,9},{9,17},{17,25},{25,1},{2,10},{10... | collective-permute-start | bytes 786440 | tf_op jit(solution)/shard_map/ppermute | solution.py:38
  10.4 25.7 %collective-permute-start.1 = (bf16[128,1024]{1,0:T(8,128)(2,1)}, bf16[128,1024]{1,0:T(8,128)(2,1)S(1)}, u32[]{:S(2)}, u32[]{:S(2)}) collective-permute-start(bf16[128,1024]{1,0:T(8,128)(2,1)} %get-tuple-element.318), channel_id=1, source_target_pairs={{0,16},{8,24},{16,0},{24,8},{1,17},{9,25},{17,1},{25,9},{2,18},{10... | collective-permute-start | bytes 786440 | tf_op jit(solution)/shard_map/ppermute | solution.py:38
  12.3 23.8 %collective-permute-start.2 = (bf16[128,1024]{1,0:T(8,128)(2,1)}, bf16[128,1024]{1,0:T(8,128)(2,1)S(1)}, u32[]{:S(2)}, u32[]{:S(2)}) collective-permute-start(bf16[128,1024]{1,0:T(8,128)(2,1)} %get-tuple-element.319), channel_id=1, source_target_pairs={{0,24},{8,0},{16,8},{24,16},{1,25},{9,1},{17,9},{25,17},{2,26},{10... | collective-permute-start | bytes 786440 | tf_op jit(solution)/shard_map/ppermute | solution.py:38
  36.1 197.7 %reduce-scatter.5.cloned.1.call-start = ((), (), s32[]{:S(2)}) async-start(), calls=%async_computation.5 | async-start | bytes 4718592 | tf_op jit(solution)/shard_map/reduce_scatter | solution.py:619
  40.5 6.8 collective-permute-start.10
  45.2 25.5 %collective-permute-start.8 = (bf16[1024,512]{1,0:T(8,128)(2,1)}, bf16[1024,512]{1,0:T(8,128)(2,1)S(1)}, u32[]{:S(2)}, u32[]{:S(2)}) collective-permute-start(bf16[1024,512]{1,0:T(8,128)(2,1)} %shard_map.242.refs_0_), channel_id=1, source_target_pairs={{0,4},{4,0},{1,5},{5,1},{2,6},{6,2},{3,7},{7,3},{8,12},{12,8},{9,1... | collective-permute-start | bytes 3145736 | tf_op jit(solution)/shard_map/ppermute | solution.py:34
  46.7 25.2 %collective-permute-start.9 = (bf16[1024,512]{1,0:T(8,128)(2,1)}, bf16[1024,512]{1,0:T(8,128)(2,1)S(1)}, u32[]{:S(2)}, u32[]{:S(2)}) collective-permute-start(bf16[1024,512]{1,0:T(8,128)(2,1)} %shard_map.242.refs_0_), channel_id=1, source_target_pairs={{0,1},{1,0},{2,3},{3,2},{4,5},{5,4},{6,7},{7,6},{8,9},{9,8},{10,11... | collective-permute-start | bytes 3145736 | tf_op jit(solution)/shard_map/ppermute | solution.py:34
  47.9 4.3 collective-permute-start.4
  47.9 5.8 collective-permute-start.5
  49.1 5.5 collective-permute-start.6
  72.0 13.1 %collective-permute-start.11 = (bf16[512,512]{1,0:T(8,128)(2,1)S(1)}, bf16[512,512]{1,0:T(8,128)(2,1)S(1)}, u32[]{:S(2)}, u32[]{:S(2)}) collective-permute-start(bf16[512,512]{1,0:T(8,128)(2,1)S(1)} %slice.100), channel_id=1, source_target_pairs={{0,4},{4,0},{1,5},{5,1},{2,6},{6,2},{3,7},{7,3},{8,12},{12,8},{9,1... | collective-permute-start | bytes 1572872 | tf_op jit(solution)/shard_map/ppermute | solution.py:34
  72.6 12.9 %collective-permute-start.12 = (bf16[512,512]{1,0:T(8,128)(2,1)S(1)}, bf16[512,512]{1,0:T(8,128)(2,1)S(1)}, u32[]{:S(2)}, u32[]{:S(2)}) collective-permute-start(bf16[512,512]{1,0:T(8,128)(2,1)S(1)} %slice.101), channel_id=1, source_target_pairs={{0,1},{1,0},{2,3},{3,2},{4,5},{5,4},{6,7},{7,6},{8,9},{9,8},{10,11... | collective-permute-start | bytes 1572872 | tf_op jit(solution)/shard_map/ppermute | solution.py:34
  73.2 25.2 %collective-permute-start.14 = (bf16[128,2048]{1,0:T(8,128)(2,1)}, bf16[128,2048]{1,0:T(8,128)(2,1)S(1)}, u32[]{:S(2)}, u32[]{:S(2)}) collective-permute-start(bf16[128,2048]{1,0:T(8,128)(2,1)} %get-tuple-element.365), channel_id=1, source_target_pairs={{0,8},{8,16},{16,24},{24,0},{1,9},{9,17},{17,25},{25,1},{2,10},{10... | collective-permute-start | bytes 1572872 | tf_op jit(solution)/shard_map/ppermute | solution.py:38
  73.2 52.4 %collective-permute-start.15 = (bf16[128,2048]{1,0:T(8,128)(2,1)}, bf16[128,2048]{1,0:T(8,128)(2,1)S(1)}, u32[]{:S(2)}, u32[]{:S(2)}) collective-permute-start(bf16[128,2048]{1,0:T(8,128)(2,1)} %get-tuple-element.366), channel_id=1, source_target_pairs={{0,16},{8,24},{16,0},{24,8},{1,17},{9,25},{17,1},{25,9},{2,18},{10... | collective-permute-start | bytes 1572872 | tf_op jit(solution)/shard_map/ppermute | solution.py:38
  74.4 51.1 %collective-permute-start.16 = (bf16[128,2048]{1,0:T(8,128)(2,1)S(1)}, bf16[128,2048]{1,0:T(8,128)(2,1)S(1)}, u32[]{:S(2)}, u32[]{:S(2)}) collective-permute-start(bf16[128,2048]{1,0:T(8,128)(2,1)S(1)} %copy-done.57), channel_id=1, source_target_pairs={{0,24},{8,0},{16,8},{24,16},{1,25},{9,1},{17,9},{25,17},{2,26},{10... | collective-permute-start | bytes 1572872 | tf_op jit(solution)/shard_map/ppermute | solution.py:38
  137.0 47.9 %collective-permute-start.20 = (bf16[1024,1024]{1,0:T(8,128)(2,1)}, bf16[1024,1024]{1,0:T(8,128)(2,1)S(1)}, u32[]{:S(2)}, u32[]{:S(2)}) collective-permute-start(bf16[1024,1024]{1,0:T(8,128)(2,1)} %shard_map.247.refs_0_), channel_id=1, source_target_pairs={{0,4},{4,0},{1,5},{5,1},{2,6},{6,2},{3,7},{7,3},{8,12},{12,8},{9,1... | collective-permute-start | bytes 6291464 | tf_op jit(solution)/shard_map/ppermute | solution.py:34
  138.4 47.7 %collective-permute-start.21 = (bf16[1024,1024]{1,0:T(8,128)(2,1)}, bf16[1024,1024]{1,0:T(8,128)(2,1)}, u32[]{:S(2)}, u32[]{:S(2)}) collective-permute-start(bf16[1024,1024]{1,0:T(8,128)(2,1)} %shard_map.247.refs_0_), channel_id=1, source_target_pairs={{0,1},{1,0},{2,3},{3,2},{4,5},{5,4},{6,7},{7,6},{8,9},{9,8},{10,11... | collective-permute-start | bytes 6291464 | tf_op jit(solution)/shard_map/ppermute | solution.py:34
  144.8 4.5 collective-permute-start.19
  149.9 16.9 %collective-permute-start.22 = (bf16[128,1024]{1,0:T(8,128)(2,1)}, bf16[128,1024]{1,0:T(8,128)(2,1)S(1)}, u32[]{:S(2)}, u32[]{:S(2)}) collective-permute-start(bf16[128,1024]{1,0:T(8,128)(2,1)} %get-tuple-element.403), channel_id=1, source_target_pairs={{0,8},{8,16},{16,24},{24,0},{1,9},{9,17},{17,25},{25,1},{2,10},{10... | collective-permute-start | bytes 786440 | tf_op jit(solution)/shard_map/ppermute | solution.py:38
  150.4 22.8 %collective-permute-start.23 = (bf16[128,1024]{1,0:T(8,128)(2,1)}, bf16[128,1024]{1,0:T(8,128)(2,1)S(1)}, u32[]{:S(2)}, u32[]{:S(2)}) collective-permute-start(bf16[128,1024]{1,0:T(8,128)(2,1)} %get-tuple-element.404), channel_id=1, source_target_pairs={{0,16},{8,24},{16,0},{24,8},{1,17},{9,25},{17,1},{25,9},{2,18},{10... | collective-permute-start | bytes 786440 | tf_op jit(solution)/shard_map/ppermute | solution.py:38
  151.4 21.8 %collective-permute-start.24 = (bf16[128,1024]{1,0:T(8,128)(2,1)}, bf16[128,1024]{1,0:T(8,128)(2,1)S(1)}, u32[]{:S(2)}, u32[]{:S(2)}) collective-permute-start(bf16[128,1024]{1,0:T(8,128)(2,1)} %get-tuple-element.405), channel_id=1, source_target_pairs={{0,24},{8,0},{16,8},{24,16},{1,25},{9,1},{17,9},{25,17},{2,26},{10... | collective-permute-start | bytes 786440 | tf_op jit(solution)/shard_map/ppermute | solution.py:38
  186.2 99.7 %all-gather.7.cloned.1.call-start = ((), (), s32[]{:S(2)}) async-start(), calls=%async_computation.6 | async-start | bytes 4718592 | tf_op jit(solution)/shard_map/all_gather | solution.py:622
  188.5 24.6 %collective-permute-start.25 = (bf16[512,1024]{1,0:T(8,128)(2,1)}, bf16[512,1024]{1,0:T(8,128)(2,1)S(1)}, u32[]{:S(2)}, u32[]{:S(2)}) collective-permute-start(bf16[512,1024]{1,0:T(8,128)(2,1)} %slice.102), channel_id=1, source_target_pairs={{0,4},{4,0},{1,5},{5,1},{2,6},{6,2},{3,7},{7,3},{8,12},{12,8},{9,1... | collective-permute-start | bytes 3145736 | tf_op jit(solution)/shard_map/ppermute | solution.py:34
  192.2 24.5 %collective-permute-start.26 = (bf16[512,1024]{1,0:T(8,128)(2,1)}, bf16[512,1024]{1,0:T(8,128)(2,1)}, u32[]{:S(2)}, u32[]{:S(2)}) collective-permute-start(bf16[512,1024]{1,0:T(8,128)(2,1)} %slice.103), channel_id=1, source_target_pairs={{0,1},{1,0},{2,3},{3,2},{4,5},{5,4},{6,7},{7,6},{8,9},{9,8},{10,11... | collective-permute-start | bytes 3145736 | tf_op jit(solution)/shard_map/ppermute | solution.py:34
  237.7 118.3 %reduce-scatter.7.cloned.1.call-start = ((), (), s32[]{:S(2)}) async-start(), calls=%async_computation.7 | async-start | bytes 4718592 | tf_op jit(solution)/shard_map/reduce_scatter | solution.py:619
  240.0 25.1 %collective-permute-start.28 = (bf16[1024,512]{1,0:T(8,128)(2,1)}, bf16[1024,512]{1,0:T(8,128)(2,1)S(1)}, u32[]{:S(2)}, u32[]{:S(2)}) collective-permute-start(bf16[1024,512]{1,0:T(8,128)(2,1)} %shard_map.251.refs_0_), channel_id=1, source_target_pairs={{0,4},{4,0},{1,5},{5,1},{2,6},{6,2},{3,7},{7,3},{8,12},{12,8},{9,1... | collective-permute-start | bytes 3145736 | tf_op jit(solution)/shard_map/ppermute | solution.py:34
  240.7 25.6 %collective-permute-start.29 = (bf16[1024,512]{1,0:T(8,128)(2,1)}, bf16[1024,512]{1,0:T(8,128)(2,1)S(1)}, u32[]{:S(2)}, u32[]{:S(2)}) collective-permute-start(bf16[1024,512]{1,0:T(8,128)(2,1)} %shard_map.251.refs_0_), channel_id=1, source_target_pairs={{0,1},{1,0},{2,3},{3,2},{4,5},{5,4},{6,7},{7,6},{8,9},{9,8},{10,11... | collective-permute-start | bytes 3145736 | tf_op jit(solution)/shard_map/ppermute | solution.py:34
  267.2 13.7 %collective-permute-start.30 = (bf16[512,512]{1,0:T(8,128)(2,1)}, bf16[512,512]{1,0:T(8,128)(2,1)}, u32[]{:S(2)}, u32[]{:S(2)}) collective-permute-start(bf16[512,512]{1,0:T(8,128)(2,1)} %slice.104), channel_id=1, source_target_pairs={{0,4},{4,0},{1,5},{5,1},{2,6},{6,2},{3,7},{7,3},{8,12},{12,8},{9,1... | collective-permute-start | bytes 1572872 | tf_op jit(solution)/shard_map/ppermute | solution.py:34
  268.6 13.4 %collective-permute-start.31 = (bf16[512,512]{1,0:T(8,128)(2,1)}, bf16[512,512]{1,0:T(8,128)(2,1)}, u32[]{:S(2)}, u32[]{:S(2)}) collective-permute-start(bf16[512,512]{1,0:T(8,128)(2,1)} %slice.105), channel_id=1, source_target_pairs={{0,1},{1,0},{2,3},{3,2},{4,5},{5,4},{6,7},{7,6},{8,9},{9,8},{10,11... | collective-permute-start | bytes 1572872 | tf_op jit(solution)/shard_map/ppermute | solution.py:34
  307.6 99.4 %all-gather.9.cloned.1.call-start = ((), (), s32[]{:S(2)}) async-start(), calls=%async_computation.8 | async-start | bytes 4718592 | tf_op jit(solution)/shard_map/all_gather | solution.py:622
  361.1 116.8 %reduce-scatter.9.cloned.1.call-start = ((), (), s32[]{:S(2)}) async-start(), calls=%async_computation.9 | async-start | bytes 4718592 | tf_op jit(solution)/shard_map/reduce_scatter | solution.py:619
  363.5 14.0 %collective-permute-start.32 = (bf16[128,2048]{1,0:T(8,128)(2,1)}, bf16[128,2048]{1,0:T(8,128)(2,1)S(1)}, u32[]{:S(2)}, u32[]{:S(2)}) collective-permute-start(bf16[128,2048]{1,0:T(8,128)(2,1)} %shard_map.254), channel_id=1, source_target_pairs={{0,1},{1,0},{2,3},{3,2},{4,5},{5,4},{6,7},{7,6},{8,9},{9,8},{10,11... | collective-permute-start | bytes 1572872 | tf_op jit(solution)/shard_map/ppermute | solution.py:34
  429.4 97.0 %all-gather.11.cloned.1.call-start = ((), (), s32[]{:S(2)}) async-start(), calls=%async_computation.10 | async-start | bytes 4718592 | tf_op jit(solution)/shard_map/all_gather | solution.py:622
  438.4 25.7 %collective-permute-start.33 = (bf16[2,512,512]{2,1,0:T(8,128)(2,1)}, bf16[2,512,512]{2,1,0:T(8,128)(2,1)}, u32[]{:S(2)}, u32[]{:S(2)}) collective-permute-start(bf16[2,512,512]{2,1,0:T(8,128)(2,1)} %get-tuple-element.469), channel_id=1, source_target_pairs={{0,4},{4,0},{1,5},{5,1},{2,6},{6,2},{3,7},{7,3},{8,12},{12,8},{9,1... | collective-permute-start | bytes 3145736 | tf_op jit(solution)/shard_map/ppermute | solution.py:34
  439.9 25.3 %collective-permute-start.34 = (bf16[2,512,512]{2,1,0:T(8,128)(2,1)}, bf16[2,512,512]{2,1,0:T(8,128)(2,1)}, u32[]{:S(2)}, u32[]{:S(2)}) collective-permute-start(bf16[2,512,512]{2,1,0:T(8,128)(2,1)} %get-tuple-element.470), channel_id=1, source_target_pairs={{0,1},{1,0},{2,3},{3,2},{4,5},{5,4},{6,7},{7,6},{8,9},{9,8},{10,11... | collective-permute-start | bytes 3145736 | tf_op jit(solution)/shard_map/ppermute | solution.py:34
  480.6 221.8 %reduce-scatter.11.cloned.1.call-start = ((), (), s32[]{:S(2)}) async-start(), calls=%async_computation.11 | async-start | bytes 4718592 | tf_op jit(solution)/shard_map/reduce_scatter | solution.py:619
  482.0 13.7 %collective-permute-start.36 = (bf16[512,512]{1,0:T(8,128)(2,1)S(1)}, bf16[512,512]{1,0:T(8,128)(2,1)S(1)}, u32[]{:S(2)}, u32[]{:S(2)}) collective-permute-start(bf16[512,512]{1,0:T(8,128)(2,1)S(1)} %fusion.34), channel_id=1, source_target_pairs={{0,4},{4,0},{1,5},{5,1},{2,6},{6,2},{3,7},{7,3},{8,12},{12,8},{9,1... | collective-permute-start | bytes 1572872 | tf_op jit(solution)/shard_map/ppermute | solution.py:34
  483.8 14.4 %collective-permute-start.35 = (bf16[512,512]{1,0:T(8,128)(2,1)S(1)}, bf16[512,512]{1,0:T(8,128)(2,1)S(1)}, u32[]{:S(2)}, u32[]{:S(2)}) collective-permute-start(bf16[512,512]{1,0:T(8,128)(2,1)S(1)} %fusion.35), channel_id=1, source_target_pairs={{0,1},{1,0},{2,3},{3,2},{4,5},{5,4},{6,7},{7,6},{8,9},{9,8},{10,11... | collective-permute-start | bytes 1572872 | tf_op jit(solution)/shard_map/ppermute | solution.py:34
  498.1 50.3 %collective-permute-start.38 = (bf16[2,512,1024]{2,1,0:T(8,128)(2,1)}, bf16[2,512,1024]{2,1,0:T(8,128)(2,1)}, u32[]{:S(2)}, u32[]{:S(2)}) collective-permute-start(bf16[2,512,1024]{2,1,0:T(8,128)(2,1)} %get-tuple-element.526), channel_id=1, source_target_pairs={{0,4},{4,0},{1,5},{5,1},{2,6},{6,2},{3,7},{7,3},{8,12},{12,8},{9,1... | collective-permute-start | bytes 6291464 | tf_op jit(solution)/shard_map/ppermute | solution.py:34
  498.7 49.8 %collective-permute-start.39 = (bf16[2,512,1024]{2,1,0:T(8,128)(2,1)}, bf16[2,512,1024]{2,1,0:T(8,128)(2,1)}, u32[]{:S(2)}, u32[]{:S(2)}) collective-permute-start(bf16[2,512,1024]{2,1,0:T(8,128)(2,1)} %get-tuple-element.527), channel_id=1, source_target_pairs={{0,1},{1,0},{2,3},{3,2},{4,5},{5,4},{6,7},{7,6},{8,9},{9,8},{10,11... | collective-permute-start | bytes 6291464 | tf_op jit(solution)/shard_map/ppermute | solution.py:34
  543.3 9.5 %collective-permute-start.41 = (bf16[128,1024]{1,0:T(8,128)(2,1)S(1)}, bf16[128,1024]{1,0:T(8,128)(2,1)S(1)}, u32[]{:S(2)}, u32[]{:S(2)}) collective-permute-start(bf16[128,1024]{1,0:T(8,128)(2,1)S(1)} %copy-done.60), channel_id=1, source_target_pairs={{0,8},{8,16},{16,24},{24,0},{1,9},{9,17},{17,25},{25,1},{2,10},{10... | collective-permute-start | bytes 786440 | tf_op jit(solution)/shard_map/ppermute | solution.py:38
  546.1 23.4 %collective-permute-start.42 = (bf16[128,1024]{1,0:T(8,128)(2,1)S(1)}, bf16[128,1024]{1,0:T(8,128)(2,1)S(1)}, u32[]{:S(2)}, u32[]{:S(2)}) collective-permute-start(bf16[128,1024]{1,0:T(8,128)(2,1)S(1)} %copy-done.59), channel_id=1, source_target_pairs={{0,16},{8,24},{16,0},{24,8},{1,17},{9,25},{17,1},{25,9},{2,18},{10... | collective-permute-start | bytes 786440 | tf_op jit(solution)/shard_map/ppermute | solution.py:38
  546.2 23.3 %collective-permute-start.43 = (bf16[128,1024]{1,0:T(8,128)(2,1)S(1)}, bf16[128,1024]{1,0:T(8,128)(2,1)S(1)}, u32[]{:S(2)}, u32[]{:S(2)}) collective-permute-start(bf16[128,1024]{1,0:T(8,128)(2,1)S(1)} %copy-done.58), channel_id=1, source_target_pairs={{0,24},{8,0},{16,8},{24,16},{1,25},{9,1},{17,9},{25,17},{2,26},{10... | collective-permute-start | bytes 786440 | tf_op jit(solution)/shard_map/ppermute | solution.py:38
  548.5 21.0 %collective-permute-start.40 = (f32[80,128]{1,0:T(8,128)S(1)}, f32[80,128]{1,0:T(8,128)S(1)}, u32[]{:S(2)}, u32[]{:S(2)}) collective-permute-start(f32[80,128]{1,0:T(8,128)S(1)} %pad_maximum_fusion.2), channel_id=1, source_target_pairs={{0,2},{2,0},{1,3},{3,1},{4,6},{6,4},{5,7},{7,5},{8,10},{10,8},{9,1... | collective-permute-start | bytes 122888 | tf_op jit(solution)/shard_map/ppermute | solution.py:34
  569.5 4.1 collective-permute-start.44
  573.6 4.9 collective-permute-start.45
  595.3 22.4 %collective-permute-start.47 = (bf16[512,1024]{1,0:T(8,128)(2,1)S(1)}, bf16[512,1024]{1,0:T(8,128)(2,1)S(1)}, u32[]{:S(2)}, u32[]{:S(2)}) collective-permute-start(bf16[512,1024]{1,0:T(8,128)(2,1)S(1)} %fusion.4), channel_id=1, source_target_pairs={{0,4},{4,0},{1,5},{5,1},{2,6},{6,2},{3,7},{7,3},{8,12},{12,8},{9,1... | collective-permute-start | bytes 3145736 | tf_op jit(solution)/shard_map/ppermute | solution.py:34
  598.4 22.1 %collective-permute-start.46 = (bf16[512,1024]{1,0:T(8,128)(2,1)S(1)}, bf16[512,1024]{1,0:T(8,128)(2,1)S(1)}, u32[]{:S(2)}, u32[]{:S(2)}) collective-permute-start(bf16[512,1024]{1,0:T(8,128)(2,1)S(1)} %fusion.5), channel_id=1, source_target_pairs={{0,1},{1,0},{2,3},{3,2},{4,5},{5,4},{6,7},{7,6},{8,9},{9,8},{10,11... | collective-permute-start | bytes 3145736 | tf_op jit(solution)/shard_map/ppermute | solution.py:34
  624.6 9.6 %collective-permute-start.48 = (bf16[512,1024]{1,0:T(8,128)(2,1)S(1)}, bf16[512,1024]{1,0:T(8,128)(2,1)S(1)}, u32[]{:S(2)}, u32[]{:S(2)}) collective-permute-start(bf16[512,1024]{1,0:T(8,128)(2,1)S(1)} %get-tuple-element.626), channel_id=1, source_target_pairs={{0,2},{2,0},{1,3},{3,1},{4,6},{6,4},{5,7},{7,5},{8,10},{10,8},{9,1... | collective-permute-start | bytes 3145736 | tf_op jit(solution)/shard_map/ppermute | solution.py:34
  635.2 25.8 %collective-permute-start.49 = (bf16[2,512,512]{2,1,0:T(8,128)(2,1)}, bf16[2,512,512]{2,1,0:T(8,128)(2,1)S(1)}, u32[]{:S(2)}, u32[]{:S(2)}) collective-permute-start(bf16[2,512,512]{2,1,0:T(8,128)(2,1)} %get-tuple-element.565), channel_id=1, source_target_pairs={{0,4},{4,0},{1,5},{5,1},{2,6},{6,2},{3,7},{7,3},{8,12},{12,8},{9,1... | collective-permute-start | bytes 3145736 | tf_op jit(solution)/shard_map/ppermute | solution.py:34
  635.8 25.6 %collective-permute-start.50 = (bf16[2,512,512]{2,1,0:T(8,128)(2,1)}, bf16[2,512,512]{2,1,0:T(8,128)(2,1)}, u32[]{:S(2)}, u32[]{:S(2)}) collective-permute-start(bf16[2,512,512]{2,1,0:T(8,128)(2,1)} %get-tuple-element.566), channel_id=1, source_target_pairs={{0,1},{1,0},{2,3},{3,2},{4,5},{5,4},{6,7},{7,6},{8,9},{9,8},{10,11... | collective-permute-start | bytes 3145736 | tf_op jit(solution)/shard_map/ppermute | solution.py:34
  642.9 24.0 %collective-permute-start.53 = (bf16[128,2048]{1,0:T(8,128)(2,1)}, bf16[128,2048]{1,0:T(8,128)(2,1)S(1)}, u32[]{:S(2)}, u32[]{:S(2)}) collective-permute-start(bf16[128,2048]{1,0:T(8,128)(2,1)} %get-tuple-element.579), channel_id=1, source_target_pairs={{0,8},{8,16},{16,24},{24,0},{1,9},{9,17},{17,25},{25,1},{2,10},{10... | collective-permute-start | bytes 1572872 | tf_op jit(solution)/shard_map/ppermute | solution.py:38
  644.5 46.4 %collective-permute-start.54 = (bf16[128,2048]{1,0:T(8,128)(2,1)}, bf16[128,2048]{1,0:T(8,128)(2,1)}, u32[]{:S(2)}, u32[]{:S(2)}) collective-permute-start(bf16[128,2048]{1,0:T(8,128)(2,1)} %get-tuple-element.580), channel_id=1, source_target_pairs={{0,16},{8,24},{16,0},{24,8},{1,17},{9,25},{17,1},{25,9},{2,18},{10... | collective-permute-start | bytes 1572872 | tf_op jit(solution)/shard_map/ppermute | solution.py:38
  644.8 46.1 %collective-permute-start.55 = (bf16[128,2048]{1,0:T(8,128)(2,1)}, bf16[128,2048]{1,0:T(8,128)(2,1)}, u32[]{:S(2)}, u32[]{:S(2)}) collective-permute-start(bf16[128,2048]{1,0:T(8,128)(2,1)} %get-tuple-element.581), channel_id=1, source_target_pairs={{0,24},{8,0},{16,8},{24,16},{1,25},{9,1},{17,9},{25,17},{2,26},{10... | collective-permute-start | bytes 1572872 | tf_op jit(solution)/shard_map/ppermute | solution.py:38
  662.7 28.2 %collective-permute-start.52 = (bf16[512,512]{1,0:T(8,128)(2,1)S(1)}, bf16[512,512]{1,0:T(8,128)(2,1)S(1)}, u32[]{:S(2)}, u32[]{:S(2)}) collective-permute-start(bf16[512,512]{1,0:T(8,128)(2,1)S(1)} %fusion.29), channel_id=1, source_target_pairs={{0,4},{4,0},{1,5},{5,1},{2,6},{6,2},{3,7},{7,3},{8,12},{12,8},{9,1... | collective-permute-start | bytes 1572872 | tf_op jit(solution)/shard_map/ppermute | solution.py:34
  665.4 25.5 %collective-permute-start.51 = (bf16[512,512]{1,0:T(8,128)(2,1)S(1)}, bf16[512,512]{1,0:T(8,128)(2,1)S(1)}, u32[]{:S(2)}, u32[]{:S(2)}) collective-permute-start(bf16[512,512]{1,0:T(8,128)(2,1)S(1)} %fusion.30), channel_id=1, source_target_pairs={{0,1},{1,0},{2,3},{3,2},{4,5},{5,4},{6,7},{7,6},{8,9},{9,8},{10,11... | collective-permute-start | bytes 1572872 | tf_op jit(solution)/shard_map/ppermute | solution.py:34
  693.2 3.9 collective-permute-start.56
  697.1 5.3 collective-permute-start.58
  706.4 31.0 %collective-permute-start.59 = (bf16[128,2048]{1,0:T(8,128)(2,1)}, bf16[128,2048]{1,0:T(8,128)(2,1)S(1)}, u32[]{:S(2)}, u32[]{:S(2)}) collective-permute-start(bf16[128,2048]{1,0:T(8,128)(2,1)} %shard_map.265), channel_id=1, source_target_pairs={{0,1},{1,0},{2,3},{3,2},{4,5},{5,4},{6,7},{7,6},{8,9},{9,8},{10,11... | collective-permute-start | bytes 1572872 | tf_op jit(solution)/shard_map/ppermute | solution.py:34
  709.2 7.9 %collective-permute-start.60 = (bf16[128,1024]{1,0:T(8,128)(2,1)}, bf16[128,1024]{1,0:T(8,128)(2,1)S(1)}, u32[]{:S(2)}, u32[]{:S(2)}) collective-permute-start(bf16[128,1024]{1,0:T(8,128)(2,1)} %get-tuple-element.600), channel_id=1, source_target_pairs={{0,8},{8,16},{16,24},{24,0},{1,9},{9,17},{17,25},{25,1},{2,10},{10... | collective-permute-start | bytes 786440 | tf_op jit(solution)/shard_map/ppermute | solution.py:38
  709.2 24.8 %collective-permute-start.61 = (bf16[128,1024]{1,0:T(8,128)(2,1)}, bf16[128,1024]{1,0:T(8,128)(2,1)S(1)}, u32[]{:S(2)}, u32[]{:S(2)}) collective-permute-start(bf16[128,1024]{1,0:T(8,128)(2,1)} %get-tuple-element.601), channel_id=1, source_target_pairs={{0,16},{8,24},{16,0},{24,8},{1,17},{9,25},{17,1},{25,9},{2,18},{10... | collective-permute-start | bytes 786440 | tf_op jit(solution)/shard_map/ppermute | solution.py:38
  711.7 22.3 %collective-permute-start.62 = (bf16[128,1024]{1,0:T(8,128)(2,1)}, bf16[128,1024]{1,0:T(8,128)(2,1)S(1)}, u32[]{:S(2)}, u32[]{:S(2)}) collective-permute-start(bf16[128,1024]{1,0:T(8,128)(2,1)} %get-tuple-element.602), channel_id=1, source_target_pairs={{0,24},{8,0},{16,8},{24,16},{1,25},{9,1},{17,9},{25,17},{2,26},{10... | collective-permute-start | bytes 786440 | tf_op jit(solution)/shard_map/ppermute | solution.py:38
  (69 other events, 1052.2 us)
Sparse Core Ops, SparseCore 0:
  36.2 50.1 all-gather.4
  186.3 47.4 reduce-scatter.4
  237.8 45.6 all-gather.6
  307.8 48.2 reduce-scatter.6
  361.2 45.7 all-gather.8
  429.5 48.3 reduce-scatter.8
  480.7 45.6 all-gather.10
  592.4 48.3 reduce-scatter.10

commit v3 on v2

--- a/solution.py
+++ b/solution.py
@@ -306,6 +306,8 @@
 VMEM_LIMIT = 60 << 20
 LOCAL_BYTES = 200 << 20
 HEADS_HERE = 2
+ROWS = 2
+LENGTH = 128
 ROOT = HEAD_DIM ** (-0.5)
 
 
@@ -363,11 +365,11 @@
     def spec(shape, block):
         if block == "whole":
             return pl.BlockSpec(shape, lambda i: (0,) * len(shape))
-        return pl.BlockSpec((block,) + shape[1:], lambda i: (i,) + (0,) * (len(shape) - 1))
+        return pl.BlockSpec((ROWS * block,) + shape[1:], lambda i: (i,) + (0,) * (len(shape) - 1))
 
     return pl.pallas_call(
         kernel,
-        grid=(rows,),
+        grid=(rows // ROWS,),
         in_specs=[spec(v.shape, block) for v, block in ins],
         out_specs=[spec(shape, block) for shape, _, block in outs],
         out_shape=[jax.ShapeDtypeStruct(shape, dtype) for shape, dtype, _ in outs],
@@ -376,92 +378,113 @@
     )(*[v for v, _ in ins])
 
 
+def row_views(row, *refs):
+    return [ref.at[row * LENGTH : (row + 1) * LENGTH] for ref in refs]
+
+
 def project_kernel(tokens, weights, out, squares):
-    product = mm(tokens[...], weights[...])
-    out[...] = product
-    for kind in range(2):
-        total = 0.0
+    out[...] = mm(tokens[...], weights[...])
+    for row in range(ROWS):
+        [product] = row_views(row, out)
+        for kind in range(2):
+            total = 0.0
+            for number in range(HEADS_HERE):
+                part = head(product, kind, number)
+                total = total + jnp.sum(part * part, axis=1, keepdims=True)
+            squares[row, kind : kind + 1] = to_row(total)
+
+
+def attend_kernel(
+    qkv_all, squares, gains, cosine_all, sine_all, segments, weights,
+    query_all, key_all, value_all, mixed_all, out,
+):
+    for row in range(ROWS):
+        qkv, cosine, sine, query_out, key_out, value_out, mixed = row_views(
+            row, qkv_all, cosine_all, sine_all, query_all, key_all, value_all, mixed_all
+        )
+        allowed = allowed_keys(segments[row])
+        scales = [scale_of(squares[row], kind) for kind in range(2)]
         for number in range(HEADS_HERE):
-            part = head(product, kind, number)
-            total = total + jnp.sum(part * part, axis=1, keepdims=True)
-        squares[0, kind : kind + 1] = to_row(total)
-
-
-def attend_kernel(
-    qkv, squares, gains, cosine, sine, segments, weights, query_out, key_out, value_out, mixed, out
-):
-    allowed = allowed_keys(segments[0])
-    scales = [scale_of(squares[0], kind) for kind in range(2)]
-    for number in range(HEADS_HERE):
-        low = [
-            rotated(
-                head(qkv, kind, number) * scales[kind] * gains[kind, number : number + 1],
-                cosine[...],
-                sine[...],
-            ).astype(BF16)
-            for kind in range(2)
-        ]
-        value = head(qkv, 2, number).astype(BF16)
-        probs = softmax_of(*low, allowed).astype(BF16)
-        where = slice(number * HEAD_DIM, (number + 1) * HEAD_DIM)
-        query_out[:, where] = low[0]
-        key_out[:, where] = low[1]
-        value_out[:, where] = value
-        mixed[:, where] = mm(probs, value).astype(BF16)
-    out[...] = mm(mixed[...], weights[...], NT).astype(BF16)
+            low = [
+                rotated(
+                    head(qkv, kind, number) * scales[kind] * gains[kind, number : number + 1],
+                    cosine[...],
+                    sine[...],
+                ).astype(BF16)
+                for kind in range(2)
+            ]
+            value = head(qkv, 2, number).astype(BF16)
+            probs = softmax_of(*low, allowed).astype(BF16)
+            where = slice(number * HEAD_DIM, (number + 1) * HEAD_DIM)
+            query_out[:, where] = low[0]
+            key_out[:, where] = low[1]
+            value_out[:, where] = value
+            mixed[:, where] = mm(probs, value).astype(BF16)
+    out[...] = mm(mixed_all[...], weights[...], NT).astype(BF16)
 
 
 def attend_back_kernel(
-    grads, weights, queries, keys, values, qkv, squares, gains, cosine, sine, segments,
-    weighted, value_grad, inner, gain_grad,
+    grads, weights, query_all, key_all, value_all, qkv_all, squares, gains, cosine_all, sine_all,
+    segments, weighted_all, value_grad_all, inner, gain_grad,
 ):
     @pl.when(pl.program_id(0) == 0)
     def _():
         gain_grad[...] = jnp.zeros_like(gain_grad)
 
-    allowed = allowed_keys(segments[0])
-    scales = [scale_of(squares[0], kind) for kind in range(2)]
     mixed_grads = mm(grads[...], weights[...]).astype(BF16)
-    sums = [0.0, 0.0]
-    for number in range(HEADS_HERE):
-        query, key, value = pair(queries, number), pair(keys, number), pair(values, number)
-        mixed_grad = pair(mixed_grads, number)
-        probs = softmax_of(query, key, allowed)
-        where = slice(number * HEAD_DIM, (number + 1) * HEAD_DIM)
-        value_grad[:, where] = mm(probs.astype(BF16), mixed_grad, TN).astype(BF16)
-        prob_grad = mm(mixed_grad, value, NT)
-        score_grad = probs * (prob_grad - jnp.sum(probs * prob_grad, axis=1, keepdims=True))
-        score_low = (score_grad * ROOT).astype(BF16)
-        turned = (mm(score_low, key), mm(score_low, query, TN))
+    for row in range(ROWS):
+        queries, keys, values, qkv, cosine, sine, weighted, value_grad = row_views(
+            row, query_all, key_all, value_all, qkv_all, cosine_all, sine_all, weighted_all,
+            value_grad_all,
+        )
+        allowed = allowed_keys(segments[row])
+        scales = [scale_of(squares[row], kind) for kind in range(2)]
+        sums = [0.0, 0.0]
+        for number in range(HEADS_HERE):
+            query, key, value = pair(queries, number), pair(keys, number), pair(values, number)
+            mixed_grad = pair(mixed_grads[row * LENGTH : (row + 1) * LENGTH], number)
+            probs = softmax_of(query, key, allowed)
+            where = slice(number * HEAD_DIM, (number + 1) * HEAD_DIM)
+            value_grad[:, where] = mm(probs.astype(BF16), mixed_grad, TN).astype(BF16)
+            prob_grad = mm(mixed_grad, value, NT)
+            score_grad = probs * (prob_grad - jnp.sum(probs * prob_grad, axis=1, keepdims=True))
+            score_low = (score_grad * ROOT).astype(BF16)
+            turned = (mm(score_low, key), mm(score_low, query, TN))
+            for kind in range(2):
+                normed = rotated(turned[kind], cosine[...], -sine[...])
+                part = head(qkv, kind, number)
+                gain_grad[kind, number : number + 1] += jnp.sum(
+                    normed * part * scales[kind], axis=0, keepdims=True
+                )
+                normed = normed * gains[kind, number : number + 1]
+                sums[kind] = sums[kind] + jnp.sum(part * normed, axis=1, keepdims=True)
+                start = (kind * HEADS_HERE + number) * HEAD_DIM
+                weighted[:, start : start + HEAD_DIM] = normed
         for kind in range(2):
-            normed = rotated(turned[kind], cosine[...], -sine[...])
-            part = head(qkv, kind, number)
-            gain_grad[kind, number : number + 1] += jnp.sum(
-                normed * part * scales[kind], axis=0, keepdims=True
-            )
-            normed = normed * gains[kind, number : number + 1]
-            sums[kind] = sums[kind] + jnp.sum(part * normed, axis=1, keepdims=True)
-            start = (kind * HEADS_HERE + number) * HEAD_DIM
-            weighted[:, start : start + HEAD_DIM] = normed
-    for kind in range(2):
-        inner[0, kind : kind + 1] = to_row(sums[kind])
-
-
-def input_grad_kernel(weighted, qkv, squares, inner, value_grad, weights, qkv_grad, out):
-    for kind in range(2):
-        scale = scale_of(squares[0], kind)
-        shift_by = scale * scale * scale * (to_column(inner[0][kind : kind + 1]) / D)
+            inner[row, kind : kind + 1] = to_row(sums[kind])
+
+
+def input_grad_kernel(
+    weighted_all, qkv_all, squares, inner, value_grad_all, weights, qkv_grad_all, out
+):
+    for row in range(ROWS):
+        weighted, qkv, value_grad, qkv_grad = row_views(
+            row, weighted_all, qkv_all, value_grad_all, qkv_grad_all
+        )
+        for kind in range(2):
+            scale = scale_of(squares[row], kind)
+            shift_by = scale * scale * scale * (to_column(inner[row][kind : kind + 1]) / D)
+            for number in range(HEADS_HERE):
+                start = (kind * HEADS_HERE + number) * HEAD_DIM
+                part = weighted[:, start : start + HEAD_DIM]
+                start = (number * 3 + kind) * HEAD_DIM
+                qkv_grad[:, start : start + HEAD_DIM] = (
+                    scale * part - head(qkv, kind, number) * shift_by
+                ).astype(BF16)
         for number in range(HEADS_HERE):
-            start = (kind * HEADS_HERE + number) * HEAD_DIM
-            part = weighted[:, start : start + HEAD_DIM]
-            start = (number * 3 + kind) * HEAD_DIM
-            qkv_grad[:, start : start + HEAD_DIM] = (
-                scale * part - head(qkv, kind, number) * shift_by
-            ).astype(BF16)
-    for number in range(HEADS_HERE):
-        start = (number * 3 + 2) * HEAD_DIM
-        qkv_grad[:, start : start + HEAD_DIM] = pair(value_grad, number)
-    out[...] = mm(qkv_grad[...], weights[...], NT).astype(BF16)
+            start = (number * 3 + 2) * HEAD_DIM
+            qkv_grad[:, start : start + HEAD_DIM] = pair(value_grad, number)
+    out[...] = mm(qkv_grad_all[...], weights[...], NT).astype(BF16)
 
 
 class Place:
@@ -633,8 +656,8 @@
     own_row = place.to_local(pick(tokens, place.x, 0)[0])
     segments = pick(segment_ids, place.x, 0)
     segments = ordered(place.c, segments, swap(segments, "c"), 0)[:, 0]
-    gate = pack([gate_proj, up_proj], place.g)
-    feed = pack([down_proj], place.g)
+    gate = pack([gate_proj], place.g)
+    feed = pack([up_proj, down_proj], place.g)
     attn, own_row, segments, gate, feed = step(attn, own_row, segments, gate, feed)
     all_rows = team_gather(own_row)
     segments = [segments] + [shift(segments, by) for by in range(1, GROUP)]
@@ -668,7 +691,7 @@
     squares, feed = step(squares, feed)
     feed = place.send(feed)
     low = ((count, 2 * HEAD_DIM), BF16, length)
-    query_low, key_low, value_low, mixed, attn_part = step(
+    query_low, key_low, value_low, mixed, attn_part, gate = step(
         *row_call(
             attend_kernel,
             slots,
@@ -682,15 +705,16 @@
                 (out_full, "whole"),
             ],
             [low, low, low, low, ((count, D), BF16, length)],
-        )
-    )
+        ),
+        gate,
+    )
+    gate = place.widened(gate)
     attn_part, gate, feed = step(attn_part, gate, feed)
     projected = team_scatter(attn_part)
-    gate = place.widened(gate)
     feed = place.settle(feed)
     feed = place.widen(place.settled(step(feed)))
-    gate = step(gate)
     width = gate_proj.shape[1] // slots
+    feed = step(feed)
     projected = step(projected)
     projected = projected.astype(F32)
     attn_gain, mlp_gain = place.to_local(jnp.stack([attn_gain, mlp_gain]))
@@ -698,9 +722,9 @@
     hidden = own_row.astype(F32) + projected * projected_scale * attn_gain
     hidden_low, hidden = step(hidden.astype(BF16), hidden)
     hidden_all = team_gather(hidden_low)
-    gate_full, up_full = step(place.join(gate, [(0, width), (width, 2 * width)]))
-    feed = place.widened(step(feed))
-    [down_full] = place.join(step(feed), [(0, width)])
+    [gate_full] = step(place.join(gate, [(0, width)]))
+    feed = place.widened(feed)
+    up_full, down_full = place.join(step(feed), [(0, width), (width, 2 * width)])
     own_cotangent = place.to_local(pick(cotangent, place.x, 0)[0]).astype(F32)
     hidden_all, gate_full, up_full, down_full, own_cotangent = step(
         hidden_all, gate_full, up_full, down_full, own_cotangent
@@ -749,7 +773,7 @@
 
     projected_all, down = step(projected_all, down)
     down = place.send(down)
-    weighted, value_grad, inner, head_gain_grads = step(
+    weighted, value_grad, inner, head_gain_grads, down, feed_came = step(
         *row_call(
             attend_back_kernel,
             slots,
@@ -772,7 +796,9 @@
                 ((slots, 2, length), F32, 1),
                 (gains.shape, F32, "whole"),
             ],
-        )
+        ),
+        down,
+        feed_came,
     )
     spots = jnp.zeros((2, 2, slots, HEAD_DIM), F32)
     for number in range(2):
@@ -782,12 +808,11 @@
             (0, place.x if number == 0 else 1 - place.x, slot, 0),
         )
     message = jnp.concatenate([v.reshape(-1, HEAD_DIM) for v in (inner, spots, norm_gain_grads)])
-    message, feed_came = step(message, feed_came)
     feed_more = place.narrow_next(feed, feed_came)
-    down = step(down)
     message = team_sum(message)
     inner, gain_grads = message[: 2 * slots].reshape(inner.shape), message[2 * slots :]
-    qkv_grad, input_part = step(
+    gain_x = swap(gain_grads, "x")
+    qkv_grad, input_part, feed_more, gain_x = step(
         *row_call(
             input_grad_kernel,
             slots,
@@ -800,31 +825,31 @@
                 (qkv_full, "whole"),
             ],
             [((count, 6 * HEAD_DIM), BF16, length), ((count, D), BF16, length)],
-        )
+        ),
+        feed_more,
+        gain_x,
     )
     input_part = team_scatter(input_part)
-    feed = place.unsettle(place.narrowed(feed, feed_came, step(feed_more)))
-    feed = place.collect(step(feed))
     attn = step(
         weight_grads([(all_rows, qkv_grad), (projected_all, mixed)], reps, [cut, HEAD_DIM])
     )
     attn_came = place.narrow(attn)
+    feed = step(place.unsettle(place.narrowed(feed, feed_came, feed_more)))
+    feed = place.send(step(deal(*feed, place.g, place.c)))
+    gain_grads = gain_grads + gain_x
+    gain_q = swap(gain_grads, "q") if reps == 2 else lax.psum(gain_grads, "q") - gain_grads
     [down_grad] = step(unpack(down, place.g, 1))
     attn_came = step(attn_came)
     attn_more = place.narrow_next(attn, attn_came)
-    gain_x = swap(gain_grads, "x")
     feed = step(feed)
     attn_more = step(attn_more)
-    attn = place.unsettle(place.narrowed(attn, attn_came, attn_more))
-    attn, gain_x = step(attn, gain_x)
-    attn = place.collect(attn)
-    gain_grads = gain_grads + gain_x
-    gain_q = swap(gain_grads, "q") if reps == 2 else lax.psum(gain_grads, "q") - gain_grads
-    gate_grad, up_grad = step(unpack(feed, place.g, 2))
+    attn = step(place.unsettle(place.narrowed(attn, attn_came, attn_more)))
+    attn = place.send(step(deal(*attn, place.g, place.c)))
     input_part, gain_q = step(input_part, gain_q)
+    summed = (gain_grads + gain_q).reshape(4, D)
     own_grad = place.to_global((hidden_grad + input_part.astype(F32)).astype(BF16))
     own_grad_x = swap(own_grad, "x")
-    summed = (gain_grads + gain_q).reshape(4, D)
+    gate_grad, up_grad = unpack(feed, place.g, 2)
     attn_grads = unpack(step(attn), place.g, 4)
     tokens_grad = ordered(place.x, own_grad, step(own_grad_x), 0)[:, None].astype(F32)
     summed = summed + step.token

time: 759 us -> 736 us (0.970)
  waiting for transfers between devices: 407 us -> 390 us
  Pallas kernels: 142 us -> 133 us
    reduce_scatter x4, waiting for transfers between devices: 78.1 us -> 60.9 us  [team_scatter(): return lax.psum_scatter(value, TEAM, scatter_dimension=0, tiled=True)]
    ppermute x38, waiting for transfers between devices: 153 us -> 137 us  [swap(): return lax.ppermute(value, axis, [(0, 1), (1, 0)])]
    all_gather x4, waiting for transfers between devices: 44.8 us -> 55.7 us  [team_gather(): return lax.all_gather(value, TEAM, axis=0, tiled=True)]
    pallas_call x4, Pallas kernels: 53.4 us -> 44.8 us  [row_call(): pl.pallas_call(kernel, grid=(rows // ROWS,), in_specs=[spec(v.shape, bloc...]
    unnamed x124 -> x122, local copies, waits for them, and re-layouts: 19 us -> 23.5 us
  transfers between devices with their start and end apart: 71 -> 71, of which waited for: 44 -> 40; matrix products, arithmetic and copies ran while one was open for 6% -> 5% of each run, Pallas kernels for 16% -> 17%
where the time goes in v3:
time: 736 us; the launch traced here: 726 us
  waiting for transfers between devices  390 us (53%)
  Pallas kernels  133 us (18%)
  starting transfers between devices  62.5 us (8%)
  other arithmetic  49.1 us (7%)
  matrix products  42.6 us (6%)
  local copies, waits for them, and re-layouts  33.8 us (5%)
  between operations  15.3 us (2%)
    ppermute x38, waiting for transfers between devices, swap(): return lax.ppermute(value, axis, [(0, 1), (1, 0)])  137 us
    ppermute x21, waiting for transfers between devices, shift(): lax.ppermute(value, 'g', [(i, (i + by) % GROUP) for i in range(GROUP)])  124 us
    reduce_scatter x4, waiting for transfers between devices, team_scatter(): return lax.psum_scatter(value, TEAM, scatter_dimension=0, tiled=True)  60.9 us
    all_gather x4, waiting for transfers between devices, team_gather(): return lax.all_gather(value, TEAM, axis=0, tiled=True)  55.7 us
    pallas_call x4, Pallas kernels, row_call(): pl.pallas_call(kernel, grid=(rows // ROWS,), in_specs=[spec(v.shape, bloc...  44.8 us
    pallas_call x15, Pallas kernels, vmem_call(): pl.pallas_call(kernel, out_shape=shapes, in_specs=[pl.BlockSpec(memory_sp...  39.5 us
    pallas_call x3, Pallas kernels, weight_grads(): pl.pallas_call(kernel, grid=(steps,), in_specs=[pl.BlockSpec((count, step...  33.4 us
    ppermute x38, starting transfers between devices, swap(): return lax.ppermute(value, axis, [(0, 1), (1, 0)])  31.2 us
  transfers between devices with their start and end apart: 71, of which 40 were waited for; matrix products, arithmetic and copies ran while one was open for 5% of the time, Pallas kernels for 17%

profile of v3, /device:TPU:24, one launch (start us, length us, event | category | flops | bytes accessed | tf_op | source)
XLA Modules:
  0.0 726.2 jit_solution(2584828605218840281)
XLA Ops:
  8.0 2.4 shard_map.237
  17.8 3.1 shard_map.240
  21.0 15.1 %collective-permute-done.1.refs_2_ = bf16[128,1024]{1,0:T(8,128)(2,1)S(1)} collective-permute-done((bf16[128,1024]{1,0:T(8,128)(2,1)}, bf16[128,1024]{1,0:T(8,128)(2,1)S(1)}, u32[]{:S(2)}, u32[]{:S(2)}) %collective-permute-start.1) | collective-permute-done | bytes 262176 | tf_op jit(solution)/shard_map/ppermute | solution.py:38
  55.6 15.1 %collective-permute-done.8.refs_1_ = bf16[1024,512]{1,0:T(8,128)(2,1)S(1)} collective-permute-done((bf16[1024,512]{1,0:T(8,128)(2,1)}, bf16[1024,512]{1,0:T(8,128)(2,1)S(1)}, u32[]{:S(2)}, u32[]{:S(2)}) %collective-permute-start.8) | collective-permute-done | bytes 1048608 | tf_op jit(solution)/shard_map/ppermute | solution.py:34
  80.4 4.7 collective-permute-done.11.refs_3_
  88.8 7.8 %shard_map.244 = (f32[1024,768]{1,0:T(8,128)}, f32[8,2,128]{2,1,0:T(2,128)}) custom-call(bf16[1024,2048]{1,0:T(8,128)(2,1)} %all-gather.5.cloned.1.call-done.tokens.refs_0_.refs_2_, bf16[2048,768]{1,0:T(8,128)(2,1)} %copy-done.2), custom_call_target="tpu_custom_call" | custom-call | tf_op jit(solution)/shard_map/pallas_call | solution.py:370
  96.7 6.4 collective-permute-done.15.refs_2_
  116.9 3.6 collective-permute-done.18
  120.6 2.6 collective-permute-start.19
  125.7 4.1 collective-permute-start.24
  130.4 11.0 %shard_map.246 = (bf16[1024,256]{1,0:T(8,128)(2,1)}, bf16[1024,256]{1,0:T(8,128)(2,1)}, bf16[1024,256]{1,0:T(8,128)(2,1)}, bf16[1024,256]{1,0:T(8,128)(2,1)}, bf16[1024,2048]{1,0:T(8,128)(2,1)}) custom-call(f32[1024,768]{1,0:T(8,128)} %get-tuple-element.363.qkv_all, f32[8,2,128]{2,1,0:T(2,128)} %add.204.squares, f32[2,2,128]{2,1,0:T(2,128)} %pad_maximum_fusion.5.gains, ...), custom_call_target="tpu_custom_call" | custom-call | tf_op jit(solution)/shard_map/pallas_call | solution.py:370
  142.7 30.3 %collective-permute-done.25.refs_2_ = bf16[128,2048]{1,0:T(8,128)(2,1)S(1)} collective-permute-done((bf16[128,2048]{1,0:T(8,128)(2,1)}, bf16[128,2048]{1,0:T(8,128)(2,1)S(1)}, u32[]{:S(2)}, u32[]{:S(2)}) %collective-permute-start.25) | collective-permute-done | bytes 524320 | tf_op jit(solution)/shard_map/ppermute | solution.py:38
  174.8 3.0 shard_map.248
  177.8 2.9 collective-permute-done.27.second
  181.7 3.0 shard_map.249.refs_0_
  188.9 43.6 %collective-permute-done.28.refs_1_ = bf16[1024,1024]{1,0:T(8,128)(2,1)S(1)} collective-permute-done((bf16[1024,1024]{1,0:T(8,128)(2,1)}, bf16[1024,1024]{1,0:T(8,128)(2,1)S(1)}, u32[]{:S(2)}, u32[]{:S(2)}) %collective-permute-start.28) | collective-permute-done | bytes 2097184 | tf_op jit(solution)/shard_map/ppermute | solution.py:34
  234.3 2.6 fusion.39
  237.0 2.4 slice.104
  243.3 2.4 shard_map.253
  245.7 2.3 convert_element_type.255
  255.4 8.3 %collective-permute-done.30.refs_3_ = bf16[512,1024]{1,0:T(8,128)(2,1)} collective-permute-done((bf16[512,1024]{1,0:T(8,128)(2,1)}, bf16[512,1024]{1,0:T(8,128)(2,1)}, u32[]{:S(2)}, u32[]{:S(2)}) %collective-permute-start.30) | collective-permute-done | bytes 1048608 | tf_op jit(solution)/shard_map/ppermute | solution.py:34
  265.8 2.6 shard_map.252
  272.5 9.9 %all-gather.7.cloned.1.call-done.refs_0_.refs_1_.refs_2_.refs_3_ = bf16[1024,2048]{1,0:T(8,128)(2,1)} async-done(((bf16[128,2048]{1,0:T(8,128)(2,1)}), bf16[1024,2048]{1,0:T(8,128)(2,1)}) %all-gather.7.cloned.1.call-update) | async-done | bytes 4194320 | tf_op jit(solution)/shard_map/all_gather | solution.py:645
  282.4 7.6 %fusion.42 = f32[1024,1024]{1,0:T(8,128)S(1)} fusion(bf16[1024,2048]{1,0:T(8,128)(2,1)} %all-gather.7.cloned.1.call-done.refs_0_.refs_1_.refs_2_.refs_3_, bf16[2048,1024]{1,0:T(8,128)(2,1)} %copy-done.4), kind=kOutput, calls=%fused_computation.117 | convolution fusion | flops 4294967296 | bytes 12582912 | tf_op jit(solution)/shard_map/dot_general | solution.py:22
  290.1 6.6 multiply_convert_fusion.2
  298.1 6.2 convolution_convert_fusion
  304.3 48.3 %reduce-scatter.7.cloned.1.call-done = bf16[128,2048]{1,0:T(8,128)(2,1)} async-done(((bf16[1024,2048]{1,0:T(8,128)(2,1)}), bf16[128,2048]{1,0:T(8,128)(2,1)}) %reduce-scatter.7.cloned.1.call-update) | async-done | bytes 524304 | tf_op jit(solution)/shard_map/reduce_scatter | solution.py:642
  355.2 2.4 fusion.24
  360.6 13.2 %collective-permute-done.32 = bf16[128,2048]{1,0:T(8,128)(2,1)S(1)} collective-permute-done((bf16[128,2048]{1,0:T(8,128)(2,1)}, bf16[128,2048]{1,0:T(8,128)(2,1)S(1)}, u32[]{:S(2)}, u32[]{:S(2)}) %collective-permute-start.32) | collective-permute-done | bytes 524320 | tf_op jit(solution)/shard_map/ppermute | solution.py:34
  373.8 2.4 maximum_select_fusion
  376.2 27.4 %all-gather.9.cloned.1.call-done.refs_0_.refs_1_ = bf16[1024,2048]{1,0:T(8,128)(2,1)} async-done(((bf16[128,2048]{1,0:T(8,128)(2,1)}), bf16[1024,2048]{1,0:T(8,128)(2,1)}) %all-gather.9.cloned.1.call-update) | async-done | bytes 4194320 | tf_op jit(solution)/shard_map/all_gather | solution.py:645
  403.6 11.5 %multiply_convert_fusion = (bf16[1024,1024]{1,0:T(8,128)(2,1)S(1)}, bf16[1024,1024]{1,0:T(8,128)(2,1)S(1)}) fusion(f32[1024,1024]{1,0:T(8,128)} %copy-done.60, f32[1024,1024]{1,0:T(8,128)} %get-tuple-element.654, bf16[1024,2048]{1,0:T(8,128)(2,1)} %all-gather.9.cloned.1.call-done.refs_0_.refs_1_, bf16[2048,1024]{1,0:T(8,128)(2,1)} %copy-done.18), kind=kOutput, calls=%fused_computation.1 | convolution fusion | flops 4308598784 | bytes 20971520 | tf_op jit(solution)/shard_map/dot_general | solution.py:22
  415.2 4.6 fusion.43
  419.8 6.2 add_convert_fusion
  426.2 8.8 %shard_map.255 = (bf16[2,512,512]{2,1,0:T(8,128)(2,1)}, bf16[2,512,512]{2,1,0:T(8,128)(2,1)}, bf16[512,512]{1,0:T(8,128)(2,1)}, bf16[512,512]{1,0:T(8,128)(2,1)}, bf16[1024,512]{1,0:T(8,128)(2,1)}) custom-call(bf16[1024,2048]{1,0:T(8,128)(2,1)} %all-gather.9.cloned.1.call-done.refs_0_.refs_1_, ...), custom_call_target="tpu_custom_call" | custom-call | bytes 209715200 | tf_op jit(solution)/shard_map/pallas_call | solution.py:282
  438.0 14.7 %shard_map.256 = (bf16[2,512,1024]{2,1,0:T(8,128)(2,1)}, bf16[2,512,1024]{2,1,0:T(8,128)(2,1)}, bf16[512,1024]{1,0:T(8,128)(2,1)}, bf16[512,1024]{1,0:T(8,128)(2,1)}, bf16[1024,1024]{1,0:T(8,128)(2,1)}) custom-call(bf16[1024,2048]{1,0:T(8,128)(2,1)} %all-gather.7.cloned.1.call-done.refs_0_.refs_1_.refs_2_.refs_3_, ...), custom_call_target="tpu_custom_call" | custom-call | bytes 209715200 | tf_op jit(solution)/shard_map/pallas_call | solution.py:282
  452.7 7.9 %collective-permute-done.33 = bf16[2,512,512]{2,1,0:T(8,128)(2,1)} collective-permute-done((bf16[2,512,512]{2,1,0:T(8,128)(2,1)}, bf16[2,512,512]{2,1,0:T(8,128)(2,1)}, u32[]{:S(2)}, u32[]{:S(2)}) %collective-permute-start.33) | collective-permute-done | bytes 1048608 | tf_op jit(solution)/shard_map/ppermute | solution.py:34
  461.9 12.6 %reduce-scatter.9.cloned.1.call-done = bf16[128,2048]{1,0:T(8,128)(2,1)} async-done(((bf16[1024,2048]{1,0:T(8,128)(2,1)}), bf16[128,2048]{1,0:T(8,128)(2,1)}) %reduce-scatter.9.cloned.1.call-update) | async-done | bytes 524304 | tf_op jit(solution)/shard_map/reduce_scatter | solution.py:642
  481.9 10.4 %collective-permute-done.36 = bf16[512,512]{1,0:T(8,128)(2,1)S(1)} collective-permute-done((bf16[512,512]{1,0:T(8,128)(2,1)S(1)}, bf16[512,512]{1,0:T(8,128)(2,1)S(1)}, u32[]{:S(2)}, u32[]{:S(2)}) %collective-permute-start.36) | collective-permute-done | bytes 524320 | tf_op jit(solution)/shard_map/ppermute | solution.py:34
  492.3 2.5 collective-permute-done.35
  496.8 2.8 broadcast_select_fusion.4
  502.3 2.4 shard_map.258
  504.7 18.3 %all-gather.11.cloned.1.call-done.grads.refs_1_.refs_3_ = bf16[1024,2048]{1,0:T(8,128)(2,1)} async-done(((bf16[128,2048]{1,0:T(8,128)(2,1)}), bf16[1024,2048]{1,0:T(8,128)(2,1)}) %all-gather.11.cloned.1.call-update) | async-done | bytes 4194320 | tf_op jit(solution)/shard_map/all_gather | solution.py:645
  523.0 2.7 collective-permute-start.38
  526.3 17.0 %shard_map.259 = (f32[1024,512]{1,0:T(8,128)}, bf16[1024,256]{1,0:T(8,128)(2,1)}, f32[8,2,128]{2,1,0:T(2,128)}, f32[2,2,128]{2,1,0:T(2,128)}) custom-call(bf16[1024,2048]{1,0:T(8,128)(2,1)} %all-gather.11.cloned.1.call-done.grads.refs_1_.refs_3_, bf16[2048,256]{1,0:T(8,128)(2,1)} %copy-done.6, bf16[1024,256]{1,0:T(8,128)(2,1)} %get-tuple-element.513.query_all, ...), custom_call_target="tpu_custom_call" | custom-call | tf_op jit(solution)/shard_map/pallas_call | solution.py:370
  543.4 6.0 collective-permute-done.39.refs_2_
  549.3 2.8 fusion.4
  553.6 2.6 fusion.5
  559.4 4.0 collective-permute-done.44
  565.2 3.1 collective-permute-done.45
  569.5 8.9 %shard_map.260 = (bf16[1024,768]{1,0:T(8,128)(2,1)}, bf16[1024,2048]{1,0:T(8,128)(2,1)}) custom-call(f32[1024,512]{1,0:T(8,128)} %get-tuple-element.527.weighted_all, f32[1024,768]{1,0:T(8,128)} %get-tuple-element.363.qkv_all, f32[8,2,128]{2,1,0:T(2,128)} %add.204.squares, f32[8,2,128]{2,1,0:T(2,128)} %bitcast.141, ...), custom_call_target="tpu_custom_call" | custom-call | tf_op jit(solution)/shard_map/pallas_call | solution.py:370
  578.5 2.9 collective-permute-done.48
  581.4 5.0 broadcast_select_fusion
  586.4 9.9 %shard_map.261 = (bf16[2,512,512]{2,1,0:T(8,128)(2,1)}, bf16[2,512,512]{2,1,0:T(8,128)(2,1)}, bf16[512,512]{1,0:T(8,128)(2,1)}, bf16[512,512]{1,0:T(8,128)(2,1)}, bf16[1024,512]{1,0:T(8,128)(2,1)}) custom-call(bf16[1024,2048]{1,0:T(8,128)(2,1)} %all-gather.5.cloned.1.call-done.tokens.refs_0_.refs_2_, ...), custom_call_target="tpu_custom_call" | custom-call | bytes 209715200 | tf_op jit(solution)/shard_map/pallas_call | solution.py:282
  598.0 2.7 shard_map.262
  600.7 3.0 shard_map.263
  607.9 14.2 %collective-permute-done.50 = bf16[2,512,512]{2,1,0:T(8,128)(2,1)S(1)} collective-permute-done((bf16[2,512,512]{2,1,0:T(8,128)(2,1)}, bf16[2,512,512]{2,1,0:T(8,128)(2,1)S(1)}, u32[]{:S(2)}, u32[]{:S(2)}) %collective-permute-start.50) | collective-permute-done | bytes 1048608 | tf_op jit(solution)/shard_map/ppermute | solution.py:34
  627.1 4.1 collective-permute-done.55.refs_1_
  631.2 41.1 %collective-permute-done.56.refs_2_ = bf16[128,2048]{1,0:T(8,128)(2,1)} collective-permute-done((bf16[128,2048]{1,0:T(8,128)(2,1)}, bf16[128,2048]{1,0:T(8,128)(2,1)}, u32[]{:S(2)}, u32[]{:S(2)}) %collective-permute-start.56) | collective-permute-done | bytes 524320 | tf_op jit(solution)/shard_map/ppermute | solution.py:38
  684.2 3.3 collective-permute-start.61
  689.5 3.8 shard_map.267
  693.3 17.6 %collective-permute-done.61.refs_2_ = bf16[128,1024]{1,0:T(8,128)(2,1)S(1)} collective-permute-done((bf16[128,1024]{1,0:T(8,128)(2,1)}, bf16[128,1024]{1,0:T(8,128)(2,1)S(1)}, u32[]{:S(2)}, u32[]{:S(2)}) %collective-permute-start.61) | collective-permute-done | bytes 262176 | tf_op jit(solution)/shard_map/ppermute | solution.py:38
  712.3 2.6 shard_map.266
  716.1 2.7 fusion.25
  (321 shorter events, 144.8 us)
Async XLA Ops:
  7.2 81.6 %all-gather.5.cloned.1.call-start = ((), (), s32[]{:S(2)}) async-start(), calls=%async_computation.4 | async-start | bytes 4718592 | tf_op jit(solution)/shard_map/all_gather | solution.py:645
  8.0 13.0 %collective-permute-start.3 = (s32[1,128]{1,0:T(1,128)S(1)}, s32[1,128]{1,0:T(1,128)S(1)}, u32[]{:S(2)}, u32[]{:S(2)}) collective-permute-start(s32[1,128]{1,0:T(1,128)S(1)} %fusion.37), channel_id=1, source_target_pairs={{0,2},{2,0},{1,3},{3,1},{4,6},{6,4},{5,7},{7,5},{8,10},{10,8},{9,1... | collective-permute-start | bytes 1544 | tf_op jit(solution)/shard_map/ppermute | solution.py:34
  10.4 10.5 %collective-permute-start = (bf16[128,1024]{1,0:T(8,128)(2,1)}, bf16[128,1024]{1,0:T(8,128)(2,1)S(1)}, u32[]{:S(2)}, u32[]{:S(2)}) collective-permute-start(bf16[128,1024]{1,0:T(8,128)(2,1)} %get-tuple-element.318), channel_id=1, source_target_pairs={{0,8},{8,16},{16,24},{24,0},{1,9},{9,17},{17,25},{25,1},{2,10},{10... | collective-permute-start | bytes 786440 | tf_op jit(solution)/shard_map/ppermute | solution.py:38
  10.4 25.7 %collective-permute-start.1 = (bf16[128,1024]{1,0:T(8,128)(2,1)}, bf16[128,1024]{1,0:T(8,128)(2,1)S(1)}, u32[]{:S(2)}, u32[]{:S(2)}) collective-permute-start(bf16[128,1024]{1,0:T(8,128)(2,1)} %get-tuple-element.319), channel_id=1, source_target_pairs={{0,16},{8,24},{16,0},{24,8},{1,17},{9,25},{17,1},{25,9},{2,18},{10... | collective-permute-start | bytes 786440 | tf_op jit(solution)/shard_map/ppermute | solution.py:38
  12.3 23.8 %collective-permute-start.2 = (bf16[128,1024]{1,0:T(8,128)(2,1)}, bf16[128,1024]{1,0:T(8,128)(2,1)S(1)}, u32[]{:S(2)}, u32[]{:S(2)}) collective-permute-start(bf16[128,1024]{1,0:T(8,128)(2,1)} %get-tuple-element.320), channel_id=1, source_target_pairs={{0,24},{8,0},{16,8},{24,16},{1,25},{9,1},{17,9},{25,17},{2,26},{10... | collective-permute-start | bytes 786440 | tf_op jit(solution)/shard_map/ppermute | solution.py:38
  36.1 196.9 %reduce-scatter.5.cloned.1.call-start = ((), (), s32[]{:S(2)}) async-start(), calls=%async_computation.5 | async-start | bytes 4718592 | tf_op jit(solution)/shard_map/reduce_scatter | solution.py:642
  40.5 6.8 collective-permute-start.10
  45.2 25.5 %collective-permute-start.8 = (bf16[1024,512]{1,0:T(8,128)(2,1)}, bf16[1024,512]{1,0:T(8,128)(2,1)S(1)}, u32[]{:S(2)}, u32[]{:S(2)}) collective-permute-start(bf16[1024,512]{1,0:T(8,128)(2,1)} %shard_map.242.refs_0_), channel_id=1, source_target_pairs={{0,4},{4,0},{1,5},{5,1},{2,6},{6,2},{3,7},{7,3},{8,12},{12,8},{9,1... | collective-permute-start | bytes 3145736 | tf_op jit(solution)/shard_map/ppermute | solution.py:34
  46.7 25.2 %collective-permute-start.9 = (bf16[1024,512]{1,0:T(8,128)(2,1)}, bf16[1024,512]{1,0:T(8,128)(2,1)S(1)}, u32[]{:S(2)}, u32[]{:S(2)}) collective-permute-start(bf16[1024,512]{1,0:T(8,128)(2,1)} %shard_map.242.refs_0_), channel_id=1, source_target_pairs={{0,1},{1,0},{2,3},{3,2},{4,5},{5,4},{6,7},{7,6},{8,9},{9,8},{10,11... | collective-permute-start | bytes 3145736 | tf_op jit(solution)/shard_map/ppermute | solution.py:34
  47.9 4.3 collective-permute-start.4
  47.9 5.8 collective-permute-start.5
  49.1 5.5 collective-permute-start.6
  72.0 13.1 %collective-permute-start.11 = (bf16[512,512]{1,0:T(8,128)(2,1)S(1)}, bf16[512,512]{1,0:T(8,128)(2,1)S(1)}, u32[]{:S(2)}, u32[]{:S(2)}) collective-permute-start(bf16[512,512]{1,0:T(8,128)(2,1)S(1)} %slice.100), channel_id=1, source_target_pairs={{0,4},{4,0},{1,5},{5,1},{2,6},{6,2},{3,7},{7,3},{8,12},{12,8},{9,1... | collective-permute-start | bytes 1572872 | tf_op jit(solution)/shard_map/ppermute | solution.py:34
  72.6 12.9 %collective-permute-start.12 = (bf16[512,512]{1,0:T(8,128)(2,1)S(1)}, bf16[512,512]{1,0:T(8,128)(2,1)S(1)}, u32[]{:S(2)}, u32[]{:S(2)}) collective-permute-start(bf16[512,512]{1,0:T(8,128)(2,1)S(1)} %slice.101), channel_id=1, source_target_pairs={{0,1},{1,0},{2,3},{3,2},{4,5},{5,4},{6,7},{7,6},{8,9},{9,8},{10,11... | collective-permute-start | bytes 1572872 | tf_op jit(solution)/shard_map/ppermute | solution.py:34
  73.2 23.5 %collective-permute-start.14 = (bf16[128,1024]{1,0:T(8,128)(2,1)S(1)}, bf16[128,1024]{1,0:T(8,128)(2,1)S(1)}, u32[]{:S(2)}, u32[]{:S(2)}) collective-permute-start(bf16[128,1024]{1,0:T(8,128)(2,1)S(1)} %copy-done.59), channel_id=1, source_target_pairs={{0,8},{8,16},{16,24},{24,0},{1,9},{9,17},{17,25},{25,1},{2,10},{10... | collective-permute-start | bytes 786440 | tf_op jit(solution)/shard_map/ppermute | solution.py:38
  73.2 29.9 %collective-permute-start.15 = (bf16[128,1024]{1,0:T(8,128)(2,1)S(1)}, bf16[128,1024]{1,0:T(8,128)(2,1)S(1)}, u32[]{:S(2)}, u32[]{:S(2)}) collective-permute-start(bf16[128,1024]{1,0:T(8,128)(2,1)S(1)} %copy-done.58), channel_id=1, source_target_pairs={{0,16},{8,24},{16,0},{24,8},{1,17},{9,25},{17,1},{25,9},{2,18},{10... | collective-permute-start | bytes 786440 | tf_op jit(solution)/shard_map/ppermute | solution.py:38
  74.5 28.6 %collective-permute-start.16 = (bf16[128,1024]{1,0:T(8,128)(2,1)S(1)}, bf16[128,1024]{1,0:T(8,128)(2,1)S(1)}, u32[]{:S(2)}, u32[]{:S(2)}) collective-permute-start(bf16[128,1024]{1,0:T(8,128)(2,1)S(1)} %copy-done.57), channel_id=1, source_target_pairs={{0,24},{8,0},{16,8},{24,16},{1,25},{9,1},{17,9},{25,17},{2,26},{10... | collective-permute-start | bytes 786440 | tf_op jit(solution)/shard_map/ppermute | solution.py:38
  111.9 29.4 %collective-permute-start.20 = (bf16[1024,512]{1,0:T(8,128)(2,1)}, bf16[1024,512]{1,0:T(8,128)(2,1)S(1)}, u32[]{:S(2)}, u32[]{:S(2)}) collective-permute-start(bf16[1024,512]{1,0:T(8,128)(2,1)} %shard_map.247.refs_0_), channel_id=1, source_target_pairs={{0,4},{4,0},{1,5},{5,1},{2,6},{6,2},{3,7},{7,3},{8,12},{12,8},{9,1... | collective-permute-start | bytes 3145736 | tf_op jit(solution)/shard_map/ppermute | solution.py:34
  113.4 28.0 %collective-permute-start.21 = (bf16[1024,512]{1,0:T(8,128)(2,1)}, bf16[1024,512]{1,0:T(8,128)(2,1)S(1)}, u32[]{:S(2)}, u32[]{:S(2)}) collective-permute-start(bf16[1024,512]{1,0:T(8,128)(2,1)} %shard_map.247.refs_0_), channel_id=1, source_target_pairs={{0,1},{1,0},{2,3},{3,2},{4,5},{5,4},{6,7},{7,6},{8,9},{9,8},{10,11... | collective-permute-start | bytes 3145736 | tf_op jit(solution)/shard_map/ppermute | solution.py:34
  116.9 3.7 collective-permute-start.18
  120.6 4.5 collective-permute-start.19
  125.7 17.0 %collective-permute-start.24 = (bf16[128,2048]{1,0:T(8,128)(2,1)}, bf16[128,2048]{1,0:T(8,128)(2,1)S(1)}, u32[]{:S(2)}, u32[]{:S(2)}) collective-permute-start(bf16[128,2048]{1,0:T(8,128)(2,1)} %get-tuple-element.407), channel_id=1, source_target_pairs={{0,8},{8,16},{16,24},{24,0},{1,9},{9,17},{17,25},{25,1},{2,10},{10... | collective-permute-start | bytes 1572872 | tf_op jit(solution)/shard_map/ppermute | solution.py:38
  129.8 43.3 %collective-permute-start.25 = (bf16[128,2048]{1,0:T(8,128)(2,1)}, bf16[128,2048]{1,0:T(8,128)(2,1)S(1)}, u32[]{:S(2)}, u32[]{:S(2)}) collective-permute-start(bf16[128,2048]{1,0:T(8,128)(2,1)} %get-tuple-element.408), channel_id=1, source_target_pairs={{0,16},{8,24},{16,0},{24,8},{1,17},{9,25},{17,1},{25,9},{2,18},{10... | collective-permute-start | bytes 1572872 | tf_op jit(solution)/shard_map/ppermute | solution.py:38
  129.8 43.3 %collective-permute-start.26 = (bf16[128,2048]{1,0:T(8,128)(2,1)}, bf16[128,2048]{1,0:T(8,128)(2,1)}, u32[]{:S(2)}, u32[]{:S(2)}) collective-permute-start(bf16[128,2048]{1,0:T(8,128)(2,1)} %get-tuple-element.409), channel_id=1, source_target_pairs={{0,24},{8,0},{16,8},{24,16},{1,25},{9,1},{17,9},{25,17},{2,26},{10... | collective-permute-start | bytes 1572872 | tf_op jit(solution)/shard_map/ppermute | solution.py:38
  141.4 31.7 %collective-permute-start.22 = (bf16[512,512]{1,0:T(8,128)(2,1)S(1)}, bf16[512,512]{1,0:T(8,128)(2,1)S(1)}, u32[]{:S(2)}, u32[]{:S(2)}) collective-permute-start(bf16[512,512]{1,0:T(8,128)(2,1)S(1)} %slice.102), channel_id=1, source_target_pairs={{0,4},{4,0},{1,5},{5,1},{2,6},{6,2},{3,7},{7,3},{8,12},{12,8},{9,1... | collective-permute-start | bytes 1572872 | tf_op jit(solution)/shard_map/ppermute | solution.py:34
  142.1 31.8 %collective-permute-start.23 = (bf16[512,512]{1,0:T(8,128)(2,1)S(1)}, bf16[512,512]{1,0:T(8,128)(2,1)S(1)}, u32[]{:S(2)}, u32[]{:S(2)}) collective-permute-start(bf16[512,512]{1,0:T(8,128)(2,1)S(1)} %slice.103), channel_id=1, source_target_pairs={{0,1},{1,0},{2,3},{3,2},{4,5},{5,4},{6,7},{7,6},{8,9},{9,8},{10,11... | collective-permute-start | bytes 1572872 | tf_op jit(solution)/shard_map/ppermute | solution.py:34
  174.8 107.7 %all-gather.7.cloned.1.call-start = ((), (), s32[]{:S(2)}) async-start(), calls=%async_computation.6 | async-start | bytes 4718592 | tf_op jit(solution)/shard_map/all_gather | solution.py:645
  184.7 47.9 %collective-permute-start.28 = (bf16[1024,1024]{1,0:T(8,128)(2,1)}, bf16[1024,1024]{1,0:T(8,128)(2,1)S(1)}, u32[]{:S(2)}, u32[]{:S(2)}) collective-permute-start(bf16[1024,1024]{1,0:T(8,128)(2,1)} %shard_map.249.refs_0_), channel_id=1, source_target_pairs={{0,4},{4,0},{1,5},{5,1},{2,6},{6,2},{3,7},{7,3},{8,12},{12,8},{9,1... | collective-permute-start | bytes 6291464 | tf_op jit(solution)/shard_map/ppermute | solution.py:34
  185.3 47.7 %collective-permute-start.29 = (bf16[1024,1024]{1,0:T(8,128)(2,1)}, bf16[1024,1024]{1,0:T(8,128)(2,1)}, u32[]{:S(2)}, u32[]{:S(2)}) collective-permute-start(bf16[1024,1024]{1,0:T(8,128)(2,1)} %shard_map.249.refs_0_), channel_id=1, source_target_pairs={{0,1},{1,0},{2,3},{3,2},{4,5},{5,4},{6,7},{7,6},{8,9},{9,8},{10,11... | collective-permute-start | bytes 6291464 | tf_op jit(solution)/shard_map/ppermute | solution.py:34
  236.9 115.7 %reduce-scatter.7.cloned.1.call-start = ((), (), s32[]{:S(2)}) async-start(), calls=%async_computation.7 | async-start | bytes 4718592 | tf_op jit(solution)/shard_map/reduce_scatter | solution.py:642
  239.3 24.4 %collective-permute-start.30 = (bf16[512,1024]{1,0:T(8,128)(2,1)}, bf16[512,1024]{1,0:T(8,128)(2,1)}, u32[]{:S(2)}, u32[]{:S(2)}) collective-permute-start(bf16[512,1024]{1,0:T(8,128)(2,1)} %slice.104), channel_id=1, source_target_pairs={{0,4},{4,0},{1,5},{5,1},{2,6},{6,2},{3,7},{7,3},{8,12},{12,8},{9,1... | collective-permute-start | bytes 3145736 | tf_op jit(solution)/shard_map/ppermute | solution.py:34
  241.8 24.1 %collective-permute-start.31 = (bf16[512,1024]{1,0:T(8,128)(2,1)}, bf16[512,1024]{1,0:T(8,128)(2,1)}, u32[]{:S(2)}, u32[]{:S(2)}) collective-permute-start(bf16[512,1024]{1,0:T(8,128)(2,1)} %slice.105), channel_id=1, source_target_pairs={{0,1},{1,0},{2,3},{3,2},{4,5},{5,4},{6,7},{7,6},{8,9},{9,8},{10,11... | collective-permute-start | bytes 3145736 | tf_op jit(solution)/shard_map/ppermute | solution.py:34
  304.2 99.4 %all-gather.9.cloned.1.call-start = ((), (), s32[]{:S(2)}) async-start(), calls=%async_computation.8 | async-start | bytes 4718592 | tf_op jit(solution)/shard_map/all_gather | solution.py:645
  357.7 116.8 %reduce-scatter.9.cloned.1.call-start = ((), (), s32[]{:S(2)}) async-start(), calls=%async_computation.9 | async-start | bytes 4718592 | tf_op jit(solution)/shard_map/reduce_scatter | solution.py:642
  359.8 14.0 %collective-permute-start.32 = (bf16[128,2048]{1,0:T(8,128)(2,1)}, bf16[128,2048]{1,0:T(8,128)(2,1)S(1)}, u32[]{:S(2)}, u32[]{:S(2)}) collective-permute-start(bf16[128,2048]{1,0:T(8,128)(2,1)} %shard_map.254), channel_id=1, source_target_pairs={{0,1},{1,0},{2,3},{3,2},{4,5},{5,4},{6,7},{7,6},{8,9},{9,8},{10,11... | collective-permute-start | bytes 1572872 | tf_op jit(solution)/shard_map/ppermute | solution.py:34
  426.0 97.0 %all-gather.11.cloned.1.call-start = ((), (), s32[]{:S(2)}) async-start(), calls=%async_computation.10 | async-start | bytes 4718592 | tf_op jit(solution)/shard_map/all_gather | solution.py:645
  435.0 25.7 %collective-permute-start.33 = (bf16[2,512,512]{2,1,0:T(8,128)(2,1)}, bf16[2,512,512]{2,1,0:T(8,128)(2,1)}, u32[]{:S(2)}, u32[]{:S(2)}) collective-permute-start(bf16[2,512,512]{2,1,0:T(8,128)(2,1)} %get-tuple-element.468), channel_id=1, source_target_pairs={{0,4},{4,0},{1,5},{5,1},{2,6},{6,2},{3,7},{7,3},{8,12},{12,8},{9,1... | collective-permute-start | bytes 3145736 | tf_op jit(solution)/shard_map/ppermute | solution.py:34
  436.5 25.3 %collective-permute-start.34 = (bf16[2,512,512]{2,1,0:T(8,128)(2,1)}, bf16[2,512,512]{2,1,0:T(8,128)(2,1)}, u32[]{:S(2)}, u32[]{:S(2)}) collective-permute-start(bf16[2,512,512]{2,1,0:T(8,128)(2,1)} %get-tuple-element.469), channel_id=1, source_target_pairs={{0,1},{1,0},{2,3},{3,2},{4,5},{5,4},{6,7},{7,6},{8,9},{9,8},{10,11... | collective-permute-start | bytes 3145736 | tf_op jit(solution)/shard_map/ppermute | solution.py:34
  477.2 202.4 %reduce-scatter.11.cloned.1.call-start = ((), (), s32[]{:S(2)}) async-start(), calls=%async_computation.11 | async-start | bytes 4718592 | tf_op jit(solution)/shard_map/reduce_scatter | solution.py:642
  478.6 13.7 %collective-permute-start.36 = (bf16[512,512]{1,0:T(8,128)(2,1)S(1)}, bf16[512,512]{1,0:T(8,128)(2,1)S(1)}, u32[]{:S(2)}, u32[]{:S(2)}) collective-permute-start(bf16[512,512]{1,0:T(8,128)(2,1)S(1)} %fusion.34), channel_id=1, source_target_pairs={{0,4},{4,0},{1,5},{5,1},{2,6},{6,2},{3,7},{7,3},{8,12},{12,8},{9,1... | collective-permute-start | bytes 1572872 | tf_op jit(solution)/shard_map/ppermute | solution.py:34
  480.5 14.2 %collective-permute-start.35 = (bf16[512,512]{1,0:T(8,128)(2,1)S(1)}, bf16[512,512]{1,0:T(8,128)(2,1)S(1)}, u32[]{:S(2)}, u32[]{:S(2)}) collective-permute-start(bf16[512,512]{1,0:T(8,128)(2,1)S(1)} %fusion.35), channel_id=1, source_target_pairs={{0,1},{1,0},{2,3},{3,2},{4,5},{5,4},{6,7},{7,6},{8,9},{9,8},{10,11... | collective-permute-start | bytes 1572872 | tf_op jit(solution)/shard_map/ppermute | solution.py:34
  494.7 48.6 %collective-permute-start.41 = (bf16[2,512,1024]{2,1,0:T(8,128)(2,1)}, bf16[2,512,1024]{2,1,0:T(8,128)(2,1)}, u32[]{:S(2)}, u32[]{:S(2)}) collective-permute-start(bf16[2,512,1024]{2,1,0:T(8,128)(2,1)} %get-tuple-element.524), channel_id=1, source_target_pairs={{0,4},{4,0},{1,5},{5,1},{2,6},{6,2},{3,7},{7,3},{8,12},{12,8},{9,1... | collective-permute-start | bytes 6291464 | tf_op jit(solution)/shard_map/ppermute | solution.py:34
  495.3 48.1 %collective-permute-start.42 = (bf16[2,512,1024]{2,1,0:T(8,128)(2,1)}, bf16[2,512,1024]{2,1,0:T(8,128)(2,1)}, u32[]{:S(2)}, u32[]{:S(2)}) collective-permute-start(bf16[2,512,1024]{2,1,0:T(8,128)(2,1)} %get-tuple-element.525), channel_id=1, source_target_pairs={{0,1},{1,0},{2,3},{3,2},{4,5},{5,4},{6,7},{7,6},{8,9},{9,8},{10,11... | collective-permute-start | bytes 6291464 | tf_op jit(solution)/shard_map/ppermute | solution.py:34
  523.0 20.3 %collective-permute-start.38 = (bf16[128,1024]{1,0:T(8,128)(2,1)}, bf16[128,1024]{1,0:T(8,128)(2,1)S(1)}, u32[]{:S(2)}, u32[]{:S(2)}) collective-permute-start(bf16[128,1024]{1,0:T(8,128)(2,1)} %get-tuple-element.521), channel_id=1, source_target_pairs={{0,8},{8,16},{16,24},{24,0},{1,9},{9,17},{17,25},{25,1},{2,10},{10... | collective-permute-start | bytes 786440 | tf_op jit(solution)/shard_map/ppermute | solution.py:38
  525.7 23.6 %collective-permute-start.39 = (bf16[128,1024]{1,0:T(8,128)(2,1)}, bf16[128,1024]{1,0:T(8,128)(2,1)S(1)}, u32[]{:S(2)}, u32[]{:S(2)}) collective-permute-start(bf16[128,1024]{1,0:T(8,128)(2,1)} %get-tuple-element.522), channel_id=1, source_target_pairs={{0,16},{8,24},{16,0},{24,8},{1,17},{9,25},{17,1},{25,9},{2,18},{10... | collective-permute-start | bytes 786440 | tf_op jit(solution)/shard_map/ppermute | solution.py:38
  525.8 23.5 %collective-permute-start.40 = (bf16[128,1024]{1,0:T(8,128)(2,1)}, bf16[128,1024]{1,0:T(8,128)(2,1)S(1)}, u32[]{:S(2)}, u32[]{:S(2)}) collective-permute-start(bf16[128,1024]{1,0:T(8,128)(2,1)} %get-tuple-element.523), channel_id=1, source_target_pairs={{0,24},{8,0},{16,8},{24,16},{1,25},{9,1},{17,9},{25,17},{2,26},{10... | collective-permute-start | bytes 786440 | tf_op jit(solution)/shard_map/ppermute | solution.py:38
  552.1 29.2 %collective-permute-start.47 = (bf16[512,1024]{1,0:T(8,128)(2,1)}, bf16[512,1024]{1,0:T(8,128)(2,1)S(1)}, u32[]{:S(2)}, u32[]{:S(2)}) collective-permute-start(bf16[512,1024]{1,0:T(8,128)(2,1)} %fusion.4), channel_id=1, source_target_pairs={{0,4},{4,0},{1,5},{5,1},{2,6},{6,2},{3,7},{7,3},{8,12},{12,8},{9,1... | collective-permute-start | bytes 3145736 | tf_op jit(solution)/shard_map/ppermute | solution.py:34
  556.2 25.1 %collective-permute-start.46 = (bf16[512,1024]{1,0:T(8,128)(2,1)}, bf16[512,1024]{1,0:T(8,128)(2,1)S(1)}, u32[]{:S(2)}, u32[]{:S(2)}) collective-permute-start(bf16[512,1024]{1,0:T(8,128)(2,1)} %fusion.5), channel_id=1, source_target_pairs={{0,1},{1,0},{2,3},{3,2},{4,5},{5,4},{6,7},{7,6},{8,9},{9,8},{10,11... | collective-permute-start | bytes 3145736 | tf_op jit(solution)/shard_map/ppermute | solution.py:34
  559.4 4.0 collective-permute-start.44
  563.4 4.9 collective-permute-start.45
  568.3 13.0 %collective-permute-start.48 = (f32[64,128]{1,0:T(8,128)S(1)}, f32[64,128]{1,0:T(8,128)S(1)}, u32[]{:S(2)}, u32[]{:S(2)}) collective-permute-start(f32[64,128]{1,0:T(8,128)S(1)} %slice.133), channel_id=1, source_target_pairs={{0,1},{1,0},{2,3},{3,2},{4,5},{5,4},{6,7},{7,6},{8,9},{9,8},{10,11... | collective-permute-start | bytes 98312 | tf_op jit(solution)/shard_map/ppermute | solution.py:34
  586.3 14.3 %collective-permute-start.52 = (bf16[512,1024]{1,0:T(8,128)(2,1)}, bf16[512,1024]{1,0:T(8,128)(2,1)}, u32[]{:S(2)}, u32[]{:S(2)}) collective-permute-start(bf16[512,1024]{1,0:T(8,128)(2,1)} %get-tuple-element.628), channel_id=1, source_target_pairs={{0,2},{2,0},{1,3},{3,1},{4,6},{6,4},{5,7},{7,5},{8,10},{10,8},{9,1... | collective-permute-start | bytes 3145736 | tf_op jit(solution)/shard_map/ppermute | solution.py:34
  596.3 25.9 %collective-permute-start.50 = (bf16[2,512,512]{2,1,0:T(8,128)(2,1)}, bf16[2,512,512]{2,1,0:T(8,128)(2,1)S(1)}, u32[]{:S(2)}, u32[]{:S(2)}) collective-permute-start(bf16[2,512,512]{2,1,0:T(8,128)(2,1)} %get-tuple-element.557), channel_id=1, source_target_pairs={{0,4},{4,0},{1,5},{5,1},{2,6},{6,2},{3,7},{7,3},{8,12},{12,8},{9,1... | collective-permute-start | bytes 3145736 | tf_op jit(solution)/shard_map/ppermute | solution.py:34
  596.5 25.9 %collective-permute-start.51 = (bf16[2,512,512]{2,1,0:T(8,128)(2,1)}, bf16[2,512,512]{2,1,0:T(8,128)(2,1)}, u32[]{:S(2)}, u32[]{:S(2)}) collective-permute-start(bf16[2,512,512]{2,1,0:T(8,128)(2,1)} %get-tuple-element.558), channel_id=1, source_target_pairs={{0,1},{1,0},{2,3},{3,2},{4,5},{5,4},{6,7},{7,6},{8,9},{9,8},{10,11... | collective-permute-start | bytes 3145736 | tf_op jit(solution)/shard_map/ppermute | solution.py:34
  603.7 27.5 %collective-permute-start.55 = (bf16[128,2048]{1,0:T(8,128)(2,1)}, bf16[128,2048]{1,0:T(8,128)(2,1)}, u32[]{:S(2)}, u32[]{:S(2)}) collective-permute-start(bf16[128,2048]{1,0:T(8,128)(2,1)} %get-tuple-element.580), channel_id=1, source_target_pairs={{0,8},{8,16},{16,24},{24,0},{1,9},{9,17},{17,25},{25,1},{2,10},{10... | collective-permute-start | bytes 1572872 | tf_op jit(solution)/shard_map/ppermute | solution.py:38
  603.7 68.6 %collective-permute-start.56 = (bf16[128,2048]{1,0:T(8,128)(2,1)}, bf16[128,2048]{1,0:T(8,128)(2,1)}, u32[]{:S(2)}, u32[]{:S(2)}) collective-permute-start(bf16[128,2048]{1,0:T(8,128)(2,1)} %get-tuple-element.581), channel_id=1, source_target_pairs={{0,16},{8,24},{16,0},{24,8},{1,17},{9,25},{17,1},{25,9},{2,18},{10... | collective-permute-start | bytes 1572872 | tf_op jit(solution)/shard_map/ppermute | solution.py:38
  605.9 66.4 %collective-permute-start.57 = (bf16[128,2048]{1,0:T(8,128)(2,1)}, bf16[128,2048]{1,0:T(8,128)(2,1)}, u32[]{:S(2)}, u32[]{:S(2)}) collective-permute-start(bf16[128,2048]{1,0:T(8,128)(2,1)} %get-tuple-element.582), channel_id=1, source_target_pairs={{0,24},{8,0},{16,8},{24,16},{1,25},{9,1},{17,9},{25,17},{2,26},{10... | collective-permute-start | bytes 1572872 | tf_op jit(solution)/shard_map/ppermute | solution.py:38
  623.7 48.6 %collective-permute-start.54 = (bf16[512,512]{1,0:T(8,128)(2,1)S(1)}, bf16[512,512]{1,0:T(8,128)(2,1)S(1)}, u32[]{:S(2)}, u32[]{:S(2)}) collective-permute-start(bf16[512,512]{1,0:T(8,128)(2,1)S(1)} %fusion.29), channel_id=1, source_target_pairs={{0,4},{4,0},{1,5},{5,1},{2,6},{6,2},{3,7},{7,3},{8,12},{12,8},{9,1... | collective-permute-start | bytes 1572872 | tf_op jit(solution)/shard_map/ppermute | solution.py:34
  625.5 46.8 %collective-permute-start.53 = (bf16[512,512]{1,0:T(8,128)(2,1)S(1)}, bf16[512,512]{1,0:T(8,128)(2,1)S(1)}, u32[]{:S(2)}, u32[]{:S(2)}) collective-permute-start(bf16[512,512]{1,0:T(8,128)(2,1)S(1)} %fusion.30), channel_id=1, source_target_pairs={{0,1},{1,0},{2,3},{3,2},{4,5},{5,4},{6,7},{7,6},{8,9},{9,8},{10,11... | collective-permute-start | bytes 1572872 | tf_op jit(solution)/shard_map/ppermute | solution.py:34
  674.6 4.9 collective-permute-start.49
  683.6 31.4 %collective-permute-start.59 = (bf16[128,2048]{1,0:T(8,128)(2,1)}, bf16[128,2048]{1,0:T(8,128)(2,1)S(1)}, u32[]{:S(2)}, u32[]{:S(2)}) collective-permute-start(bf16[128,2048]{1,0:T(8,128)(2,1)} %shard_map.265), channel_id=1, source_target_pairs={{0,1},{1,0},{2,3},{3,2},{4,5},{5,4},{6,7},{7,6},{8,9},{9,8},{10,11... | collective-permute-start | bytes 1572872 | tf_op jit(solution)/shard_map/ppermute | solution.py:34
  684.2 9.1 %collective-permute-start.60 = (bf16[128,1024]{1,0:T(8,128)(2,1)}, bf16[128,1024]{1,0:T(8,128)(2,1)S(1)}, u32[]{:S(2)}, u32[]{:S(2)}) collective-permute-start(bf16[128,1024]{1,0:T(8,128)(2,1)} %get-tuple-element.598), channel_id=1, source_target_pairs={{0,8},{8,16},{16,24},{24,0},{1,9},{9,17},{17,25},{25,1},{2,10},{10... | collective-permute-start | bytes 786440 | tf_op jit(solution)/shard_map/ppermute | solution.py:38
  684.2 26.7 %collective-permute-start.61 = (bf16[128,1024]{1,0:T(8,128)(2,1)}, bf16[128,1024]{1,0:T(8,128)(2,1)S(1)}, u32[]{:S(2)}, u32[]{:S(2)}) collective-permute-start(bf16[128,1024]{1,0:T(8,128)(2,1)} %get-tuple-element.599), channel_id=1, source_target_pairs={{0,16},{8,24},{16,0},{24,8},{1,17},{9,25},{17,1},{25,9},{2,18},{10... | collective-permute-start | bytes 786440 | tf_op jit(solution)/shard_map/ppermute | solution.py:38
  687.5 23.4 %collective-permute-start.62 = (bf16[128,1024]{1,0:T(8,128)(2,1)}, bf16[128,1024]{1,0:T(8,128)(2,1)S(1)}, u32[]{:S(2)}, u32[]{:S(2)}) collective-permute-start(bf16[128,1024]{1,0:T(8,128)(2,1)} %get-tuple-element.600), channel_id=1, source_target_pairs={{0,24},{8,0},{16,8},{24,16},{1,25},{9,1},{17,9},{25,17},{2,26},{10... | collective-permute-start | bytes 786440 | tf_op jit(solution)/shard_map/ppermute | solution.py:38
  (68 other events, 956.6 us)
Sparse Core Ops, SparseCore 0:
  36.2 50.3 all-gather.4
  174.9 46.9 reduce-scatter.4
  237.0 45.3 all-gather.6
  304.4 48.1 reduce-scatter.6
  357.8 45.7 all-gather.8
  426.1 48.3 reduce-scatter.8
  477.3 45.6 all-gather.10
  581.5 83.2 reduce-scatter.10

commit v4 on v3

--- a/solution.py
+++ b/solution.py
@@ -841,17 +841,20 @@
     [down_grad] = step(unpack(down, place.g, 1))
     attn_came = step(attn_came)
     attn_more = place.narrow_next(attn, attn_came)
+    input_part = step(input_part)
+    own_grad = place.to_global((hidden_grad + input_part.astype(F32)).astype(BF16))
+    own_grad_x = swap(step(own_grad), "x")
     feed = step(feed)
     attn_more = step(attn_more)
-    attn = step(place.unsettle(place.narrowed(attn, attn_came, attn_more)))
+    attn = place.unsettle(place.narrowed(attn, attn_came, attn_more))
+    attn, gain_q = step(attn, gain_q)
     attn = place.send(step(deal(*attn, place.g, place.c)))
-    input_part, gain_q = step(input_part, gain_q)
+    attn[1], feed, own_grad_x = step(attn[1], feed, own_grad_x)
+    gate_grad, up_grad = unpack(feed, place.g, 2)
     summed = (gain_grads + gain_q).reshape(4, D)
-    own_grad = place.to_global((hidden_grad + input_part.astype(F32)).astype(BF16))
-    own_grad_x = swap(own_grad, "x")
-    gate_grad, up_grad = unpack(feed, place.g, 2)
+    tokens_grad = ordered(place.x, own_grad, own_grad_x, 0)[:, None].astype(F32)
+    tokens_grad, gate_grad, up_grad, summed = step(tokens_grad, gate_grad, up_grad, summed)
     attn_grads = unpack(step(attn), place.g, 4)
-    tokens_grad = ordered(place.x, own_grad, step(own_grad_x), 0)[:, None].astype(F32)
     summed = summed + step.token
     half_of = lambda v: pick(v.reshape(2, -1), place.x, 0)
     return (

time: 736 us -> 732 us (level)
    ppermute x21, waiting for transfers between devices: 124 us -> 112 us  [shift(): lax.ppermute(value, 'g', [(i, (i + by) % GROUP) for i in range(GROUP)])]
    unnamed x122 -> x128, local copies, waits for them, and re-layouts: 23.5 us -> 23.1 us
  transfers between devices with their start and end apart: 71 -> 71, of which waited for: 40 -> 42; matrix products, arithmetic and copies ran while one was open for 5% -> 6% of each run, Pallas kernels for 17% -> 17%
where the time goes in v4:
time: 732 us; the launch traced here: 720 us
  waiting for transfers between devices  385 us (53%)
  Pallas kernels  133 us (18%)
  starting transfers between devices  61.3 us (8%)
  other arithmetic  50 us (7%)
  matrix products  42.6 us (6%)
  local copies, waits for them, and re-layouts  33.5 us (5%)
  between operations  15.3 us (2%)
    ppermute x38, waiting for transfers between devices, swap(): return lax.ppermute(value, axis, [(0, 1), (1, 0)])  143 us
    ppermute x21, waiting for transfers between devices, shift(): lax.ppermute(value, 'g', [(i, (i + by) % GROUP) for i in range(GROUP)])  112 us
    reduce_scatter x4, waiting for transfers between devices, team_scatter(): return lax.psum_scatter(value, TEAM, scatter_dimension=0, tiled=True)  61 us
    all_gather x4, waiting for transfers between devices, team_gather(): return lax.all_gather(value, TEAM, axis=0, tiled=True)  55.7 us
    pallas_call x4, Pallas kernels, row_call(): pl.pallas_call(kernel, grid=(rows // ROWS,), in_specs=[spec(v.shape, bloc...  44.7 us
    pallas_call x15, Pallas kernels, vmem_call(): pl.pallas_call(kernel, out_shape=shapes, in_specs=[pl.BlockSpec(memory_sp...  39.8 us
    pallas_call x3, Pallas kernels, weight_grads(): pl.pallas_call(kernel, grid=(steps,), in_specs=[pl.BlockSpec((count, step...  33.4 us
    ppermute x38, starting transfers between devices, swap(): return lax.ppermute(value, axis, [(0, 1), (1, 0)])  31.7 us
  transfers between devices with their start and end apart: 71, of which 42 were waited for; matrix products, arithmetic and copies ran while one was open for 6% of the time, Pallas kernels for 17%

profile of v4, /device:TPU:24, one launch (start us, length us, event | category | flops | bytes accessed | tf_op | source)
XLA Modules:
  0.0 720.3 jit_solution(1092470598162724407)
XLA Ops:
  8.0 2.4 shard_map.237
  17.9 3.1 shard_map.240
  21.0 15.1 %collective-permute-done.1.refs_2_ = bf16[128,1024]{1,0:T(8,128)(2,1)S(1)} collective-permute-done((bf16[128,1024]{1,0:T(8,128)(2,1)}, bf16[128,1024]{1,0:T(8,128)(2,1)S(1)}, u32[]{:S(2)}, u32[]{:S(2)}) %collective-permute-start.1) | collective-permute-done | bytes 262176 | tf_op jit(solution)/shard_map/ppermute | solution.py:38
  55.6 15.1 %collective-permute-done.8.refs_1_ = bf16[1024,512]{1,0:T(8,128)(2,1)S(1)} collective-permute-done((bf16[1024,512]{1,0:T(8,128)(2,1)}, bf16[1024,512]{1,0:T(8,128)(2,1)S(1)}, u32[]{:S(2)}, u32[]{:S(2)}) %collective-permute-start.8) | collective-permute-done | bytes 1048608 | tf_op jit(solution)/shard_map/ppermute | solution.py:34
  80.4 4.7 collective-permute-done.11.refs_3_
  88.8 7.8 %shard_map.244 = (f32[1024,768]{1,0:T(8,128)}, f32[8,2,128]{2,1,0:T(2,128)}) custom-call(bf16[1024,2048]{1,0:T(8,128)(2,1)} %all-gather.5.cloned.1.call-done.tokens.refs_0_.refs_2_, bf16[2048,768]{1,0:T(8,128)(2,1)} %copy-done.2), custom_call_target="tpu_custom_call" | custom-call | tf_op jit(solution)/shard_map/pallas_call | solution.py:370
  96.7 6.4 collective-permute-done.15.refs_2_
  116.9 3.6 collective-permute-done.18
  120.6 2.6 collective-permute-start.19
  125.7 4.0 collective-permute-start.24
  130.4 11.0 %shard_map.246 = (bf16[1024,256]{1,0:T(8,128)(2,1)}, bf16[1024,256]{1,0:T(8,128)(2,1)}, bf16[1024,256]{1,0:T(8,128)(2,1)}, bf16[1024,256]{1,0:T(8,128)(2,1)}, bf16[1024,2048]{1,0:T(8,128)(2,1)}) custom-call(f32[1024,768]{1,0:T(8,128)} %get-tuple-element.375.qkv_all, f32[8,2,128]{2,1,0:T(2,128)} %add.203.squares, f32[2,2,128]{2,1,0:T(2,128)} %pad_maximum_fusion.5.gains, ...), custom_call_target="tpu_custom_call" | custom-call | tf_op jit(solution)/shard_map/pallas_call | solution.py:370
  142.7 30.3 %collective-permute-done.25.refs_2_ = bf16[128,2048]{1,0:T(8,128)(2,1)S(1)} collective-permute-done((bf16[128,2048]{1,0:T(8,128)(2,1)}, bf16[128,2048]{1,0:T(8,128)(2,1)S(1)}, u32[]{:S(2)}, u32[]{:S(2)}) %collective-permute-start.25) | collective-permute-done | bytes 524320 | tf_op jit(solution)/shard_map/ppermute | solution.py:38
  174.8 3.0 shard_map.248
  177.8 2.9 collective-permute-done.27.second
  181.6 3.0 shard_map.249.refs_0_
  188.9 43.6 %collective-permute-done.28.refs_1_ = bf16[1024,1024]{1,0:T(8,128)(2,1)S(1)} collective-permute-done((bf16[1024,1024]{1,0:T(8,128)(2,1)}, bf16[1024,1024]{1,0:T(8,128)(2,1)S(1)}, u32[]{:S(2)}, u32[]{:S(2)}) %collective-permute-start.28) | collective-permute-done | bytes 2097184 | tf_op jit(solution)/shard_map/ppermute | solution.py:34
  234.2 2.6 fusion.39
  236.9 2.4 slice.100
  243.3 2.4 shard_map.253
  255.4 8.3 %collective-permute-done.30.refs_3_ = bf16[512,1024]{1,0:T(8,128)(2,1)} collective-permute-done((bf16[512,1024]{1,0:T(8,128)(2,1)}, bf16[512,1024]{1,0:T(8,128)(2,1)}, u32[]{:S(2)}, u32[]{:S(2)}) %collective-permute-start.30) | collective-permute-done | bytes 1048608 | tf_op jit(solution)/shard_map/ppermute | solution.py:34
  265.8 2.6 shard_map.252
  272.5 10.0 %all-gather.7.cloned.1.call-done.refs_0_.refs_1_.refs_2_.refs_3_ = bf16[1024,2048]{1,0:T(8,128)(2,1)} async-done(((bf16[128,2048]{1,0:T(8,128)(2,1)}), bf16[1024,2048]{1,0:T(8,128)(2,1)}) %all-gather.7.cloned.1.call-update) | async-done | bytes 4194320 | tf_op jit(solution)/shard_map/all_gather | solution.py:645
  282.4 7.6 %fusion.43 = f32[1024,1024]{1,0:T(8,128)S(1)} fusion(bf16[1024,2048]{1,0:T(8,128)(2,1)} %all-gather.7.cloned.1.call-done.refs_0_.refs_1_.refs_2_.refs_3_, bf16[2048,1024]{1,0:T(8,128)(2,1)} %copy-done.4), kind=kOutput, calls=%fused_computation.118 | convolution fusion | flops 4294967296 | bytes 12582912 | tf_op jit(solution)/shard_map/dot_general | solution.py:22
  290.1 6.5 multiply_convert_fusion.2
  298.0 6.2 convolution_convert_fusion
  304.2 48.4 %reduce-scatter.7.cloned.1.call-done = bf16[128,2048]{1,0:T(8,128)(2,1)} async-done(((bf16[1024,2048]{1,0:T(8,128)(2,1)}), bf16[128,2048]{1,0:T(8,128)(2,1)}) %reduce-scatter.7.cloned.1.call-update) | async-done | bytes 524304 | tf_op jit(solution)/shard_map/reduce_scatter | solution.py:642
  355.2 2.4 fusion.24
  360.7 13.1 %collective-permute-done.32 = bf16[128,2048]{1,0:T(8,128)(2,1)S(1)} collective-permute-done((bf16[128,2048]{1,0:T(8,128)(2,1)}, bf16[128,2048]{1,0:T(8,128)(2,1)S(1)}, u32[]{:S(2)}, u32[]{:S(2)}) %collective-permute-start.32) | collective-permute-done | bytes 524320 | tf_op jit(solution)/shard_map/ppermute | solution.py:34
  373.8 2.4 maximum_select_fusion
  376.2 27.4 %all-gather.9.cloned.1.call-done.refs_0_.refs_1_ = bf16[1024,2048]{1,0:T(8,128)(2,1)} async-done(((bf16[128,2048]{1,0:T(8,128)(2,1)}), bf16[1024,2048]{1,0:T(8,128)(2,1)}) %all-gather.9.cloned.1.call-update) | async-done | bytes 4194320 | tf_op jit(solution)/shard_map/all_gather | solution.py:645
  403.6 11.5 %multiply_convert_fusion = (bf16[1024,1024]{1,0:T(8,128)(2,1)S(1)}, bf16[1024,1024]{1,0:T(8,128)(2,1)S(1)}) fusion(f32[1024,1024]{1,0:T(8,128)} %copy-done.63, f32[1024,1024]{1,0:T(8,128)} %get-tuple-element.680, bf16[1024,2048]{1,0:T(8,128)(2,1)} %all-gather.9.cloned.1.call-done.refs_0_.refs_1_, bf16[2048,1024]{1,0:T(8,128)(2,1)} %copy-done.18), kind=kOutput, calls=%fused_computation.1 | convolution fusion | flops 4308598784 | bytes 20971520 | tf_op jit(solution)/shard_map/dot_general | solution.py:22
  415.2 4.6 fusion.44
  419.8 6.2 add_convert_fusion
  426.2 8.8 %shard_map.255 = (bf16[2,512,512]{2,1,0:T(8,128)(2,1)}, bf16[2,512,512]{2,1,0:T(8,128)(2,1)}, bf16[512,512]{1,0:T(8,128)(2,1)}, bf16[512,512]{1,0:T(8,128)(2,1)}, bf16[1024,512]{1,0:T(8,128)(2,1)}) custom-call(bf16[1024,2048]{1,0:T(8,128)(2,1)} %all-gather.9.cloned.1.call-done.refs_0_.refs_1_, ...), custom_call_target="tpu_custom_call" | custom-call | bytes 209715200 | tf_op jit(solution)/shard_map/pallas_call | solution.py:282
  438.0 14.8 %shard_map.256 = (bf16[2,512,1024]{2,1,0:T(8,128)(2,1)}, bf16[2,512,1024]{2,1,0:T(8,128)(2,1)}, bf16[512,1024]{1,0:T(8,128)(2,1)}, bf16[512,1024]{1,0:T(8,128)(2,1)}, bf16[1024,1024]{1,0:T(8,128)(2,1)}) custom-call(bf16[1024,2048]{1,0:T(8,128)(2,1)} %all-gather.7.cloned.1.call-done.refs_0_.refs_1_.refs_2_.refs_3_, ...), custom_call_target="tpu_custom_call" | custom-call | bytes 209715200 | tf_op jit(solution)/shard_map/pallas_call | solution.py:282
  452.8 7.9 %collective-permute-done.33 = bf16[2,512,512]{2,1,0:T(8,128)(2,1)} collective-permute-done((bf16[2,512,512]{2,1,0:T(8,128)(2,1)}, bf16[2,512,512]{2,1,0:T(8,128)(2,1)}, u32[]{:S(2)}, u32[]{:S(2)}) %collective-permute-start.33) | collective-permute-done | bytes 1048608 | tf_op jit(solution)/shard_map/ppermute | solution.py:34
  461.9 12.6 %reduce-scatter.9.cloned.1.call-done = bf16[128,2048]{1,0:T(8,128)(2,1)} async-done(((bf16[1024,2048]{1,0:T(8,128)(2,1)}), bf16[128,2048]{1,0:T(8,128)(2,1)}) %reduce-scatter.9.cloned.1.call-update) | async-done | bytes 524304 | tf_op jit(solution)/shard_map/reduce_scatter | solution.py:642
  482.1 10.2 %collective-permute-done.36 = bf16[512,512]{1,0:T(8,128)(2,1)S(1)} collective-permute-done((bf16[512,512]{1,0:T(8,128)(2,1)S(1)}, bf16[512,512]{1,0:T(8,128)(2,1)S(1)}, u32[]{:S(2)}, u32[]{:S(2)}) %collective-permute-start.36) | collective-permute-done | bytes 524320 | tf_op jit(solution)/shard_map/ppermute | solution.py:34
  492.3 2.4 collective-permute-done.35
  496.8 2.8 broadcast_select_fusion.4
  502.3 2.4 shard_map.258
  504.7 18.3 %all-gather.11.cloned.1.call-done.grads.refs_1_.refs_3_ = bf16[1024,2048]{1,0:T(8,128)(2,1)} async-done(((bf16[128,2048]{1,0:T(8,128)(2,1)}), bf16[1024,2048]{1,0:T(8,128)(2,1)}) %all-gather.11.cloned.1.call-update) | async-done | bytes 4194320 | tf_op jit(solution)/shard_map/all_gather | solution.py:645
  523.0 2.7 collective-permute-start.38
  526.3 17.0 %shard_map.259 = (f32[1024,512]{1,0:T(8,128)}, bf16[1024,256]{1,0:T(8,128)(2,1)}, f32[8,2,128]{2,1,0:T(2,128)}, f32[2,2,128]{2,1,0:T(2,128)}) custom-call(bf16[1024,2048]{1,0:T(8,128)(2,1)} %all-gather.11.cloned.1.call-done.grads.refs_1_.refs_3_, bf16[2048,256]{1,0:T(8,128)(2,1)} %copy-done.6, bf16[1024,256]{1,0:T(8,128)(2,1)} %get-tuple-element.525.query_all, ...), custom_call_target="tpu_custom_call" | custom-call | tf_op jit(solution)/shard_map/pallas_call | solution.py:370
  543.4 6.0 collective-permute-done.39.refs_2_
  549.4 2.8 fusion.4
  553.6 2.6 fusion.5
  559.4 4.0 collective-permute-done.44
  565.2 3.1 collective-permute-done.45
  569.5 8.9 %shard_map.260 = (bf16[1024,768]{1,0:T(8,128)(2,1)}, bf16[1024,2048]{1,0:T(8,128)(2,1)}) custom-call(f32[1024,512]{1,0:T(8,128)} %get-tuple-element.539.weighted_all, f32[1024,768]{1,0:T(8,128)} %get-tuple-element.375.qkv_all, f32[8,2,128]{2,1,0:T(2,128)} %add.203.squares, f32[8,2,128]{2,1,0:T(2,128)} %bitcast.139, ...), custom_call_target="tpu_custom_call" | custom-call | tf_op jit(solution)/shard_map/pallas_call | solution.py:370
  578.5 2.9 collective-permute-done.48
  581.4 5.0 broadcast_select_fusion
  586.4 9.9 %shard_map.261 = (bf16[2,512,512]{2,1,0:T(8,128)(2,1)}, bf16[2,512,512]{2,1,0:T(8,128)(2,1)}, bf16[512,512]{1,0:T(8,128)(2,1)}, bf16[512,512]{1,0:T(8,128)(2,1)}, bf16[1024,512]{1,0:T(8,128)(2,1)}) custom-call(bf16[1024,2048]{1,0:T(8,128)(2,1)} %all-gather.5.cloned.1.call-done.tokens.refs_0_.refs_2_, ...), custom_call_target="tpu_custom_call" | custom-call | bytes 209715200 | tf_op jit(solution)/shard_map/pallas_call | solution.py:282
  598.0 2.7 shard_map.262
  601.6 3.1 shard_map.263
  604.8 17.4 %collective-permute-done.49 = bf16[2,512,512]{2,1,0:T(8,128)(2,1)S(1)} collective-permute-done((bf16[2,512,512]{2,1,0:T(8,128)(2,1)}, bf16[2,512,512]{2,1,0:T(8,128)(2,1)S(1)}, u32[]{:S(2)}, u32[]{:S(2)}) %collective-permute-start.49) | collective-permute-done | bytes 1048608 | tf_op jit(solution)/shard_map/ppermute | solution.py:34
  635.9 3.3 collective-permute-done.54.refs_1_
  639.2 33.7 %collective-permute-done.55.refs_2_ = bf16[128,2048]{1,0:T(8,128)(2,1)} collective-permute-done((bf16[128,2048]{1,0:T(8,128)(2,1)}, bf16[128,2048]{1,0:T(8,128)(2,1)}, u32[]{:S(2)}, u32[]{:S(2)}) %collective-permute-start.55) | collective-permute-done | bytes 524320 | tf_op jit(solution)/shard_map/ppermute | solution.py:38
  672.9 2.8 broadcast_select_fusion.2
  678.7 2.4 collective-permute-done.58
  690.1 2.6 collective-permute-done.59.refs_1_
  692.7 3.9 shard_map.266
  698.1 10.9 %collective-permute-done.61.refs_2_ = bf16[128,1024]{1,0:T(8,128)(2,1)S(1)} collective-permute-done((bf16[128,1024]{1,0:T(8,128)(2,1)}, bf16[128,1024]{1,0:T(8,128)(2,1)S(1)}, u32[]{:S(2)}, u32[]{:S(2)}) %collective-permute-start.61) | collective-permute-done | bytes 262176 | tf_op jit(solution)/shard_map/ppermute | solution.py:38
  710.4 2.7 shard_map.267
  (329 shorter events, 151.1 us)
Async XLA Ops:
  7.2 81.6 %all-gather.5.cloned.1.call-start = ((), (), s32[]{:S(2)}) async-start(), calls=%async_computation.4 | async-start | bytes 4718592 | tf_op jit(solution)/shard_map/all_gather | solution.py:645
  8.0 13.0 %collective-permute-start.3 = (s32[1,128]{1,0:T(1,128)S(1)}, s32[1,128]{1,0:T(1,128)S(1)}, u32[]{:S(2)}, u32[]{:S(2)}) collective-permute-start(s32[1,128]{1,0:T(1,128)S(1)} %fusion.37), channel_id=1, source_target_pairs={{0,2},{2,0},{1,3},{3,1},{4,6},{6,4},{5,7},{7,5},{8,10},{10,8},{9,1... | collective-permute-start | bytes 1544 | tf_op jit(solution)/shard_map/ppermute | solution.py:34
  10.4 10.6 %collective-permute-start = (bf16[128,1024]{1,0:T(8,128)(2,1)}, bf16[128,1024]{1,0:T(8,128)(2,1)S(1)}, u32[]{:S(2)}, u32[]{:S(2)}) collective-permute-start(bf16[128,1024]{1,0:T(8,128)(2,1)} %get-tuple-element.330), channel_id=1, source_target_pairs={{0,8},{8,16},{16,24},{24,0},{1,9},{9,17},{17,25},{25,1},{2,10},{10... | collective-permute-start | bytes 786440 | tf_op jit(solution)/shard_map/ppermute | solution.py:38
  10.4 25.7 %collective-permute-start.1 = (bf16[128,1024]{1,0:T(8,128)(2,1)}, bf16[128,1024]{1,0:T(8,128)(2,1)S(1)}, u32[]{:S(2)}, u32[]{:S(2)}) collective-permute-start(bf16[128,1024]{1,0:T(8,128)(2,1)} %get-tuple-element.331), channel_id=1, source_target_pairs={{0,16},{8,24},{16,0},{24,8},{1,17},{9,25},{17,1},{25,9},{2,18},{10... | collective-permute-start | bytes 786440 | tf_op jit(solution)/shard_map/ppermute | solution.py:38
  12.3 23.8 %collective-permute-start.2 = (bf16[128,1024]{1,0:T(8,128)(2,1)}, bf16[128,1024]{1,0:T(8,128)(2,1)S(1)}, u32[]{:S(2)}, u32[]{:S(2)}) collective-permute-start(bf16[128,1024]{1,0:T(8,128)(2,1)} %get-tuple-element.332), channel_id=1, source_target_pairs={{0,24},{8,0},{16,8},{24,16},{1,25},{9,1},{17,9},{25,17},{2,26},{10... | collective-permute-start | bytes 786440 | tf_op jit(solution)/shard_map/ppermute | solution.py:38
  36.1 196.9 %reduce-scatter.5.cloned.1.call-start = ((), (), s32[]{:S(2)}) async-start(), calls=%async_computation.5 | async-start | bytes 4718592 | tf_op jit(solution)/shard_map/reduce_scatter | solution.py:642
  40.5 6.8 collective-permute-start.10
  45.2 25.5 %collective-permute-start.8 = (bf16[1024,512]{1,0:T(8,128)(2,1)}, bf16[1024,512]{1,0:T(8,128)(2,1)S(1)}, u32[]{:S(2)}, u32[]{:S(2)}) collective-permute-start(bf16[1024,512]{1,0:T(8,128)(2,1)} %shard_map.242.refs_0_), channel_id=1, source_target_pairs={{0,4},{4,0},{1,5},{5,1},{2,6},{6,2},{3,7},{7,3},{8,12},{12,8},{9,1... | collective-permute-start | bytes 3145736 | tf_op jit(solution)/shard_map/ppermute | solution.py:34
  46.7 25.2 %collective-permute-start.9 = (bf16[1024,512]{1,0:T(8,128)(2,1)}, bf16[1024,512]{1,0:T(8,128)(2,1)S(1)}, u32[]{:S(2)}, u32[]{:S(2)}) collective-permute-start(bf16[1024,512]{1,0:T(8,128)(2,1)} %shard_map.242.refs_0_), channel_id=1, source_target_pairs={{0,1},{1,0},{2,3},{3,2},{4,5},{5,4},{6,7},{7,6},{8,9},{9,8},{10,11... | collective-permute-start | bytes 3145736 | tf_op jit(solution)/shard_map/ppermute | solution.py:34
  47.9 4.3 collective-permute-start.4
  47.9 5.8 collective-permute-start.5
  49.1 5.5 collective-permute-start.6
  72.0 13.1 %collective-permute-start.11 = (bf16[512,512]{1,0:T(8,128)(2,1)S(1)}, bf16[512,512]{1,0:T(8,128)(2,1)S(1)}, u32[]{:S(2)}, u32[]{:S(2)}) collective-permute-start(bf16[512,512]{1,0:T(8,128)(2,1)S(1)} %slice.96), channel_id=1, source_target_pairs={{0,4},{4,0},{1,5},{5,1},{2,6},{6,2},{3,7},{7,3},{8,12},{12,8},{9,1... | collective-permute-start | bytes 1572872 | tf_op jit(solution)/shard_map/ppermute | solution.py:34
  72.6 12.9 %collective-permute-start.12 = (bf16[512,512]{1,0:T(8,128)(2,1)S(1)}, bf16[512,512]{1,0:T(8,128)(2,1)S(1)}, u32[]{:S(2)}, u32[]{:S(2)}) collective-permute-start(bf16[512,512]{1,0:T(8,128)(2,1)S(1)} %slice.97), channel_id=1, source_target_pairs={{0,1},{1,0},{2,3},{3,2},{4,5},{5,4},{6,7},{7,6},{8,9},{9,8},{10,11... | collective-permute-start | bytes 1572872 | tf_op jit(solution)/shard_map/ppermute | solution.py:34
  73.2 23.5 %collective-permute-start.14 = (bf16[128,1024]{1,0:T(8,128)(2,1)S(1)}, bf16[128,1024]{1,0:T(8,128)(2,1)S(1)}, u32[]{:S(2)}, u32[]{:S(2)}) collective-permute-start(bf16[128,1024]{1,0:T(8,128)(2,1)S(1)} %copy-done.62), channel_id=1, source_target_pairs={{0,8},{8,16},{16,24},{24,0},{1,9},{9,17},{17,25},{25,1},{2,10},{10... | collective-permute-start | bytes 786440 | tf_op jit(solution)/shard_map/ppermute | solution.py:38
  73.2 29.9 %collective-permute-start.15 = (bf16[128,1024]{1,0:T(8,128)(2,1)S(1)}, bf16[128,1024]{1,0:T(8,128)(2,1)S(1)}, u32[]{:S(2)}, u32[]{:S(2)}) collective-permute-start(bf16[128,1024]{1,0:T(8,128)(2,1)S(1)} %copy-done.61), channel_id=1, source_target_pairs={{0,16},{8,24},{16,0},{24,8},{1,17},{9,25},{17,1},{25,9},{2,18},{10... | collective-permute-start | bytes 786440 | tf_op jit(solution)/shard_map/ppermute | solution.py:38
  74.5 28.6 %collective-permute-start.16 = (bf16[128,1024]{1,0:T(8,128)(2,1)S(1)}, bf16[128,1024]{1,0:T(8,128)(2,1)S(1)}, u32[]{:S(2)}, u32[]{:S(2)}) collective-permute-start(bf16[128,1024]{1,0:T(8,128)(2,1)S(1)} %copy-done.60), channel_id=1, source_target_pairs={{0,24},{8,0},{16,8},{24,16},{1,25},{9,1},{17,9},{25,17},{2,26},{10... | collective-permute-start | bytes 786440 | tf_op jit(solution)/shard_map/ppermute | solution.py:38
  111.9 29.4 %collective-permute-start.20 = (bf16[1024,512]{1,0:T(8,128)(2,1)}, bf16[1024,512]{1,0:T(8,128)(2,1)S(1)}, u32[]{:S(2)}, u32[]{:S(2)}) collective-permute-start(bf16[1024,512]{1,0:T(8,128)(2,1)} %shard_map.247.refs_0_), channel_id=1, source_target_pairs={{0,4},{4,0},{1,5},{5,1},{2,6},{6,2},{3,7},{7,3},{8,12},{12,8},{9,1... | collective-permute-start | bytes 3145736 | tf_op jit(solution)/shard_map/ppermute | solution.py:34
  113.4 27.9 %collective-permute-start.21 = (bf16[1024,512]{1,0:T(8,128)(2,1)}, bf16[1024,512]{1,0:T(8,128)(2,1)S(1)}, u32[]{:S(2)}, u32[]{:S(2)}) collective-permute-start(bf16[1024,512]{1,0:T(8,128)(2,1)} %shard_map.247.refs_0_), channel_id=1, source_target_pairs={{0,1},{1,0},{2,3},{3,2},{4,5},{5,4},{6,7},{7,6},{8,9},{9,8},{10,11... | collective-permute-start | bytes 3145736 | tf_op jit(solution)/shard_map/ppermute | solution.py:34
  120.6 4.5 collective-permute-start.19
  125.7 17.0 %collective-permute-start.24 = (bf16[128,2048]{1,0:T(8,128)(2,1)}, bf16[128,2048]{1,0:T(8,128)(2,1)S(1)}, u32[]{:S(2)}, u32[]{:S(2)}) collective-permute-start(bf16[128,2048]{1,0:T(8,128)(2,1)} %get-tuple-element.419), channel_id=1, source_target_pairs={{0,8},{8,16},{16,24},{24,0},{1,9},{9,17},{17,25},{25,1},{2,10},{10... | collective-permute-start | bytes 1572872 | tf_op jit(solution)/shard_map/ppermute | solution.py:38
  129.8 43.3 %collective-permute-start.25 = (bf16[128,2048]{1,0:T(8,128)(2,1)}, bf16[128,2048]{1,0:T(8,128)(2,1)S(1)}, u32[]{:S(2)}, u32[]{:S(2)}) collective-permute-start(bf16[128,2048]{1,0:T(8,128)(2,1)} %get-tuple-element.420), channel_id=1, source_target_pairs={{0,16},{8,24},{16,0},{24,8},{1,17},{9,25},{17,1},{25,9},{2,18},{10... | collective-permute-start | bytes 1572872 | tf_op jit(solution)/shard_map/ppermute | solution.py:38
  129.8 43.3 %collective-permute-start.26 = (bf16[128,2048]{1,0:T(8,128)(2,1)}, bf16[128,2048]{1,0:T(8,128)(2,1)}, u32[]{:S(2)}, u32[]{:S(2)}) collective-permute-start(bf16[128,2048]{1,0:T(8,128)(2,1)} %get-tuple-element.421), channel_id=1, source_target_pairs={{0,24},{8,0},{16,8},{24,16},{1,25},{9,1},{17,9},{25,17},{2,26},{10... | collective-permute-start | bytes 1572872 | tf_op jit(solution)/shard_map/ppermute | solution.py:38
  141.4 31.7 %collective-permute-start.22 = (bf16[512,512]{1,0:T(8,128)(2,1)S(1)}, bf16[512,512]{1,0:T(8,128)(2,1)S(1)}, u32[]{:S(2)}, u32[]{:S(2)}) collective-permute-start(bf16[512,512]{1,0:T(8,128)(2,1)S(1)} %slice.98), channel_id=1, source_target_pairs={{0,4},{4,0},{1,5},{5,1},{2,6},{6,2},{3,7},{7,3},{8,12},{12,8},{9,1... | collective-permute-start | bytes 1572872 | tf_op jit(solution)/shard_map/ppermute | solution.py:34
  142.1 31.8 %collective-permute-start.23 = (bf16[512,512]{1,0:T(8,128)(2,1)S(1)}, bf16[512,512]{1,0:T(8,128)(2,1)S(1)}, u32[]{:S(2)}, u32[]{:S(2)}) collective-permute-start(bf16[512,512]{1,0:T(8,128)(2,1)S(1)} %slice.99), channel_id=1, source_target_pairs={{0,1},{1,0},{2,3},{3,2},{4,5},{5,4},{6,7},{7,6},{8,9},{9,8},{10,11... | collective-permute-start | bytes 1572872 | tf_op jit(solution)/shard_map/ppermute | solution.py:34
  174.7 107.7 %all-gather.7.cloned.1.call-start = ((), (), s32[]{:S(2)}) async-start(), calls=%async_computation.6 | async-start | bytes 4718592 | tf_op jit(solution)/shard_map/all_gather | solution.py:645
  184.6 47.9 %collective-permute-start.28 = (bf16[1024,1024]{1,0:T(8,128)(2,1)}, bf16[1024,1024]{1,0:T(8,128)(2,1)S(1)}, u32[]{:S(2)}, u32[]{:S(2)}) collective-permute-start(bf16[1024,1024]{1,0:T(8,128)(2,1)} %shard_map.249.refs_0_), channel_id=1, source_target_pairs={{0,4},{4,0},{1,5},{5,1},{2,6},{6,2},{3,7},{7,3},{8,12},{12,8},{9,1... | collective-permute-start | bytes 6291464 | tf_op jit(solution)/shard_map/ppermute | solution.py:34
  185.3 47.7 %collective-permute-start.29 = (bf16[1024,1024]{1,0:T(8,128)(2,1)}, bf16[1024,1024]{1,0:T(8,128)(2,1)}, u32[]{:S(2)}, u32[]{:S(2)}) collective-permute-start(bf16[1024,1024]{1,0:T(8,128)(2,1)} %shard_map.249.refs_0_), channel_id=1, source_target_pairs={{0,1},{1,0},{2,3},{3,2},{4,5},{5,4},{6,7},{7,6},{8,9},{9,8},{10,11... | collective-permute-start | bytes 6291464 | tf_op jit(solution)/shard_map/ppermute | solution.py:34
  236.9 115.7 %reduce-scatter.7.cloned.1.call-start = ((), (), s32[]{:S(2)}) async-start(), calls=%async_computation.7 | async-start | bytes 4718592 | tf_op jit(solution)/shard_map/reduce_scatter | solution.py:642
  239.3 24.4 %collective-permute-start.30 = (bf16[512,1024]{1,0:T(8,128)(2,1)}, bf16[512,1024]{1,0:T(8,128)(2,1)}, u32[]{:S(2)}, u32[]{:S(2)}) collective-permute-start(bf16[512,1024]{1,0:T(8,128)(2,1)} %slice.100), channel_id=1, source_target_pairs={{0,4},{4,0},{1,5},{5,1},{2,6},{6,2},{3,7},{7,3},{8,12},{12,8},{9,1... | collective-permute-start | bytes 3145736 | tf_op jit(solution)/shard_map/ppermute | solution.py:34
  241.7 24.1 %collective-permute-start.31 = (bf16[512,1024]{1,0:T(8,128)(2,1)}, bf16[512,1024]{1,0:T(8,128)(2,1)}, u32[]{:S(2)}, u32[]{:S(2)}) collective-permute-start(bf16[512,1024]{1,0:T(8,128)(2,1)} %slice.101), channel_id=1, source_target_pairs={{0,1},{1,0},{2,3},{3,2},{4,5},{5,4},{6,7},{7,6},{8,9},{9,8},{10,11... | collective-permute-start | bytes 3145736 | tf_op jit(solution)/shard_map/ppermute | solution.py:34
  304.2 99.4 %all-gather.9.cloned.1.call-start = ((), (), s32[]{:S(2)}) async-start(), calls=%async_computation.8 | async-start | bytes 4718592 | tf_op jit(solution)/shard_map/all_gather | solution.py:645
  357.7 116.8 %reduce-scatter.9.cloned.1.call-start = ((), (), s32[]{:S(2)}) async-start(), calls=%async_computation.9 | async-start | bytes 4718592 | tf_op jit(solution)/shard_map/reduce_scatter | solution.py:642
  359.8 14.0 %collective-permute-start.32 = (bf16[128,2048]{1,0:T(8,128)(2,1)}, bf16[128,2048]{1,0:T(8,128)(2,1)S(1)}, u32[]{:S(2)}, u32[]{:S(2)}) collective-permute-start(bf16[128,2048]{1,0:T(8,128)(2,1)} %shard_map.254), channel_id=1, source_target_pairs={{0,1},{1,0},{2,3},{3,2},{4,5},{5,4},{6,7},{7,6},{8,9},{9,8},{10,11... | collective-permute-start | bytes 1572872 | tf_op jit(solution)/shard_map/ppermute | solution.py:34
  426.0 97.0 %all-gather.11.cloned.1.call-start = ((), (), s32[]{:S(2)}) async-start(), calls=%async_computation.10 | async-start | bytes 4718592 | tf_op jit(solution)/shard_map/all_gather | solution.py:645
  435.0 25.7 %collective-permute-start.33 = (bf16[2,512,512]{2,1,0:T(8,128)(2,1)}, bf16[2,512,512]{2,1,0:T(8,128)(2,1)}, u32[]{:S(2)}, u32[]{:S(2)}) collective-permute-start(bf16[2,512,512]{2,1,0:T(8,128)(2,1)} %get-tuple-element.480), channel_id=1, source_target_pairs={{0,4},{4,0},{1,5},{5,1},{2,6},{6,2},{3,7},{7,3},{8,12},{12,8},{9,1... | collective-permute-start | bytes 3145736 | tf_op jit(solution)/shard_map/ppermute | solution.py:34
  436.5 25.3 %collective-permute-start.34 = (bf16[2,512,512]{2,1,0:T(8,128)(2,1)}, bf16[2,512,512]{2,1,0:T(8,128)(2,1)}, u32[]{:S(2)}, u32[]{:S(2)}) collective-permute-start(bf16[2,512,512]{2,1,0:T(8,128)(2,1)} %get-tuple-element.481), channel_id=1, source_target_pairs={{0,1},{1,0},{2,3},{3,2},{4,5},{5,4},{6,7},{7,6},{8,9},{9,8},{10,11... | collective-permute-start | bytes 3145736 | tf_op jit(solution)/shard_map/ppermute | solution.py:34
  477.2 154.8 %reduce-scatter.11.cloned.1.call-start = ((), (), s32[]{:S(2)}) async-start(), calls=%async_computation.11 | async-start | bytes 4718592 | tf_op jit(solution)/shard_map/reduce_scatter | solution.py:642
  478.6 13.7 %collective-permute-start.36 = (bf16[512,512]{1,0:T(8,128)(2,1)S(1)}, bf16[512,512]{1,0:T(8,128)(2,1)S(1)}, u32[]{:S(2)}, u32[]{:S(2)}) collective-permute-start(bf16[512,512]{1,0:T(8,128)(2,1)S(1)} %fusion.34), channel_id=1, source_target_pairs={{0,4},{4,0},{1,5},{5,1},{2,6},{6,2},{3,7},{7,3},{8,12},{12,8},{9,1... | collective-permute-start | bytes 1572872 | tf_op jit(solution)/shard_map/ppermute | solution.py:34
  480.5 14.2 %collective-permute-start.35 = (bf16[512,512]{1,0:T(8,128)(2,1)S(1)}, bf16[512,512]{1,0:T(8,128)(2,1)S(1)}, u32[]{:S(2)}, u32[]{:S(2)}) collective-permute-start(bf16[512,512]{1,0:T(8,128)(2,1)S(1)} %fusion.35), channel_id=1, source_target_pairs={{0,1},{1,0},{2,3},{3,2},{4,5},{5,4},{6,7},{7,6},{8,9},{9,8},{10,11... | collective-permute-start | bytes 1572872 | tf_op jit(solution)/shard_map/ppermute | solution.py:34
  494.7 48.6 %collective-permute-start.41 = (bf16[2,512,1024]{2,1,0:T(8,128)(2,1)}, bf16[2,512,1024]{2,1,0:T(8,128)(2,1)}, u32[]{:S(2)}, u32[]{:S(2)}) collective-permute-start(bf16[2,512,1024]{2,1,0:T(8,128)(2,1)} %get-tuple-element.536), channel_id=1, source_target_pairs={{0,4},{4,0},{1,5},{5,1},{2,6},{6,2},{3,7},{7,3},{8,12},{12,8},{9,1... | collective-permute-start | bytes 6291464 | tf_op jit(solution)/shard_map/ppermute | solution.py:34
  495.3 48.1 %collective-permute-start.42 = (bf16[2,512,1024]{2,1,0:T(8,128)(2,1)}, bf16[2,512,1024]{2,1,0:T(8,128)(2,1)}, u32[]{:S(2)}, u32[]{:S(2)}) collective-permute-start(bf16[2,512,1024]{2,1,0:T(8,128)(2,1)} %get-tuple-element.537), channel_id=1, source_target_pairs={{0,1},{1,0},{2,3},{3,2},{4,5},{5,4},{6,7},{7,6},{8,9},{9,8},{10,11... | collective-permute-start | bytes 6291464 | tf_op jit(solution)/shard_map/ppermute | solution.py:34
  523.0 20.3 %collective-permute-start.38 = (bf16[128,1024]{1,0:T(8,128)(2,1)}, bf16[128,1024]{1,0:T(8,128)(2,1)S(1)}, u32[]{:S(2)}, u32[]{:S(2)}) collective-permute-start(bf16[128,1024]{1,0:T(8,128)(2,1)} %get-tuple-element.533), channel_id=1, source_target_pairs={{0,8},{8,16},{16,24},{24,0},{1,9},{9,17},{17,25},{25,1},{2,10},{10... | collective-permute-start | bytes 786440 | tf_op jit(solution)/shard_map/ppermute | solution.py:38
  525.7 23.6 %collective-permute-start.39 = (bf16[128,1024]{1,0:T(8,128)(2,1)}, bf16[128,1024]{1,0:T(8,128)(2,1)S(1)}, u32[]{:S(2)}, u32[]{:S(2)}) collective-permute-start(bf16[128,1024]{1,0:T(8,128)(2,1)} %get-tuple-element.534), channel_id=1, source_target_pairs={{0,16},{8,24},{16,0},{24,8},{1,17},{9,25},{17,1},{25,9},{2,18},{10... | collective-permute-start | bytes 786440 | tf_op jit(solution)/shard_map/ppermute | solution.py:38
  525.9 23.5 %collective-permute-start.40 = (bf16[128,1024]{1,0:T(8,128)(2,1)}, bf16[128,1024]{1,0:T(8,128)(2,1)S(1)}, u32[]{:S(2)}, u32[]{:S(2)}) collective-permute-start(bf16[128,1024]{1,0:T(8,128)(2,1)} %get-tuple-element.535), channel_id=1, source_target_pairs={{0,24},{8,0},{16,8},{24,16},{1,25},{9,1},{17,9},{25,17},{2,26},{10... | collective-permute-start | bytes 786440 | tf_op jit(solution)/shard_map/ppermute | solution.py:38
  552.1 29.2 %collective-permute-start.47 = (bf16[512,1024]{1,0:T(8,128)(2,1)}, bf16[512,1024]{1,0:T(8,128)(2,1)S(1)}, u32[]{:S(2)}, u32[]{:S(2)}) collective-permute-start(bf16[512,1024]{1,0:T(8,128)(2,1)} %fusion.4), channel_id=1, source_target_pairs={{0,4},{4,0},{1,5},{5,1},{2,6},{6,2},{3,7},{7,3},{8,12},{12,8},{9,1... | collective-permute-start | bytes 3145736 | tf_op jit(solution)/shard_map/ppermute | solution.py:34
  556.2 25.1 %collective-permute-start.46 = (bf16[512,1024]{1,0:T(8,128)(2,1)}, bf16[512,1024]{1,0:T(8,128)(2,1)S(1)}, u32[]{:S(2)}, u32[]{:S(2)}) collective-permute-start(bf16[512,1024]{1,0:T(8,128)(2,1)} %fusion.5), channel_id=1, source_target_pairs={{0,1},{1,0},{2,3},{3,2},{4,5},{5,4},{6,7},{7,6},{8,9},{9,8},{10,11... | collective-permute-start | bytes 3145736 | tf_op jit(solution)/shard_map/ppermute | solution.py:34
  559.4 4.0 collective-permute-start.44
  563.4 4.9 collective-permute-start.45
  568.3 13.0 %collective-permute-start.48 = (f32[64,128]{1,0:T(8,128)S(1)}, f32[64,128]{1,0:T(8,128)S(1)}, u32[]{:S(2)}, u32[]{:S(2)}) collective-permute-start(f32[64,128]{1,0:T(8,128)S(1)} %slice.129), channel_id=1, source_target_pairs={{0,1},{1,0},{2,3},{3,2},{4,5},{5,4},{6,7},{7,6},{8,9},{9,8},{10,11... | collective-permute-start | bytes 98312 | tf_op jit(solution)/shard_map/ppermute | solution.py:34
  586.3 14.3 %collective-permute-start.51 = (bf16[512,1024]{1,0:T(8,128)(2,1)}, bf16[512,1024]{1,0:T(8,128)(2,1)S(1)}, u32[]{:S(2)}, u32[]{:S(2)}) collective-permute-start(bf16[512,1024]{1,0:T(8,128)(2,1)} %get-tuple-element.654), channel_id=1, source_target_pairs={{0,2},{2,0},{1,3},{3,1},{4,6},{6,4},{5,7},{7,5},{8,10},{10,8},{9,1... | collective-permute-start | bytes 3145736 | tf_op jit(solution)/shard_map/ppermute | solution.py:34
  596.2 25.9 %collective-permute-start.49 = (bf16[2,512,512]{2,1,0:T(8,128)(2,1)}, bf16[2,512,512]{2,1,0:T(8,128)(2,1)S(1)}, u32[]{:S(2)}, u32[]{:S(2)}) collective-permute-start(bf16[2,512,512]{2,1,0:T(8,128)(2,1)} %get-tuple-element.566), channel_id=1, source_target_pairs={{0,4},{4,0},{1,5},{5,1},{2,6},{6,2},{3,7},{7,3},{8,12},{12,8},{9,1... | collective-permute-start | bytes 3145736 | tf_op jit(solution)/shard_map/ppermute | solution.py:34
  596.5 25.9 %collective-permute-start.50 = (bf16[2,512,512]{2,1,0:T(8,128)(2,1)}, bf16[2,512,512]{2,1,0:T(8,128)(2,1)}, u32[]{:S(2)}, u32[]{:S(2)}) collective-permute-start(bf16[2,512,512]{2,1,0:T(8,128)(2,1)} %get-tuple-element.567), channel_id=1, source_target_pairs={{0,1},{1,0},{2,3},{3,2},{4,5},{5,4},{6,7},{7,6},{8,9},{9,8},{10,11... | collective-permute-start | bytes 3145736 | tf_op jit(solution)/shard_map/ppermute | solution.py:34
  622.4 16.8 %collective-permute-start.54 = (bf16[128,2048]{1,0:T(8,128)(2,1)}, bf16[128,2048]{1,0:T(8,128)(2,1)}, u32[]{:S(2)}, u32[]{:S(2)}) collective-permute-start(bf16[128,2048]{1,0:T(8,128)(2,1)} %get-tuple-element.593), channel_id=1, source_target_pairs={{0,8},{8,16},{16,24},{24,0},{1,9},{9,17},{17,25},{25,1},{2,10},{10... | collective-permute-start | bytes 1572872 | tf_op jit(solution)/shard_map/ppermute | solution.py:38
  622.4 50.5 %collective-permute-start.55 = (bf16[128,2048]{1,0:T(8,128)(2,1)}, bf16[128,2048]{1,0:T(8,128)(2,1)}, u32[]{:S(2)}, u32[]{:S(2)}) collective-permute-start(bf16[128,2048]{1,0:T(8,128)(2,1)} %get-tuple-element.594), channel_id=1, source_target_pairs={{0,16},{8,24},{16,0},{24,8},{1,17},{9,25},{17,1},{25,9},{2,18},{10... | collective-permute-start | bytes 1572872 | tf_op jit(solution)/shard_map/ppermute | solution.py:38
  624.2 48.7 %collective-permute-start.56 = (bf16[128,2048]{1,0:T(8,128)(2,1)}, bf16[128,2048]{1,0:T(8,128)(2,1)}, u32[]{:S(2)}, u32[]{:S(2)}) collective-permute-start(bf16[128,2048]{1,0:T(8,128)(2,1)} %get-tuple-element.595), channel_id=1, source_target_pairs={{0,24},{8,0},{16,8},{24,16},{1,25},{9,1},{17,9},{25,17},{2,26},{10... | collective-permute-start | bytes 1572872 | tf_op jit(solution)/shard_map/ppermute | solution.py:38
  628.4 44.5 %collective-permute-start.53 = (bf16[512,512]{1,0:T(8,128)(2,1)}, bf16[512,512]{1,0:T(8,128)(2,1)}, u32[]{:S(2)}, u32[]{:S(2)}) collective-permute-start(bf16[512,512]{1,0:T(8,128)(2,1)} %fusion.29), channel_id=1, source_target_pairs={{0,4},{4,0},{1,5},{5,1},{2,6},{6,2},{3,7},{7,3},{8,12},{12,8},{9,1... | collective-permute-start | bytes 1572872 | tf_op jit(solution)/shard_map/ppermute | solution.py:34
  630.5 42.4 %collective-permute-start.52 = (bf16[512,512]{1,0:T(8,128)(2,1)}, bf16[512,512]{1,0:T(8,128)(2,1)}, u32[]{:S(2)}, u32[]{:S(2)}) collective-permute-start(bf16[512,512]{1,0:T(8,128)(2,1)} %fusion.30), channel_id=1, source_target_pairs={{0,1},{1,0},{2,3},{3,2},{4,5},{5,4},{6,7},{7,6},{8,9},{9,8},{10,11... | collective-permute-start | bytes 1572872 | tf_op jit(solution)/shard_map/ppermute | solution.py:34
  675.8 5.4 collective-permute-start.57
  675.8 14.3 %collective-permute-start.60 = (bf16[128,2048]{1,0:T(8,128)(2,1)S(1)}, bf16[128,2048]{1,0:T(8,128)(2,1)S(1)}, u32[]{:S(2)}, u32[]{:S(2)}) collective-permute-start(bf16[128,2048]{1,0:T(8,128)(2,1)S(1)} %copy-done.27), channel_id=1, source_target_pairs={{0,1},{1,0},{2,3},{3,2},{4,5},{5,4},{6,7},{7,6},{8,9},{9,8},{10,11... | collective-permute-start | bytes 1572872 | tf_op jit(solution)/shard_map/ppermute | solution.py:34
  677.3 3.9 collective-permute-start.58
  684.2 8.5 %collective-permute-start.59 = (bf16[128,1024]{1,0:T(8,128)(2,1)}, bf16[128,1024]{1,0:T(8,128)(2,1)S(1)}, u32[]{:S(2)}, u32[]{:S(2)}) collective-permute-start(bf16[128,1024]{1,0:T(8,128)(2,1)} %get-tuple-element.610), channel_id=1, source_target_pairs={{0,8},{8,16},{16,24},{24,0},{1,9},{9,17},{17,25},{25,1},{2,10},{10... | collective-permute-start | bytes 786440 | tf_op jit(solution)/shard_map/ppermute | solution.py:38
  684.3 24.8 %collective-permute-start.61 = (bf16[128,1024]{1,0:T(8,128)(2,1)}, bf16[128,1024]{1,0:T(8,128)(2,1)S(1)}, u32[]{:S(2)}, u32[]{:S(2)}) collective-permute-start(bf16[128,1024]{1,0:T(8,128)(2,1)} %get-tuple-element.629), channel_id=1, source_target_pairs={{0,16},{8,24},{16,0},{24,8},{1,17},{9,25},{17,1},{25,9},{2,18},{10... | collective-permute-start | bytes 786440 | tf_op jit(solution)/shard_map/ppermute | solution.py:38
  686.2 22.8 %collective-permute-start.62 = (bf16[128,1024]{1,0:T(8,128)(2,1)}, bf16[128,1024]{1,0:T(8,128)(2,1)S(1)}, u32[]{:S(2)}, u32[]{:S(2)}) collective-permute-start(bf16[128,1024]{1,0:T(8,128)(2,1)} %get-tuple-element.630), channel_id=1, source_target_pairs={{0,24},{8,0},{16,8},{24,16},{1,25},{9,1},{17,9},{25,17},{2,26},{10... | collective-permute-start | bytes 786440 | tf_op jit(solution)/shard_map/ppermute | solution.py:38
  (71 other events, 1012.4 us)
Sparse Core Ops, SparseCore 0:
  36.2 50.3 all-gather.4
  174.8 47.0 reduce-scatter.4
  237.0 45.3 all-gather.6
  304.3 48.2 reduce-scatter.6
  357.8 45.7 all-gather.8
  426.1 48.3 reduce-scatter.8
  477.3 45.6 all-gather.10
  581.5 50.4 reduce-scatter.10

commit v5 on v4

--- a/solution.py
+++ b/solution.py
@@ -830,12 +830,14 @@
         gain_x,
     )
     input_part = team_scatter(input_part)
-    attn = step(
-        weight_grads([(all_rows, qkv_grad), (projected_all, mixed)], reps, [cut, HEAD_DIM])
+    feed = step(place.unsettle(place.narrowed(feed, feed_came, feed_more)))
+    qkv_grad, feed = step(qkv_grad, deal(*feed, place.g, place.c))
+    feed = place.send(feed)
+    attn, feed[1] = step(
+        weight_grads([(all_rows, qkv_grad), (projected_all, mixed)], reps, [cut, HEAD_DIM]),
+        feed[1],
     )
     attn_came = place.narrow(attn)
-    feed = step(place.unsettle(place.narrowed(feed, feed_came, feed_more)))
-    feed = place.send(step(deal(*feed, place.g, place.c)))
     gain_grads = gain_grads + gain_x
     gain_q = swap(gain_grads, "q") if reps == 2 else lax.psum(gain_grads, "q") - gain_grads
     [down_grad] = step(unpack(down, place.g, 1))

time: 732 us -> 737 us (level)
  transfers between devices with their start and end apart: 71 -> 71, of which waited for: 42 -> 43; matrix products, arithmetic and copies ran while one was open for 6% -> 6% of each run, Pallas kernels for 17% -> 17%
where the time goes in v5:
time: 737 us; the launch traced here: 725 us
  waiting for transfers between devices  387 us (53%)
  Pallas kernels  132 us (18%)
  starting transfers between devices  63.1 us (9%)
  other arithmetic  50.9 us (7%)
  matrix products  42.6 us (6%)
  local copies, waits for them, and re-layouts  33.6 us (5%)
  between operations  15.3 us (2%)
    ppermute x38, waiting for transfers between devices, swap(): return lax.ppermute(value, axis, [(0, 1), (1, 0)])  145 us
    ppermute x21, waiting for transfers between devices, shift(): lax.ppermute(value, 'g', [(i, (i + by) % GROUP) for i in range(GROUP)])  112 us
    reduce_scatter x4, waiting for transfers between devices, team_scatter(): return lax.psum_scatter(value, TEAM, scatter_dimension=0, tiled=True)  61.9 us
    all_gather x4, waiting for transfers between devices, team_gather(): return lax.all_gather(value, TEAM, axis=0, tiled=True)  55.7 us
    pallas_call x4, Pallas kernels, row_call(): pl.pallas_call(kernel, grid=(rows // ROWS,), in_specs=[spec(v.shape, bloc...  44.7 us
    pallas_call x15, Pallas kernels, vmem_call(): pl.pallas_call(kernel, out_shape=shapes, in_specs=[pl.BlockSpec(memory_sp...  39.7 us
    pallas_call x3, Pallas kernels, weight_grads(): pl.pallas_call(kernel, grid=(steps,), in_specs=[pl.BlockSpec((count, step...  33.1 us
    ppermute x38, starting transfers between devices, swap(): return lax.ppermute(value, axis, [(0, 1), (1, 0)])  31.8 us
  transfers between devices with their start and end apart: 71, of which 43 were waited for; matrix products, arithmetic and copies ran while one was open for 6% of the time, Pallas kernels for 17%

profile of v5, /device:TPU:24, one launch (start us, length us, event | category | flops | bytes accessed | tf_op | source)
XLA Modules:
  0.0 725.1 jit_solution(5225359992987426729)
XLA Ops:
  8.0 2.4 shard_map.237
  17.9 3.1 shard_map.240
  21.0 15.1 %collective-permute-done.1.refs_2_ = bf16[128,1024]{1,0:T(8,128)(2,1)S(1)} collective-permute-done((bf16[128,1024]{1,0:T(8,128)(2,1)}, bf16[128,1024]{1,0:T(8,128)(2,1)S(1)}, u32[]{:S(2)}, u32[]{:S(2)}) %collective-permute-start.1) | collective-permute-done | bytes 262176 | tf_op jit(solution)/shard_map/ppermute | solution.py:38
  55.6 15.1 %collective-permute-done.8.refs_1_ = bf16[1024,512]{1,0:T(8,128)(2,1)S(1)} collective-permute-done((bf16[1024,512]{1,0:T(8,128)(2,1)}, bf16[1024,512]{1,0:T(8,128)(2,1)S(1)}, u32[]{:S(2)}, u32[]{:S(2)}) %collective-permute-start.8) | collective-permute-done | bytes 1048608 | tf_op jit(solution)/shard_map/ppermute | solution.py:34
  80.4 4.7 collective-permute-done.11.refs_3_
  88.8 7.8 %shard_map.244 = (f32[1024,768]{1,0:T(8,128)}, f32[8,2,128]{2,1,0:T(2,128)}) custom-call(bf16[1024,2048]{1,0:T(8,128)(2,1)} %all-gather.5.cloned.1.call-done.tokens.refs_0_.refs_2_, bf16[2048,768]{1,0:T(8,128)(2,1)} %copy-done.2), custom_call_target="tpu_custom_call" | custom-call | tf_op jit(solution)/shard_map/pallas_call | solution.py:370
  96.7 6.4 collective-permute-done.15.refs_2_
  116.9 3.6 collective-permute-done.18
  120.6 2.6 collective-permute-start.19
  125.7 4.0 collective-permute-start.24
  130.4 11.0 %shard_map.246 = (bf16[1024,256]{1,0:T(8,128)(2,1)}, bf16[1024,256]{1,0:T(8,128)(2,1)}, bf16[1024,256]{1,0:T(8,128)(2,1)}, bf16[1024,256]{1,0:T(8,128)(2,1)}, bf16[1024,2048]{1,0:T(8,128)(2,1)}) custom-call(f32[1024,768]{1,0:T(8,128)} %get-tuple-element.377.qkv_all, f32[8,2,128]{2,1,0:T(2,128)} %add.203.squares, f32[2,2,128]{2,1,0:T(2,128)} %pad_maximum_fusion.5.gains, ...), custom_call_target="tpu_custom_call" | custom-call | tf_op jit(solution)/shard_map/pallas_call | solution.py:370
  142.7 30.3 %collective-permute-done.25.refs_2_ = bf16[128,2048]{1,0:T(8,128)(2,1)S(1)} collective-permute-done((bf16[128,2048]{1,0:T(8,128)(2,1)}, bf16[128,2048]{1,0:T(8,128)(2,1)S(1)}, u32[]{:S(2)}, u32[]{:S(2)}) %collective-permute-start.25) | collective-permute-done | bytes 524320 | tf_op jit(solution)/shard_map/ppermute | solution.py:38
  174.8 3.0 shard_map.248
  177.8 2.9 collective-permute-done.27.second
  181.6 3.0 shard_map.249.refs_0_
  188.9 43.6 %collective-permute-done.28.refs_1_ = bf16[1024,1024]{1,0:T(8,128)(2,1)S(1)} collective-permute-done((bf16[1024,1024]{1,0:T(8,128)(2,1)}, bf16[1024,1024]{1,0:T(8,128)(2,1)S(1)}, u32[]{:S(2)}, u32[]{:S(2)}) %collective-permute-start.28) | collective-permute-done | bytes 2097184 | tf_op jit(solution)/shard_map/ppermute | solution.py:34
  234.2 2.6 fusion.39
  243.3 2.4 shard_map.253
  255.4 8.3 %collective-permute-done.30.refs_3_ = bf16[512,1024]{1,0:T(8,128)(2,1)} collective-permute-done((bf16[512,1024]{1,0:T(8,128)(2,1)}, bf16[512,1024]{1,0:T(8,128)(2,1)}, u32[]{:S(2)}, u32[]{:S(2)}) %collective-permute-start.30) | collective-permute-done | bytes 1048608 | tf_op jit(solution)/shard_map/ppermute | solution.py:34
  265.8 2.6 shard_map.252
  272.5 10.0 %all-gather.7.cloned.1.call-done.refs_0_.refs_1_.refs_2_.refs_3_ = bf16[1024,2048]{1,0:T(8,128)(2,1)} async-done(((bf16[128,2048]{1,0:T(8,128)(2,1)}), bf16[1024,2048]{1,0:T(8,128)(2,1)}) %all-gather.7.cloned.1.call-update) | async-done | bytes 4194320 | tf_op jit(solution)/shard_map/all_gather | solution.py:645
  282.4 7.6 %fusion.43 = f32[1024,1024]{1,0:T(8,128)S(1)} fusion(bf16[1024,2048]{1,0:T(8,128)(2,1)} %all-gather.7.cloned.1.call-done.refs_0_.refs_1_.refs_2_.refs_3_, bf16[2048,1024]{1,0:T(8,128)(2,1)} %copy-done.4), kind=kOutput, calls=%fused_computation.118 | convolution fusion | flops 4294967296 | bytes 12582912 | tf_op jit(solution)/shard_map/dot_general | solution.py:22
  290.1 6.5 multiply_convert_fusion.2
  298.0 6.2 convolution_convert_fusion
  304.2 48.4 %reduce-scatter.7.cloned.1.call-done = bf16[128,2048]{1,0:T(8,128)(2,1)} async-done(((bf16[1024,2048]{1,0:T(8,128)(2,1)}), bf16[128,2048]{1,0:T(8,128)(2,1)}) %reduce-scatter.7.cloned.1.call-update) | async-done | bytes 524304 | tf_op jit(solution)/shard_map/reduce_scatter | solution.py:642
  355.2 2.4 fusion.24
  360.7 13.1 %collective-permute-done.32 = bf16[128,2048]{1,0:T(8,128)(2,1)S(1)} collective-permute-done((bf16[128,2048]{1,0:T(8,128)(2,1)}, bf16[128,2048]{1,0:T(8,128)(2,1)S(1)}, u32[]{:S(2)}, u32[]{:S(2)}) %collective-permute-start.32) | collective-permute-done | bytes 524320 | tf_op jit(solution)/shard_map/ppermute | solution.py:34
  376.2 27.4 %all-gather.9.cloned.1.call-done.refs_0_.refs_1_ = bf16[1024,2048]{1,0:T(8,128)(2,1)} async-done(((bf16[128,2048]{1,0:T(8,128)(2,1)}), bf16[1024,2048]{1,0:T(8,128)(2,1)}) %all-gather.9.cloned.1.call-update) | async-done | bytes 4194320 | tf_op jit(solution)/shard_map/all_gather | solution.py:645
  403.6 11.5 %multiply_convert_fusion = (bf16[1024,1024]{1,0:T(8,128)(2,1)S(1)}, bf16[1024,1024]{1,0:T(8,128)(2,1)S(1)}) fusion(f32[1024,1024]{1,0:T(8,128)} %copy-done.63, f32[1024,1024]{1,0:T(8,128)} %get-tuple-element.684, bf16[1024,2048]{1,0:T(8,128)(2,1)} %all-gather.9.cloned.1.call-done.refs_0_.refs_1_, bf16[2048,1024]{1,0:T(8,128)(2,1)} %copy-done.18), kind=kOutput, calls=%fused_computation.1 | convolution fusion | flops 4308598784 | bytes 20971520 | tf_op jit(solution)/shard_map/dot_general | solution.py:22
  415.2 4.6 fusion.44
  419.8 6.2 add_convert_fusion
  426.2 8.8 %shard_map.255 = (bf16[2,512,512]{2,1,0:T(8,128)(2,1)}, bf16[2,512,512]{2,1,0:T(8,128)(2,1)}, bf16[512,512]{1,0:T(8,128)(2,1)}, bf16[512,512]{1,0:T(8,128)(2,1)}, bf16[1024,512]{1,0:T(8,128)(2,1)}) custom-call(bf16[1024,2048]{1,0:T(8,128)(2,1)} %all-gather.9.cloned.1.call-done.refs_0_.refs_1_, ...), custom_call_target="tpu_custom_call" | custom-call | bytes 209715200 | tf_op jit(solution)/shard_map/pallas_call | solution.py:282
  438.0 14.8 %shard_map.256 = (bf16[2,512,1024]{2,1,0:T(8,128)(2,1)}, bf16[2,512,1024]{2,1,0:T(8,128)(2,1)}, bf16[512,1024]{1,0:T(8,128)(2,1)}, bf16[512,1024]{1,0:T(8,128)(2,1)}, bf16[1024,1024]{1,0:T(8,128)(2,1)}) custom-call(bf16[1024,2048]{1,0:T(8,128)(2,1)} %all-gather.7.cloned.1.call-done.refs_0_.refs_1_.refs_2_.refs_3_, ...), custom_call_target="tpu_custom_call" | custom-call | bytes 209715200 | tf_op jit(solution)/shard_map/pallas_call | solution.py:282
  452.8 7.9 %collective-permute-done.33 = bf16[2,512,512]{2,1,0:T(8,128)(2,1)} collective-permute-done((bf16[2,512,512]{2,1,0:T(8,128)(2,1)}, bf16[2,512,512]{2,1,0:T(8,128)(2,1)}, u32[]{:S(2)}, u32[]{:S(2)}) %collective-permute-start.33) | collective-permute-done | bytes 1048608 | tf_op jit(solution)/shard_map/ppermute | solution.py:34
  461.9 12.6 %reduce-scatter.9.cloned.1.call-done = bf16[128,2048]{1,0:T(8,128)(2,1)} async-done(((bf16[1024,2048]{1,0:T(8,128)(2,1)}), bf16[128,2048]{1,0:T(8,128)(2,1)}) %reduce-scatter.9.cloned.1.call-update) | async-done | bytes 524304 | tf_op jit(solution)/shard_map/reduce_scatter | solution.py:642
  482.1 10.2 %collective-permute-done.36 = bf16[512,512]{1,0:T(8,128)(2,1)S(1)} collective-permute-done((bf16[512,512]{1,0:T(8,128)(2,1)S(1)}, bf16[512,512]{1,0:T(8,128)(2,1)S(1)}, u32[]{:S(2)}, u32[]{:S(2)}) %collective-permute-start.36) | collective-permute-done | bytes 524320 | tf_op jit(solution)/shard_map/ppermute | solution.py:34
  492.3 2.4 collective-permute-done.35
  496.8 2.8 broadcast_select_fusion.4
  502.3 2.4 shard_map.258
  504.7 18.3 %all-gather.11.cloned.1.call-done.grads.refs_1_.refs_3_ = bf16[1024,2048]{1,0:T(8,128)(2,1)} async-done(((bf16[128,2048]{1,0:T(8,128)(2,1)}), bf16[1024,2048]{1,0:T(8,128)(2,1)}) %all-gather.11.cloned.1.call-update) | async-done | bytes 4194320 | tf_op jit(solution)/shard_map/all_gather | solution.py:645
  523.0 2.7 collective-permute-start.38
  526.3 17.0 %shard_map.259 = (f32[1024,512]{1,0:T(8,128)}, bf16[1024,256]{1,0:T(8,128)(2,1)}, f32[8,2,128]{2,1,0:T(2,128)}, f32[2,2,128]{2,1,0:T(2,128)}) custom-call(bf16[1024,2048]{1,0:T(8,128)(2,1)} %all-gather.11.cloned.1.call-done.grads.refs_1_.refs_3_, bf16[2048,256]{1,0:T(8,128)(2,1)} %copy-done.6, bf16[1024,256]{1,0:T(8,128)(2,1)} %get-tuple-element.527.query_all, ...), custom_call_target="tpu_custom_call" | custom-call | tf_op jit(solution)/shard_map/pallas_call | solution.py:370
  543.4 6.0 collective-permute-done.39.refs_2_
  549.4 2.8 fusion.4
  553.6 2.6 fusion.5
  559.4 4.0 collective-permute-done.44
  565.2 3.1 collective-permute-done.45
  569.5 8.9 %shard_map.260 = (bf16[1024,768]{1,0:T(8,128)(2,1)}, bf16[1024,2048]{1,0:T(8,128)(2,1)}) custom-call(f32[1024,512]{1,0:T(8,128)} %get-tuple-element.541.weighted_all, f32[1024,768]{1,0:T(8,128)} %get-tuple-element.377.qkv_all, f32[8,2,128]{2,1,0:T(2,128)} %add.203.squares, f32[8,2,128]{2,1,0:T(2,128)} %bitcast.139, ...), custom_call_target="tpu_custom_call" | custom-call | tf_op jit(solution)/shard_map/pallas_call | solution.py:370
  578.5 2.9 collective-permute-done.48
  581.4 4.7 broadcast_select_fusion
  586.0 2.7 collective-permute-done.49.second
  589.6 3.0 shard_map.261
  592.7 9.5 %shard_map.262 = (bf16[2,512,512]{2,1,0:T(8,128)(2,1)}, bf16[2,512,512]{2,1,0:T(8,128)(2,1)}, bf16[512,512]{1,0:T(8,128)(2,1)}, bf16[512,512]{1,0:T(8,128)(2,1)}, bf16[1024,512]{1,0:T(8,128)(2,1)}) custom-call(bf16[1024,2048]{1,0:T(8,128)(2,1)} %all-gather.5.cloned.1.call-done.tokens.refs_0_.refs_2_, ...), custom_call_target="tpu_custom_call" | custom-call | bytes 209715200 | tf_op jit(solution)/shard_map/pallas_call | solution.py:282
  602.2 16.8 %collective-permute-done.50.refs_1_ = bf16[128,2048]{1,0:T(8,128)(2,1)S(1)} collective-permute-done((bf16[128,2048]{1,0:T(8,128)(2,1)}, bf16[128,2048]{1,0:T(8,128)(2,1)S(1)}, u32[]{:S(2)}, u32[]{:S(2)}) %collective-permute-start.50) | collective-permute-done | bytes 524320 | tf_op jit(solution)/shard_map/ppermute | solution.py:38
  620.9 2.6 shard_map.263
  625.7 18.3 %collective-permute-done.51 = bf16[2,512,512]{2,1,0:T(8,128)(2,1)S(1)} collective-permute-done((bf16[2,512,512]{2,1,0:T(8,128)(2,1)}, bf16[2,512,512]{2,1,0:T(8,128)(2,1)S(1)}, u32[]{:S(2)}, u32[]{:S(2)}) %collective-permute-start.51) | collective-permute-done | bytes 1048608 | tf_op jit(solution)/shard_map/ppermute | solution.py:34
  656.3 16.6 %collective-permute-done.55.refs_2_ = bf16[128,2048]{1,0:T(8,128)(2,1)} collective-permute-done((bf16[128,2048]{1,0:T(8,128)(2,1)}, bf16[128,2048]{1,0:T(8,128)(2,1)}, u32[]{:S(2)}, u32[]{:S(2)}) %collective-permute-start.55) | collective-permute-done | bytes 524320 | tf_op jit(solution)/shard_map/ppermute | solution.py:38
  672.9 2.8 broadcast_select_fusion.2
  678.4 2.4 collective-permute-done.58
  683.9 7.4 %collective-permute-start.61 = (bf16[128,1024]{1,0:T(8,128)(2,1)}, bf16[128,1024]{1,0:T(8,128)(2,1)S(1)}, u32[]{:S(2)}, u32[]{:S(2)}) collective-permute-start(bf16[128,1024]{1,0:T(8,128)(2,1)} %get-tuple-element.633), channel_id=1, source_target_pairs={{0,16},{8,24},{16,0},{24,8},{1,17},{9,25},{17,1},{25,9},{2,18},{10... | collective-permute-start | bytes 786440 | tf_op jit(solution)/shard_map/ppermute | solution.py:38
  691.3 4.5 collective-permute-done.59.refs_1_
  695.8 3.9 shard_map.266
  701.2 12.6 %collective-permute-done.61.refs_2_ = bf16[128,1024]{1,0:T(8,128)(2,1)S(1)} collective-permute-done((bf16[128,1024]{1,0:T(8,128)(2,1)}, bf16[128,1024]{1,0:T(8,128)(2,1)S(1)}, u32[]{:S(2)}, u32[]{:S(2)}) %collective-permute-start.61) | collective-permute-done | bytes 262176 | tf_op jit(solution)/shard_map/ppermute | solution.py:38
  715.2 2.7 shard_map.267
  (329 shorter events, 150.5 us)
Async XLA Ops:
  7.2 81.6 %all-gather.5.cloned.1.call-start = ((), (), s32[]{:S(2)}) async-start(), calls=%async_computation.4 | async-start | bytes 4718592 | tf_op jit(solution)/shard_map/all_gather | solution.py:645
  8.0 13.0 %collective-permute-start.3 = (s32[1,128]{1,0:T(1,128)S(1)}, s32[1,128]{1,0:T(1,128)S(1)}, u32[]{:S(2)}, u32[]{:S(2)}) collective-permute-start(s32[1,128]{1,0:T(1,128)S(1)} %fusion.37), channel_id=1, source_target_pairs={{0,2},{2,0},{1,3},{3,1},{4,6},{6,4},{5,7},{7,5},{8,10},{10,8},{9,1... | collective-permute-start | bytes 1544 | tf_op jit(solution)/shard_map/ppermute | solution.py:34
  10.4 10.6 %collective-permute-start = (bf16[128,1024]{1,0:T(8,128)(2,1)}, bf16[128,1024]{1,0:T(8,128)(2,1)S(1)}, u32[]{:S(2)}, u32[]{:S(2)}) collective-permute-start(bf16[128,1024]{1,0:T(8,128)(2,1)} %get-tuple-element.332), channel_id=1, source_target_pairs={{0,8},{8,16},{16,24},{24,0},{1,9},{9,17},{17,25},{25,1},{2,10},{10... | collective-permute-start | bytes 786440 | tf_op jit(solution)/shard_map/ppermute | solution.py:38
  10.4 25.7 %collective-permute-start.1 = (bf16[128,1024]{1,0:T(8,128)(2,1)}, bf16[128,1024]{1,0:T(8,128)(2,1)S(1)}, u32[]{:S(2)}, u32[]{:S(2)}) collective-permute-start(bf16[128,1024]{1,0:T(8,128)(2,1)} %get-tuple-element.333), channel_id=1, source_target_pairs={{0,16},{8,24},{16,0},{24,8},{1,17},{9,25},{17,1},{25,9},{2,18},{10... | collective-permute-start | bytes 786440 | tf_op jit(solution)/shard_map/ppermute | solution.py:38
  12.3 23.8 %collective-permute-start.2 = (bf16[128,1024]{1,0:T(8,128)(2,1)}, bf16[128,1024]{1,0:T(8,128)(2,1)S(1)}, u32[]{:S(2)}, u32[]{:S(2)}) collective-permute-start(bf16[128,1024]{1,0:T(8,128)(2,1)} %get-tuple-element.334), channel_id=1, source_target_pairs={{0,24},{8,0},{16,8},{24,16},{1,25},{9,1},{17,9},{25,17},{2,26},{10... | collective-permute-start | bytes 786440 | tf_op jit(solution)/shard_map/ppermute | solution.py:38
  36.1 196.9 %reduce-scatter.5.cloned.1.call-start = ((), (), s32[]{:S(2)}) async-start(), calls=%async_computation.5 | async-start | bytes 4718592 | tf_op jit(solution)/shard_map/reduce_scatter | solution.py:642
  40.5 6.8 collective-permute-start.10
  45.2 25.5 %collective-permute-start.8 = (bf16[1024,512]{1,0:T(8,128)(2,1)}, bf16[1024,512]{1,0:T(8,128)(2,1)S(1)}, u32[]{:S(2)}, u32[]{:S(2)}) collective-permute-start(bf16[1024,512]{1,0:T(8,128)(2,1)} %shard_map.242.refs_0_), channel_id=1, source_target_pairs={{0,4},{4,0},{1,5},{5,1},{2,6},{6,2},{3,7},{7,3},{8,12},{12,8},{9,1... | collective-permute-start | bytes 3145736 | tf_op jit(solution)/shard_map/ppermute | solution.py:34
  46.7 25.2 %collective-permute-start.9 = (bf16[1024,512]{1,0:T(8,128)(2,1)}, bf16[1024,512]{1,0:T(8,128)(2,1)S(1)}, u32[]{:S(2)}, u32[]{:S(2)}) collective-permute-start(bf16[1024,512]{1,0:T(8,128)(2,1)} %shard_map.242.refs_0_), channel_id=1, source_target_pairs={{0,1},{1,0},{2,3},{3,2},{4,5},{5,4},{6,7},{7,6},{8,9},{9,8},{10,11... | collective-permute-start | bytes 3145736 | tf_op jit(solution)/shard_map/ppermute | solution.py:34
  47.9 4.3 collective-permute-start.4
  47.9 5.8 collective-permute-start.5
  49.1 5.5 collective-permute-start.6
  72.0 13.1 %collective-permute-start.11 = (bf16[512,512]{1,0:T(8,128)(2,1)S(1)}, bf16[512,512]{1,0:T(8,128)(2,1)S(1)}, u32[]{:S(2)}, u32[]{:S(2)}) collective-permute-start(bf16[512,512]{1,0:T(8,128)(2,1)S(1)} %slice.96), channel_id=1, source_target_pairs={{0,4},{4,0},{1,5},{5,1},{2,6},{6,2},{3,7},{7,3},{8,12},{12,8},{9,1... | collective-permute-start | bytes 1572872 | tf_op jit(solution)/shard_map/ppermute | solution.py:34
  72.6 12.9 %collective-permute-start.12 = (bf16[512,512]{1,0:T(8,128)(2,1)S(1)}, bf16[512,512]{1,0:T(8,128)(2,1)S(1)}, u32[]{:S(2)}, u32[]{:S(2)}) collective-permute-start(bf16[512,512]{1,0:T(8,128)(2,1)S(1)} %slice.97), channel_id=1, source_target_pairs={{0,1},{1,0},{2,3},{3,2},{4,5},{5,4},{6,7},{7,6},{8,9},{9,8},{10,11... | collective-permute-start | bytes 1572872 | tf_op jit(solution)/shard_map/ppermute | solution.py:34
  73.2 23.5 %collective-permute-start.14 = (bf16[128,1024]{1,0:T(8,128)(2,1)S(1)}, bf16[128,1024]{1,0:T(8,128)(2,1)S(1)}, u32[]{:S(2)}, u32[]{:S(2)}) collective-permute-start(bf16[128,1024]{1,0:T(8,128)(2,1)S(1)} %copy-done.62), channel_id=1, source_target_pairs={{0,8},{8,16},{16,24},{24,0},{1,9},{9,17},{17,25},{25,1},{2,10},{10... | collective-permute-start | bytes 786440 | tf_op jit(solution)/shard_map/ppermute | solution.py:38
  73.2 29.9 %collective-permute-start.15 = (bf16[128,1024]{1,0:T(8,128)(2,1)S(1)}, bf16[128,1024]{1,0:T(8,128)(2,1)S(1)}, u32[]{:S(2)}, u32[]{:S(2)}) collective-permute-start(bf16[128,1024]{1,0:T(8,128)(2,1)S(1)} %copy-done.61), channel_id=1, source_target_pairs={{0,16},{8,24},{16,0},{24,8},{1,17},{9,25},{17,1},{25,9},{2,18},{10... | collective-permute-start | bytes 786440 | tf_op jit(solution)/shard_map/ppermute | solution.py:38
  74.5 28.6 %collective-permute-start.16 = (bf16[128,1024]{1,0:T(8,128)(2,1)S(1)}, bf16[128,1024]{1,0:T(8,128)(2,1)S(1)}, u32[]{:S(2)}, u32[]{:S(2)}) collective-permute-start(bf16[128,1024]{1,0:T(8,128)(2,1)S(1)} %copy-done.60), channel_id=1, source_target_pairs={{0,24},{8,0},{16,8},{24,16},{1,25},{9,1},{17,9},{25,17},{2,26},{10... | collective-permute-start | bytes 786440 | tf_op jit(solution)/shard_map/ppermute | solution.py:38
  111.9 29.4 %collective-permute-start.20 = (bf16[1024,512]{1,0:T(8,128)(2,1)}, bf16[1024,512]{1,0:T(8,128)(2,1)S(1)}, u32[]{:S(2)}, u32[]{:S(2)}) collective-permute-start(bf16[1024,512]{1,0:T(8,128)(2,1)} %shard_map.247.refs_0_), channel_id=1, source_target_pairs={{0,4},{4,0},{1,5},{5,1},{2,6},{6,2},{3,7},{7,3},{8,12},{12,8},{9,1... | collective-permute-start | bytes 3145736 | tf_op jit(solution)/shard_map/ppermute | solution.py:34
  113.4 27.9 %collective-permute-start.21 = (bf16[1024,512]{1,0:T(8,128)(2,1)}, bf16[1024,512]{1,0:T(8,128)(2,1)S(1)}, u32[]{:S(2)}, u32[]{:S(2)}) collective-permute-start(bf16[1024,512]{1,0:T(8,128)(2,1)} %shard_map.247.refs_0_), channel_id=1, source_target_pairs={{0,1},{1,0},{2,3},{3,2},{4,5},{5,4},{6,7},{7,6},{8,9},{9,8},{10,11... | collective-permute-start | bytes 3145736 | tf_op jit(solution)/shard_map/ppermute | solution.py:34
  116.9 3.7 collective-permute-start.18
  120.6 4.5 collective-permute-start.19
  125.7 17.0 %collective-permute-start.24 = (bf16[128,2048]{1,0:T(8,128)(2,1)}, bf16[128,2048]{1,0:T(8,128)(2,1)S(1)}, u32[]{:S(2)}, u32[]{:S(2)}) collective-permute-start(bf16[128,2048]{1,0:T(8,128)(2,1)} %get-tuple-element.421), channel_id=1, source_target_pairs={{0,8},{8,16},{16,24},{24,0},{1,9},{9,17},{17,25},{25,1},{2,10},{10... | collective-permute-start | bytes 1572872 | tf_op jit(solution)/shard_map/ppermute | solution.py:38
  129.8 43.3 %collective-permute-start.25 = (bf16[128,2048]{1,0:T(8,128)(2,1)}, bf16[128,2048]{1,0:T(8,128)(2,1)S(1)}, u32[]{:S(2)}, u32[]{:S(2)}) collective-permute-start(bf16[128,2048]{1,0:T(8,128)(2,1)} %get-tuple-element.422), channel_id=1, source_target_pairs={{0,16},{8,24},{16,0},{24,8},{1,17},{9,25},{17,1},{25,9},{2,18},{10... | collective-permute-start | bytes 1572872 | tf_op jit(solution)/shard_map/ppermute | solution.py:38
  129.8 43.3 %collective-permute-start.26 = (bf16[128,2048]{1,0:T(8,128)(2,1)}, bf16[128,2048]{1,0:T(8,128)(2,1)}, u32[]{:S(2)}, u32[]{:S(2)}) collective-permute-start(bf16[128,2048]{1,0:T(8,128)(2,1)} %get-tuple-element.423), channel_id=1, source_target_pairs={{0,24},{8,0},{16,8},{24,16},{1,25},{9,1},{17,9},{25,17},{2,26},{10... | collective-permute-start | bytes 1572872 | tf_op jit(solution)/shard_map/ppermute | solution.py:38
  141.4 31.7 %collective-permute-start.22 = (bf16[512,512]{1,0:T(8,128)(2,1)S(1)}, bf16[512,512]{1,0:T(8,128)(2,1)S(1)}, u32[]{:S(2)}, u32[]{:S(2)}) collective-permute-start(bf16[512,512]{1,0:T(8,128)(2,1)S(1)} %slice.98), channel_id=1, source_target_pairs={{0,4},{4,0},{1,5},{5,1},{2,6},{6,2},{3,7},{7,3},{8,12},{12,8},{9,1... | collective-permute-start | bytes 1572872 | tf_op jit(solution)/shard_map/ppermute | solution.py:34
  142.1 31.8 %collective-permute-start.23 = (bf16[512,512]{1,0:T(8,128)(2,1)S(1)}, bf16[512,512]{1,0:T(8,128)(2,1)S(1)}, u32[]{:S(2)}, u32[]{:S(2)}) collective-permute-start(bf16[512,512]{1,0:T(8,128)(2,1)S(1)} %slice.99), channel_id=1, source_target_pairs={{0,1},{1,0},{2,3},{3,2},{4,5},{5,4},{6,7},{7,6},{8,9},{9,8},{10,11... | collective-permute-start | bytes 1572872 | tf_op jit(solution)/shard_map/ppermute | solution.py:34
  174.7 107.7 %all-gather.7.cloned.1.call-start = ((), (), s32[]{:S(2)}) async-start(), calls=%async_computation.6 | async-start | bytes 4718592 | tf_op jit(solution)/shard_map/all_gather | solution.py:645
  184.6 47.9 %collective-permute-start.28 = (bf16[1024,1024]{1,0:T(8,128)(2,1)}, bf16[1024,1024]{1,0:T(8,128)(2,1)S(1)}, u32[]{:S(2)}, u32[]{:S(2)}) collective-permute-start(bf16[1024,1024]{1,0:T(8,128)(2,1)} %shard_map.249.refs_0_), channel_id=1, source_target_pairs={{0,4},{4,0},{1,5},{5,1},{2,6},{6,2},{3,7},{7,3},{8,12},{12,8},{9,1... | collective-permute-start | bytes 6291464 | tf_op jit(solution)/shard_map/ppermute | solution.py:34
  185.3 47.7 %collective-permute-start.29 = (bf16[1024,1024]{1,0:T(8,128)(2,1)}, bf16[1024,1024]{1,0:T(8,128)(2,1)}, u32[]{:S(2)}, u32[]{:S(2)}) collective-permute-start(bf16[1024,1024]{1,0:T(8,128)(2,1)} %shard_map.249.refs_0_), channel_id=1, source_target_pairs={{0,1},{1,0},{2,3},{3,2},{4,5},{5,4},{6,7},{7,6},{8,9},{9,8},{10,11... | collective-permute-start | bytes 6291464 | tf_op jit(solution)/shard_map/ppermute | solution.py:34
  236.9 115.7 %reduce-scatter.7.cloned.1.call-start = ((), (), s32[]{:S(2)}) async-start(), calls=%async_computation.7 | async-start | bytes 4718592 | tf_op jit(solution)/shard_map/reduce_scatter | solution.py:642
  239.3 24.4 %collective-permute-start.30 = (bf16[512,1024]{1,0:T(8,128)(2,1)}, bf16[512,1024]{1,0:T(8,128)(2,1)}, u32[]{:S(2)}, u32[]{:S(2)}) collective-permute-start(bf16[512,1024]{1,0:T(8,128)(2,1)} %slice.100), channel_id=1, source_target_pairs={{0,4},{4,0},{1,5},{5,1},{2,6},{6,2},{3,7},{7,3},{8,12},{12,8},{9,1... | collective-permute-start | bytes 3145736 | tf_op jit(solution)/shard_map/ppermute | solution.py:34
  241.7 24.1 %collective-permute-start.31 = (bf16[512,1024]{1,0:T(8,128)(2,1)}, bf16[512,1024]{1,0:T(8,128)(2,1)}, u32[]{:S(2)}, u32[]{:S(2)}) collective-permute-start(bf16[512,1024]{1,0:T(8,128)(2,1)} %slice.101), channel_id=1, source_target_pairs={{0,1},{1,0},{2,3},{3,2},{4,5},{5,4},{6,7},{7,6},{8,9},{9,8},{10,11... | collective-permute-start | bytes 3145736 | tf_op jit(solution)/shard_map/ppermute | solution.py:34
  304.2 99.4 %all-gather.9.cloned.1.call-start = ((), (), s32[]{:S(2)}) async-start(), calls=%async_computation.8 | async-start | bytes 4718592 | tf_op jit(solution)/shard_map/all_gather | solution.py:645
  357.7 116.8 %reduce-scatter.9.cloned.1.call-start = ((), (), s32[]{:S(2)}) async-start(), calls=%async_computation.9 | async-start | bytes 4718592 | tf_op jit(solution)/shard_map/reduce_scatter | solution.py:642
  359.8 14.0 %collective-permute-start.32 = (bf16[128,2048]{1,0:T(8,128)(2,1)}, bf16[128,2048]{1,0:T(8,128)(2,1)S(1)}, u32[]{:S(2)}, u32[]{:S(2)}) collective-permute-start(bf16[128,2048]{1,0:T(8,128)(2,1)} %shard_map.254), channel_id=1, source_target_pairs={{0,1},{1,0},{2,3},{3,2},{4,5},{5,4},{6,7},{7,6},{8,9},{9,8},{10,11... | collective-permute-start | bytes 1572872 | tf_op jit(solution)/shard_map/ppermute | solution.py:34
  426.0 97.0 %all-gather.11.cloned.1.call-start = ((), (), s32[]{:S(2)}) async-start(), calls=%async_computation.10 | async-start | bytes 4718592 | tf_op jit(solution)/shard_map/all_gather | solution.py:645
  435.0 25.7 %collective-permute-start.33 = (bf16[2,512,512]{2,1,0:T(8,128)(2,1)}, bf16[2,512,512]{2,1,0:T(8,128)(2,1)}, u32[]{:S(2)}, u32[]{:S(2)}) collective-permute-start(bf16[2,512,512]{2,1,0:T(8,128)(2,1)} %get-tuple-element.482), channel_id=1, source_target_pairs={{0,4},{4,0},{1,5},{5,1},{2,6},{6,2},{3,7},{7,3},{8,12},{12,8},{9,1... | collective-permute-start | bytes 3145736 | tf_op jit(solution)/shard_map/ppermute | solution.py:34
  436.5 25.3 %collective-permute-start.34 = (bf16[2,512,512]{2,1,0:T(8,128)(2,1)}, bf16[2,512,512]{2,1,0:T(8,128)(2,1)}, u32[]{:S(2)}, u32[]{:S(2)}) collective-permute-start(bf16[2,512,512]{2,1,0:T(8,128)(2,1)} %get-tuple-element.483), channel_id=1, source_target_pairs={{0,1},{1,0},{2,3},{3,2},{4,5},{5,4},{6,7},{7,6},{8,9},{9,8},{10,11... | collective-permute-start | bytes 3145736 | tf_op jit(solution)/shard_map/ppermute | solution.py:34
  477.2 175.2 %reduce-scatter.11.cloned.1.call-start = ((), (), s32[]{:S(2)}) async-start(), calls=%async_computation.11 | async-start | bytes 4718592 | tf_op jit(solution)/shard_map/reduce_scatter | solution.py:642
  478.6 13.7 %collective-permute-start.36 = (bf16[512,512]{1,0:T(8,128)(2,1)S(1)}, bf16[512,512]{1,0:T(8,128)(2,1)S(1)}, u32[]{:S(2)}, u32[]{:S(2)}) collective-permute-start(bf16[512,512]{1,0:T(8,128)(2,1)S(1)} %fusion.34), channel_id=1, source_target_pairs={{0,4},{4,0},{1,5},{5,1},{2,6},{6,2},{3,7},{7,3},{8,12},{12,8},{9,1... | collective-permute-start | bytes 1572872 | tf_op jit(solution)/shard_map/ppermute | solution.py:34
  480.5 14.2 %collective-permute-start.35 = (bf16[512,512]{1,0:T(8,128)(2,1)S(1)}, bf16[512,512]{1,0:T(8,128)(2,1)S(1)}, u32[]{:S(2)}, u32[]{:S(2)}) collective-permute-start(bf16[512,512]{1,0:T(8,128)(2,1)S(1)} %fusion.35), channel_id=1, source_target_pairs={{0,1},{1,0},{2,3},{3,2},{4,5},{5,4},{6,7},{7,6},{8,9},{9,8},{10,11... | collective-permute-start | bytes 1572872 | tf_op jit(solution)/shard_map/ppermute | solution.py:34
  494.7 48.6 %collective-permute-start.41 = (bf16[2,512,1024]{2,1,0:T(8,128)(2,1)}, bf16[2,512,1024]{2,1,0:T(8,128)(2,1)}, u32[]{:S(2)}, u32[]{:S(2)}) collective-permute-start(bf16[2,512,1024]{2,1,0:T(8,128)(2,1)} %get-tuple-element.538), channel_id=1, source_target_pairs={{0,4},{4,0},{1,5},{5,1},{2,6},{6,2},{3,7},{7,3},{8,12},{12,8},{9,1... | collective-permute-start | bytes 6291464 | tf_op jit(solution)/shard_map/ppermute | solution.py:34
  495.3 48.1 %collective-permute-start.42 = (bf16[2,512,1024]{2,1,0:T(8,128)(2,1)}, bf16[2,512,1024]{2,1,0:T(8,128)(2,1)}, u32[]{:S(2)}, u32[]{:S(2)}) collective-permute-start(bf16[2,512,1024]{2,1,0:T(8,128)(2,1)} %get-tuple-element.539), channel_id=1, source_target_pairs={{0,1},{1,0},{2,3},{3,2},{4,5},{5,4},{6,7},{7,6},{8,9},{9,8},{10,11... | collective-permute-start | bytes 6291464 | tf_op jit(solution)/shard_map/ppermute | solution.py:34
  523.0 20.3 %collective-permute-start.38 = (bf16[128,1024]{1,0:T(8,128)(2,1)}, bf16[128,1024]{1,0:T(8,128)(2,1)S(1)}, u32[]{:S(2)}, u32[]{:S(2)}) collective-permute-start(bf16[128,1024]{1,0:T(8,128)(2,1)} %get-tuple-element.535), channel_id=1, source_target_pairs={{0,8},{8,16},{16,24},{24,0},{1,9},{9,17},{17,25},{25,1},{2,10},{10... | collective-permute-start | bytes 786440 | tf_op jit(solution)/shard_map/ppermute | solution.py:38
  525.7 23.6 %collective-permute-start.39 = (bf16[128,1024]{1,0:T(8,128)(2,1)}, bf16[128,1024]{1,0:T(8,128)(2,1)S(1)}, u32[]{:S(2)}, u32[]{:S(2)}) collective-permute-start(bf16[128,1024]{1,0:T(8,128)(2,1)} %get-tuple-element.536), channel_id=1, source_target_pairs={{0,16},{8,24},{16,0},{24,8},{1,17},{9,25},{17,1},{25,9},{2,18},{10... | collective-permute-start | bytes 786440 | tf_op jit(solution)/shard_map/ppermute | solution.py:38
  525.9 23.5 %collective-permute-start.40 = (bf16[128,1024]{1,0:T(8,128)(2,1)}, bf16[128,1024]{1,0:T(8,128)(2,1)S(1)}, u32[]{:S(2)}, u32[]{:S(2)}) collective-permute-start(bf16[128,1024]{1,0:T(8,128)(2,1)} %get-tuple-element.537), channel_id=1, source_target_pairs={{0,24},{8,0},{16,8},{24,16},{1,25},{9,1},{17,9},{25,17},{2,26},{10... | collective-permute-start | bytes 786440 | tf_op jit(solution)/shard_map/ppermute | solution.py:38
  552.1 29.2 %collective-permute-start.47 = (bf16[512,1024]{1,0:T(8,128)(2,1)}, bf16[512,1024]{1,0:T(8,128)(2,1)S(1)}, u32[]{:S(2)}, u32[]{:S(2)}) collective-permute-start(bf16[512,1024]{1,0:T(8,128)(2,1)} %fusion.4), channel_id=1, source_target_pairs={{0,4},{4,0},{1,5},{5,1},{2,6},{6,2},{3,7},{7,3},{8,12},{12,8},{9,1... | collective-permute-start | bytes 3145736 | tf_op jit(solution)/shard_map/ppermute | solution.py:34
  556.2 25.1 %collective-permute-start.46 = (bf16[512,1024]{1,0:T(8,128)(2,1)}, bf16[512,1024]{1,0:T(8,128)(2,1)S(1)}, u32[]{:S(2)}, u32[]{:S(2)}) collective-permute-start(bf16[512,1024]{1,0:T(8,128)(2,1)} %fusion.5), channel_id=1, source_target_pairs={{0,1},{1,0},{2,3},{3,2},{4,5},{5,4},{6,7},{7,6},{8,9},{9,8},{10,11... | collective-permute-start | bytes 3145736 | tf_op jit(solution)/shard_map/ppermute | solution.py:34
  559.4 4.0 collective-permute-start.44
  563.4 4.9 collective-permute-start.45
  568.3 13.0 %collective-permute-start.48 = (f32[64,128]{1,0:T(8,128)S(1)}, f32[64,128]{1,0:T(8,128)S(1)}, u32[]{:S(2)}, u32[]{:S(2)}) collective-permute-start(f32[64,128]{1,0:T(8,128)S(1)} %slice.129), channel_id=1, source_target_pairs={{0,1},{1,0},{2,3},{3,2},{4,5},{5,4},{6,7},{7,6},{8,9},{9,8},{10,11... | collective-permute-start | bytes 98312 | tf_op jit(solution)/shard_map/ppermute | solution.py:34
  592.7 26.3 %collective-permute-start.50 = (bf16[128,2048]{1,0:T(8,128)(2,1)}, bf16[128,2048]{1,0:T(8,128)(2,1)S(1)}, u32[]{:S(2)}, u32[]{:S(2)}) collective-permute-start(bf16[128,2048]{1,0:T(8,128)(2,1)} %get-tuple-element.579), channel_id=1, source_target_pairs={{0,8},{8,16},{16,24},{24,0},{1,9},{9,17},{17,25},{25,1},{2,10},{10... | collective-permute-start | bytes 1572872 | tf_op jit(solution)/shard_map/ppermute | solution.py:38
  619.0 25.1 %collective-permute-start.51 = (bf16[2,512,512]{2,1,0:T(8,128)(2,1)}, bf16[2,512,512]{2,1,0:T(8,128)(2,1)S(1)}, u32[]{:S(2)}, u32[]{:S(2)}) collective-permute-start(bf16[2,512,512]{2,1,0:T(8,128)(2,1)} %get-tuple-element.581), channel_id=1, source_target_pairs={{0,4},{4,0},{1,5},{5,1},{2,6},{6,2},{3,7},{7,3},{8,12},{12,8},{9,1... | collective-permute-start | bytes 3145736 | tf_op jit(solution)/shard_map/ppermute | solution.py:34
  619.4 24.8 %collective-permute-start.52 = (bf16[2,512,512]{2,1,0:T(8,128)(2,1)}, bf16[2,512,512]{2,1,0:T(8,128)(2,1)}, u32[]{:S(2)}, u32[]{:S(2)}) collective-permute-start(bf16[2,512,512]{2,1,0:T(8,128)(2,1)} %get-tuple-element.582), channel_id=1, source_target_pairs={{0,1},{1,0},{2,3},{3,2},{4,5},{5,4},{6,7},{7,6},{8,9},{9,8},{10,11... | collective-permute-start | bytes 3145736 | tf_op jit(solution)/shard_map/ppermute | solution.py:34
  623.5 49.4 %collective-permute-start.55 = (bf16[128,2048]{1,0:T(8,128)(2,1)}, bf16[128,2048]{1,0:T(8,128)(2,1)}, u32[]{:S(2)}, u32[]{:S(2)}) collective-permute-start(bf16[128,2048]{1,0:T(8,128)(2,1)} %get-tuple-element.598), channel_id=1, source_target_pairs={{0,16},{8,24},{16,0},{24,8},{1,17},{9,25},{17,1},{25,9},{2,18},{10... | collective-permute-start | bytes 1572872 | tf_op jit(solution)/shard_map/ppermute | solution.py:38
  625.2 47.7 %collective-permute-start.56 = (bf16[128,2048]{1,0:T(8,128)(2,1)}, bf16[128,2048]{1,0:T(8,128)(2,1)}, u32[]{:S(2)}, u32[]{:S(2)}) collective-permute-start(bf16[128,2048]{1,0:T(8,128)(2,1)} %get-tuple-element.599), channel_id=1, source_target_pairs={{0,24},{8,0},{16,8},{24,16},{1,25},{9,1},{17,9},{25,17},{2,26},{10... | collective-permute-start | bytes 1572872 | tf_op jit(solution)/shard_map/ppermute | solution.py:38
  646.6 26.3 %collective-permute-start.54 = (bf16[512,512]{1,0:T(8,128)(2,1)}, bf16[512,512]{1,0:T(8,128)(2,1)}, u32[]{:S(2)}, u32[]{:S(2)}) collective-permute-start(bf16[512,512]{1,0:T(8,128)(2,1)} %fusion.29), channel_id=1, source_target_pairs={{0,4},{4,0},{1,5},{5,1},{2,6},{6,2},{3,7},{7,3},{8,12},{12,8},{9,1... | collective-permute-start | bytes 1572872 | tf_op jit(solution)/shard_map/ppermute | solution.py:34
  650.0 22.9 %collective-permute-start.53 = (bf16[512,512]{1,0:T(8,128)(2,1)}, bf16[512,512]{1,0:T(8,128)(2,1)}, u32[]{:S(2)}, u32[]{:S(2)}) collective-permute-start(bf16[512,512]{1,0:T(8,128)(2,1)} %fusion.30), channel_id=1, source_target_pairs={{0,1},{1,0},{2,3},{3,2},{4,5},{5,4},{6,7},{7,6},{8,9},{9,8},{10,11... | collective-permute-start | bytes 1572872 | tf_op jit(solution)/shard_map/ppermute | solution.py:34
  675.8 5.0 collective-permute-start.57
  675.8 15.5 %collective-permute-start.60 = (bf16[128,2048]{1,0:T(8,128)(2,1)S(1)}, bf16[128,2048]{1,0:T(8,128)(2,1)S(1)}, u32[]{:S(2)}, u32[]{:S(2)}) collective-permute-start(bf16[128,2048]{1,0:T(8,128)(2,1)S(1)} %copy-done.27), channel_id=1, source_target_pairs={{0,1},{1,0},{2,3},{3,2},{4,5},{5,4},{6,7},{7,6},{8,9},{9,8},{10,11... | collective-permute-start | bytes 1572872 | tf_op jit(solution)/shard_map/ppermute | solution.py:34
  676.9 3.9 collective-permute-start.58
  683.9 11.9 %collective-permute-start.59 = (bf16[128,1024]{1,0:T(8,128)(2,1)}, bf16[128,1024]{1,0:T(8,128)(2,1)S(1)}, u32[]{:S(2)}, u32[]{:S(2)}) collective-permute-start(bf16[128,1024]{1,0:T(8,128)(2,1)} %get-tuple-element.614), channel_id=1, source_target_pairs={{0,8},{8,16},{16,24},{24,0},{1,9},{9,17},{17,25},{25,1},{2,10},{10... | collective-permute-start | bytes 786440 | tf_op jit(solution)/shard_map/ppermute | solution.py:38
  683.9 29.9 %collective-permute-start.61 = (bf16[128,1024]{1,0:T(8,128)(2,1)}, bf16[128,1024]{1,0:T(8,128)(2,1)S(1)}, u32[]{:S(2)}, u32[]{:S(2)}) collective-permute-start(bf16[128,1024]{1,0:T(8,128)(2,1)} %get-tuple-element.633), channel_id=1, source_target_pairs={{0,16},{8,24},{16,0},{24,8},{1,17},{9,25},{17,1},{25,9},{2,18},{10... | collective-permute-start | bytes 786440 | tf_op jit(solution)/shard_map/ppermute | solution.py:38
  691.3 22.5 %collective-permute-start.62 = (bf16[128,1024]{1,0:T(8,128)(2,1)}, bf16[128,1024]{1,0:T(8,128)(2,1)S(1)}, u32[]{:S(2)}, u32[]{:S(2)}) collective-permute-start(bf16[128,1024]{1,0:T(8,128)(2,1)} %get-tuple-element.634), channel_id=1, source_target_pairs={{0,24},{8,0},{16,8},{24,16},{1,25},{9,1},{17,9},{25,17},{2,26},{10... | collective-permute-start | bytes 786440 | tf_op jit(solution)/shard_map/ppermute | solution.py:38
  (71 other events, 970.4 us)
Sparse Core Ops, SparseCore 0:
  36.2 50.3 all-gather.4
  174.8 47.0 reduce-scatter.4
  237.0 45.3 all-gather.6
  304.3 48.2 reduce-scatter.6
  357.8 45.7 all-gather.8
  426.1 48.3 reduce-scatter.8
  477.3 45.6 all-gather.10
  581.5 70.8 reduce-scatter.10
